TPU v7x, 256 devices: a whole 4x4x8 slice. The times are simulated.
256 devices in a mesh: wide: 64 (over y, z, x_lo), narrow: 4 (over x_hi, core).
Axes of the slice: x: 4 (x_hi: 2, x_lo: 2; x = x_hi * 2 + x_lo), y: 4, z: 8, core: 2. Of those that a mesh axis runs over, the one named last changes fastest.
Arguments:
- logits: bfloat16 [131072, 4096], P('wide', 'narrow'), may hold values from -9 to 280
- expression: bfloat16 [131072, 512], P('wide')
- measured: float32 [512, 4096], P('wide', 'narrow')
Outputs:
- grad_logits: bfloat16 [131072, 4096], P('wide', 'narrow')
- per_gene_similarity: float32 [512], P('wide')
All inputs are finite; a program needn't handle non-finite values.
Results may differ from a plain program's by a relative error of at most 0.0054.
Values may be sent and summed in bfloat16 or wider, within the bound.
No kernel may reach another device: no remote copies, remote signals or barrier semaphores. Data moves between devices by JAX's collectives and lax.ppermute only.
A program may use at most 64 MiB of HBM per device.

v0:
```python
import jax
import jax.numpy as jnp
from jax import lax
from jax.sharding import PartitionSpec as P


def cosine_pieces_list(
    predicted_expression, measured, inner_product, predicted_squares, measured_squares
):
    norm_p = jnp.sqrt(predicted_squares + 1e-06)
    measured_norm = jnp.sqrt(measured_squares + 1e-06)
    cosine = inner_product / (norm_p * measured_norm)
    d_pred = (
        -measured / (norm_p * measured_norm)[:, None]
        + (inner_product / (norm_p**3 * measured_norm))[:, None] * predicted_expression
    )
    return (cosine, d_pred.astype(jnp.bfloat16))


def body(logits, expression, measured):
    values = logits.astype(jnp.float32)
    local_top = jnp.max(values, axis=1)
    top = lax.pmax(local_top, "narrow")
    expo = jnp.exp(values - top[:, None])
    total = lax.psum(jnp.sum(expo, axis=1), "narrow")
    probs = expo / total[:, None]
    probs_low = probs.astype(jnp.bfloat16)
    contract = (((0,), (0,)), ((), ()))
    columns = expression
    predicted_expression = lax.psum_scatter(
        lax.dot_general(columns, probs_low, contract, preferred_element_type=jnp.float32),
        "wide",
        scatter_dimension=0,
        tiled=True,
    )
    inner_product, predicted_squares, measured_squares = lax.psum(
        (
            jnp.sum(predicted_expression * measured, axis=1),
            jnp.sum(predicted_expression * predicted_expression, axis=1),
            jnp.sum(measured * measured, axis=1),
        ),
        "narrow",
    )
    per_gene_similarity, share_gradient = cosine_pieces_list(
        predicted_expression, measured, inner_product, predicted_squares, measured_squares
    )
    columns = expression
    d_probs = jnp.dot(
        columns,
        lax.all_gather(share_gradient, "wide", axis=0, tiled=True),
        preferred_element_type=jnp.float32,
    )
    row_dot = lax.psum(jnp.sum(probs * d_probs, axis=1), "narrow")
    spots_total = logits.shape[1] * lax.axis_size("narrow")
    grad_logits = (spots_total * probs * (d_probs - row_dot[:, None])).astype(jnp.bfloat16)
    return (grad_logits, per_gene_similarity)


def solution(mesh):
    placed = (P("wide", "narrow"), P("wide", None), P("wide", "narrow"))
    return jax.shard_map(
        body,
        mesh=mesh,
        in_specs=placed,
        out_specs=(P("wide", "narrow"), P("wide")),
        check_vma=False,
    )
```

profile of v0, /device:TPU:1, one launch (start us, length us, event | category | flops | bytes accessed | tf_op | source)
XLA Modules:
  0.0 702.3 jit_solution(18178039412074368381)
XLA Ops:
  7.2 0.0 copy-start
  7.2 0.0 reduce-scatter.4.cloned.1.call-start
  7.2 6.6 copy.15
  13.8 2.8 reduce_max.14
  16.6 9.8 %pmax.7 = f32[2048]{0:T(1024)S(1)} all-reduce(bf16[2048]{0:T(1024)(128)(2,1)S(1)} %reduce_max.14), channel_id=1, replica_groups=mesh['wide'=64,'narrow'=4] {'narrow'}, use_global_device_ids=true, to_apply=%region_1.0 | all-reduce | flops 2048 | bytes 12288 | tf_op jit(solution)/shard_map/pmax | solution.py:23
  26.5 3.6 fusion.4
  30.0 8.3 %psum.35 = f32[2048]{0:T(1024)S(1)} all-reduce(f32[2048]{0:T(1024)S(1)} %fusion.4), channel_id=1, replica_groups=mesh['wide'=64,'narrow'=4] {'narrow'}, use_global_device_ids=true, to_apply=%region_3.0 | all-reduce | flops 2048 | bytes 16384 | tf_op jit(solution)/shard_map/psum | solution.py:25
  38.4 0.0 copy-done
  38.4 0.0 copy-start.1
  38.4 5.8 fusion.7
  44.3 2.9 copy.19
  47.2 0.0 reduce-scatter.4.cloned.1.call-update
  47.2 0.0 all-gather.2.cloned.1.call-start
  47.3 0.0 copy-done.1
  47.3 0.2 copy.16
  47.5 0.1 multiply_reduce_fusion.2
  47.6 267.4 %reduce-scatter.4.cloned.1.call-done = f32[8,1024]{1,0:T(8,128)} async-done(((f32[512,1024]{1,0:T(8,128)}), f32[8,1024]{1,0:T(8,128)}) %reduce-scatter.4.cloned.1.call-update) | async-done | bytes 32784 | tf_op jit(solution)/shard_map/reduce_scatter | solution.py:30
  315.1 0.9 copy.20
  316.0 0.2 multiply_reduce_fusion.1
  316.2 58.8 %all-reduce = (f32[8]{0:T(128)S(1)}, f32[8]{0:T(128)S(1)}, f32[8]{0:T(128)S(1)}) all-reduce(f32[8]{0:T(128)S(1)} %get-tuple-element.9, f32[8]{0:T(128)S(1)} %get-tuple-element.8, f32[8]{0:T(128)S(1)} %multiply_reduce_fusion.2), channel_id=1, replica_groups=mesh['wide'=64,'narrow'=4] {'narrow'}, use_global_device_ids=true, to_apply=%region_10.0 | all-reduce | flops 24 | bytes 192 | tf_op jit(solution)/shard_map/psum | solution.py:36
  375.0 0.5 fusion.14
  375.5 1.4 add_convert_fusion
  377.0 0.0 all-gather.2.cloned.1.call-update
  377.0 247.2 %all-gather.2.cloned.1.call-done = bf16[512,1024]{1,0:T(8,128)(2,1)} async-done(((bf16[8,1024]{1,0:T(8,128)(2,1)}), bf16[512,1024]{1,0:T(8,128)(2,1)}) %all-gather.2.cloned.1.call-update) | async-done | bytes 1048592 | tf_op jit(solution)/shard_map/all_gather | solution.py:50
  624.2 6.8 fusion
  631.0 50.8 %psum.39 = f32[2048]{0:T(1024)S(1)} all-reduce(f32[2048]{0:T(1024)S(1)} %get-tuple-element.16), channel_id=1, replica_groups=mesh['wide'=64,'narrow'=4] {'narrow'}, use_global_device_ids=true, to_apply=%region_12.0 | all-reduce | flops 2048 | bytes 16384 | tf_op jit(solution)/shard_map/psum | solution.py:53
  681.8 7.2 %fusion.2 = bf16[2048,1024]{0,1:T(8,128)(2,1)} fusion(f32[1024,2048]{1,0:T(8,128)} %get-tuple-element.17, f32[2048]{0:T(1024)S(1)} %psum.39, f32[2048]{0:T(1024)S(1)} %psum.35, f32[2048]{0:T(1024)S(1)} %pmax.7, bf16[2048,1024]{0,1:T(8,128)(2,1)} %copy.15), kind=kLoop, calls=%fused_computation.4 | loop fusion | flops 14680064 | bytes 16801792 | tf_op jit(solution)/shard_map/convert_element_type | solution.py:55
  689.0 6.4 copy.18
Async XLA Ops:
  7.2 31.2 %copy-start = (bf16[2048,512]{1,0:T(8,128)(2,1)S(1)}, bf16[2048,512]{1,0:T(8,128)(2,1)}, u32[]{:S(2)}) copy-start(bf16[2048,512]{1,0:T(8,128)(2,1)} %param.4) | copy-start | bytes 6291460
  7.2 307.9 %reduce-scatter.4.cloned.1.call-start = ((), (), s32[]{:S(2)}) async-start(), calls=%async_computation.2 | async-start | bytes 2129920 | tf_op jit(solution)/shard_map/reduce_scatter | solution.py:30
  38.4 8.9 %copy-start.1 = (f32[8,1024]{1,0:T(8,128)S(1)}, f32[8,1024]{1,0:T(8,128)}, u32[]{:S(2)}) copy-start(f32[8,1024]{1,0:T(8,128)} %param.5) | copy-start | bytes 98308
  47.2 576.9 %all-gather.2.cloned.1.call-start = ((), (), s32[]{:S(2)}) async-start(), calls=%async_computation.1 | async-start | bytes 1064960 | tf_op jit(solution)/shard_map/all_gather | solution.py:50
Sparse Core Ops, SparseCore 0:
  47.3 267.6 reduce-scatter.3
  377.1 247.0 all-gather.1
where the time goes:
time: 703 us; the launch traced here: 702 us
  waiting for transfers between devices  515 us (73%)
  blocking collectives  128 us (18%)
  local copies, waits for them, and re-layouts  17.1 us (2%)
  other arithmetic  15.9 us (2%)
  between operations  14.1 us (2%)
  matrix products  12.7 us (2%)
    reduce_scatter x1, waiting for transfers between devices, body(): lax.psum_scatter(lax.dot_general(columns, probs_low, contract, preferred_...  267 us
    all_gather x1, waiting for transfers between devices, body(): lax.all_gather(share_gradient, 'wide', axis=0, tiled=True)  247 us
    psum x1, blocking collectives, body(): lax.psum((jnp.sum(predicted_expression * measured, axis=1), jnp.sum(predi...  58.8 us
    psum x1, blocking collectives, body(): row_dot = lax.psum(jnp.sum(probs * d_probs, axis=1), 'narrow')  50.8 us
    unnamed x9, local copies, waits for them, and re-layouts  17.1 us
  transfers between devices with their start and end apart: 2, of which 2 were waited for; matrix products, arithmetic and copies ran while one was open for 0% of the time, Pallas kernels for 0%

commit v1 on v0

v1 whole, which is shorter than its diff:
```python
import jax
import jax.numpy as jnp
from jax import lax
from jax.sharding import PartitionSpec as P

Y, Z, X, R = 4, 8, 2, 8


def wide_index(y, z, x):
    return (y * Z + z) * X + x


YX_GROUPS = [[wide_index(y, z, x) for y in range(Y) for x in range(X)] for z in range(Z)]
Z_GROUPS = [[wide_index(y, z, x) for z in range(Z)] for y in range(Y) for x in range(X)]


def swap(v, groups):
    return lax.all_to_all(v, "wide", 0, 0, axis_index_groups=groups)


def narrow_peers(v):
    return [lax.ppermute(v, "narrow", [(i, i ^ d) for i in range(4)]) for d in (3, 2, 1)]


def body(logits, expression, measured):
    spots = logits.shape[1]
    values = logits.astype(jnp.float32)
    local_top = jnp.max(values, axis=1)
    local_log = local_top + jnp.log(jnp.sum(jnp.exp(values - local_top[:, None]), axis=1))
    logs = [local_log] + narrow_peers(local_log)
    top = jnp.maximum(jnp.maximum(logs[0], logs[1]), jnp.maximum(logs[2], logs[3]))
    log_total = top + jnp.log(sum(jnp.exp(v - top) for v in logs))
    probs = jnp.exp(values - log_total[:, None])
    probs_low = probs.astype(jnp.bfloat16)
    part = lax.dot_general(
        expression, probs_low, (((0,), (0,)), ((), ())), preferred_element_type=jnp.float32
    ).astype(jnp.bfloat16)
    part = part.reshape(Y, Z, X, R, spots).transpose(0, 2, 1, 3, 4).reshape(Y * X, Z * R, spots)
    part = swap(part, YX_GROUPS).astype(jnp.float32).sum(0).astype(jnp.bfloat16)
    part = swap(part.reshape(Z, R, spots), Z_GROUPS)
    predicted = part.astype(jnp.float32).sum(0)
    sums = jnp.stack(
        [
            jnp.sum(predicted * measured, axis=1),
            jnp.sum(predicted * predicted, axis=1),
            jnp.sum(measured * measured, axis=1),
        ]
    )
    sums = sums + sum(narrow_peers(sums))
    inner, pred_sq, meas_sq = sums[0], sums[1], sums[2]
    norm_p = jnp.sqrt(pred_sq + 1e-06)
    norm_m = jnp.sqrt(meas_sq + 1e-06)
    similarity = inner / (norm_p * norm_m)
    share = (
        -measured / (norm_p * norm_m)[:, None]
        + (inner / (norm_p**3 * norm_m))[:, None] * predicted
    ).astype(jnp.bfloat16)
    share = swap(jnp.broadcast_to(share[None], (Z, R, spots)), Z_GROUPS).reshape(Z * R, spots)
    share = swap(jnp.broadcast_to(share[None], (Y * X, Z * R, spots)), YX_GROUPS)
    d_pred = share.reshape(Y, X, Z, R, spots).transpose(0, 2, 1, 3, 4).reshape(Y * X * Z * R, spots)
    d_probs = jnp.dot(expression, d_pred, preferred_element_type=jnp.float32)
    row_dot = jnp.sum(probs * d_probs, axis=1)
    row_dot = row_dot + sum(narrow_peers(row_dot))
    total_spots = spots * lax.axis_size("narrow")
    grad = (total_spots * probs * (d_probs - row_dot[:, None])).astype(jnp.bfloat16)
    return (grad, similarity)


def solution(mesh):
    placed = (P("wide", "narrow"), P("wide", None), P("wide", "narrow"))
    return jax.shard_map(
        body,
        mesh=mesh,
        in_specs=placed,
        out_specs=(P("wide", "narrow"), P("wide")),
        check_vma=False,
    )
```

time: 703 us -> 125 us (0.18)
  waiting for transfers between devices: 515 us -> 8.43 us
  blocking collectives: 128 us -> 62.2 us
  starting transfers between devices: 0.08 us -> 18.9 us
  between operations: 14.1 us -> 0.74 us
    reduce_scatter x1 -> x0, waiting for transfers between devices: 267 us -> none  [body(): lax.psum_scatter(lax.dot_general(columns, probs_low, contract, preferred_...]
    all_gather x1 -> x0, waiting for transfers between devices: 247 us -> none  [body(): lax.all_gather(share_gradient, 'wide', axis=0, tiled=True)]
    psum x3 -> x0, blocking collectives: 118 us -> none  [the longest x1 58.8 us: body(): lax.psum((jnp.sum(predicted_expression * measured, axis=1), jnp.sum(predi...]
    all_to_all x0 -> x4, blocking collectives: none -> 62.2 us  [swap(): return lax.all_to_all(v, 'wide', 0, 0, axis_index_groups=groups)]
    ppermute x0 -> x9, starting transfers between devices: none -> 18.9 us  [narrow_peers(): lax.ppermute(v, 'narrow', [(i, i ^ d) for i in range(4)])]
    pmax x1 -> x0, blocking collectives: 9.82 us -> none  [body(): top = lax.pmax(local_top, 'narrow')]
    ppermute x0 -> x9, waiting for transfers between devices: none -> 8.43 us  [narrow_peers(): lax.ppermute(v, 'narrow', [(i, i ^ d) for i in range(4)])]
    unnamed x9 -> x8, local copies, waits for them, and re-layouts: 17.1 us -> 13 us
  transfers between devices with their start and end apart: 2 -> 9, of which waited for: 2 -> 6; matrix products, arithmetic and copies ran while one was open for 0% -> 0% of each run, Pallas kernels for 0% -> 0%
where the time goes in v1:
time: 125 us; the launch traced here: 124 us
  blocking collectives  62.2 us (50%)
  starting transfers between devices  18.9 us (15%)
  local copies, waits for them, and re-layouts  13.3 us (11%)
  other arithmetic  11 us (9%)
  matrix products  9.57 us (8%)
  waiting for transfers between devices  8.43 us (7%)
    all_to_all x4, blocking collectives, swap(): return lax.all_to_all(v, 'wide', 0, 0, axis_index_groups=groups)  62.2 us
    ppermute x9, starting transfers between devices, narrow_peers(): lax.ppermute(v, 'narrow', [(i, i ^ d) for i in range(4)])  18.9 us
    unnamed x8, local copies, waits for them, and re-layouts  13 us
    ppermute x9, waiting for transfers between devices, narrow_peers(): lax.ppermute(v, 'narrow', [(i, i ^ d) for i in range(4)])  8.43 us
    dot_general x1, matrix products, body(): d_probs = jnp.dot(expression, d_pred, preferred_element_type=jnp.float32)  4.99 us
    dot_general x1, matrix products, body(): lax.dot_general(expression, probs_low, (((0,), (0,)), ((), ())), preferre...  4.59 us
    reduce_sum x1, other arithmetic, body(): jnp.sum(jnp.exp(values - local_top[:, None]), axis=1)  3.59 us
    convert_element_type x1, other arithmetic, body(): (total_spots * probs * (d_probs - row_dot[:, None])).astype(jnp.bfloat16)  3.58 us
  transfers between devices with their start and end apart: 9, of which 6 were waited for; matrix products, arithmetic and copies ran while one was open for 0% of the time, Pallas kernels for 0%

profile of v1, /device:TPU:1, one launch (start us, length us, event | category | flops | bytes accessed | tf_op | source)
XLA Modules:
  0.0 124.2 jit_solution(18331093687990184132)
XLA Ops:
  0.6 0.0 copy-start
  0.6 6.6 %copy.14 = bf16[2048,1024]{0,1:T(8,128)(2,1)} copy(bf16[2048,1024]{1,0:T(8,128)(2,1)} %param.3) | data formatting | bytes 8388608 | tf_op args[0]
  7.2 2.8 %reduce_max.14 = bf16[2048]{0:T(1024)(128)(2,1)S(1)} reduce(bf16[2048,1024]{1,0:T(8,128)(2,1)} %param.3, bf16[]{:T(256)} %constant.2.clone.1), dimensions={1}, to_apply=%region_0.0 | reduce | flops 2095104 | bytes 4198402 | tf_op jit(solution)/shard_map/reduce_max | solution.py:28
  10.1 3.6 %fusion.1 = f32[2048]{0:T(1024)S(1)} fusion(bf16[2048,1024]{0,1:T(8,128)(2,1)} %copy.14, f32[2048]{0:T(1024)S(1)} %reduce_max.15), kind=kLoop, calls=%fused_computation.3 | loop fusion | flops 6289408 | bytes 4210688 | tf_op jit(solution)/shard_map/reduce_sum | solution.py:29
  13.7 3.3 %collective-permute-start.2 = (f32[2048]{0:T(1024)S(1)}, f32[2048]{0:T(1024)S(1)}, u32[]{:S(2)}, u32[]{:S(2)}) collective-permute-start(f32[2048]{0:T(1024)S(1)} %log_add_fusion.1), channel_id=1, source_target_pairs={{0,1},{1,0},{2,3},{3,2},{4,5},{5,4},{6,7},{7,6},{8,9},{9,8},{10,11... | collective-permute-start | bytes 24584 | tf_op jit(solution)/shard_map/ppermute | solution.py:22
  17.0 1.0 collective-permute-start.1
  18.0 2.2 %collective-permute-start = (f32[2048]{0:T(1024)S(1)}, f32[2048]{0:T(1024)S(1)}, u32[]{:S(2)}, u32[]{:S(2)}) collective-permute-start(f32[2048]{0:T(1024)S(1)} %log_add_fusion.1), channel_id=1, source_target_pairs={{0,3},{1,2},{2,1},{3,0},{4,7},{5,6},{6,5},{7,4},{8,11},{9,10},{10,... | collective-permute-start | bytes 24584 | tf_op jit(solution)/shard_map/ppermute | solution.py:22
  20.2 0.0 collective-permute-done.2
  20.2 0.8 collective-permute-done.1
  21.0 1.6 %collective-permute-done = f32[2048]{0:T(1024)S(1)} collective-permute-done((f32[2048]{0:T(1024)S(1)}, f32[2048]{0:T(1024)S(1)}, u32[]{:S(2)}, u32[]{:S(2)}) %collective-permute-start) | collective-permute-done | bytes 8224 | tf_op jit(solution)/shard_map/ppermute | solution.py:22
  22.6 0.0 copy-done
  22.6 0.0 copy-start.2
  22.7 4.6 %fusion.12 = bf16[1024,512]{0,1:T(8,128)(2,1)S(1)} fusion(bf16[2048,512]{1,0:T(8,128)(2,1)S(1)} %copy-done, bf16[2048,1024]{0,1:T(8,128)(2,1)} %copy.14, f32[2048]{0:T(1024)S(1)} %log_add_fusion), kind=kOutput, calls=%fused_computation.14 | convolution fusion | flops 2154299392 | bytes 7348224 | tf_op jit(solution)/shard_map/dot_general | solution.py:35
  27.2 0.1 copy.15
  27.3 18.9 %all_to_all.20 = bf16[8,64,1024]{2,1,0:T(8,128)(2,1)S(1)} all-to-all(bf16[8,64,1024]{2,1,0:T(8,128)(2,1)S(1)} %bitcast.34), channel_id=1, replica_groups={{0,4,64,68,128,132,192,196},{8,12,72,76,136,140,200,204},{16,20,80,84,1..., dimensions={0} | all-to-all | bytes 2097152 | tf_op jit(solution)/shard_map/all_to_all | solution.py:18
  46.2 0.2 reduce_sum.67
  46.4 16.0 %all_to_all.21 = bf16[8,8,1024]{2,1,0:T(8,128)(2,1)S(1)} all-to-all(bf16[8,8,1024]{2,1,0:T(8,128)(2,1)S(1)} %bitcast.38), channel_id=1, replica_groups={{0,8,16,24,32,40,48,56},{4,12,20,28,36,44,52,60},{64,72,80,88,96,104,11..., dimensions={0} | all-to-all | bytes 262144 | tf_op jit(solution)/shard_map/all_to_all | solution.py:18
  62.4 0.0 copy-done.2
  62.4 0.2 multiply_reduce_fusion.2
  62.6 3.2 %collective-permute-start.5 = (f32[3,8]{1,0:T(4,128)S(1)}, f32[3,8]{1,0:T(4,128)S(1)}, u32[]{:S(2)}, u32[]{:S(2)}) collective-permute-start(f32[3,8]{1,0:T(4,128)S(1)} %pad_maximum_fusion), channel_id=1, source_target_pairs={{0,1},{1,0},{2,3},{3,2},{4,5},{5,4},{6,7},{7,6},{8,9},{9,8},{10,11... | collective-permute-start | bytes 296 | tf_op jit(solution)/shard_map/ppermute | solution.py:22
  65.8 1.7 %collective-permute-start.4 = (f32[3,8]{1,0:T(4,128)S(1)}, f32[3,8]{1,0:T(4,128)S(1)}, u32[]{:S(2)}, u32[]{:S(2)}) collective-permute-start(f32[3,8]{1,0:T(4,128)S(1)} %pad_maximum_fusion), channel_id=1, source_target_pairs={{0,2},{1,3},{2,0},{3,1},{4,6},{5,7},{6,4},{7,5},{8,10},{9,11},{10,... | collective-permute-start | bytes 296 | tf_op jit(solution)/shard_map/ppermute | solution.py:22
  67.6 1.5 %collective-permute-start.3 = (f32[3,8]{1,0:T(4,128)S(1)}, f32[3,8]{1,0:T(4,128)S(1)}, u32[]{:S(2)}, u32[]{:S(2)}) collective-permute-start(f32[3,8]{1,0:T(4,128)S(1)} %pad_maximum_fusion), channel_id=1, source_target_pairs={{0,3},{1,2},{2,1},{3,0},{4,7},{5,6},{6,5},{7,4},{8,11},{9,10},{10,... | collective-permute-start | bytes 296 | tf_op jit(solution)/shard_map/ppermute | solution.py:22
  69.1 0.0 collective-permute-done.5
  69.1 0.7 collective-permute-done.4
  69.8 2.3 %collective-permute-done.3 = f32[3,8]{1,0:T(4,128)S(1)} collective-permute-done((f32[3,8]{1,0:T(4,128)S(1)}, f32[3,8]{1,0:T(4,128)S(1)}, u32[]{:S(2)}, u32[]{:S(2)}) %collective-permute-start.3) | collective-permute-done | bytes 128 | tf_op jit(solution)/shard_map/ppermute | solution.py:22
  72.1 0.5 bitcast_divide_fusion
  72.6 0.1 add_convert_fusion
  72.7 10.8 %all_to_all.22 = bf16[8,8,1024]{2,1,0:T(8,128)(2,1)S(1)} all-to-all(bf16[8,8,1024]{2,1,0:T(8,128)(2,1)S(1)} %broadcast_in_dim.6), channel_id=1, replica_groups={{0,8,16,24,32,40,48,56},{4,12,20,28,36,44,52,60},{64,72,80,88,96,104,11..., dimensions={0} | all-to-all | bytes 262144 | tf_op jit(solution)/shard_map/all_to_all | solution.py:18
  83.5 0.1 broadcast_in_dim.8
  83.7 16.6 %all_to_all.23 = bf16[8,64,1024]{2,1,0:T(8,128)(2,1)S(1)} all-to-all(bf16[8,64,1024]{2,1,0:T(8,128)(2,1)S(1)} %broadcast_in_dim.8), channel_id=1, replica_groups={{0,4,64,68,128,132,192,196},{8,12,72,76,136,140,200,204},{16,20,80,84,1..., dimensions={0} | all-to-all | bytes 2097152 | tf_op jit(solution)/shard_map/all_to_all | solution.py:18
  100.2 0.1 copy.16
  100.3 0.0 copy-start.1
  100.3 5.0 %fusion.8 = (f32[2048]{0:T(1024)S(1)}, f32[1024,2048]{1,0:T(8,128)S(1)}) fusion(bf16[2048,1024]{0,1:T(8,128)(2,1)} %copy.14, f32[2048]{0:T(1024)S(1)} %log_add_fusion, bf16[512,1024]{1,0:T(8,128)(2,1)S(1)} %bitcast.36, bf16[2048,512]{1,0:T(8,128)(2,1)S(1)} %copy-done), kind=kOutput, calls=%fused_computation.10 | convolution fusion | flops 2155870208 | bytes 15745024 | tf_op jit(solution)/shard_map/dot_general | solution.py:61
  105.3 2.6 %collective-permute-start.8 = (f32[2048]{0:T(1024)S(1)}, f32[2048]{0:T(1024)S(1)}, u32[]{:S(2)}, u32[]{:S(2)}) collective-permute-start(f32[2048]{0:T(1024)S(1)} %get-tuple-element.16), channel_id=1, source_target_pairs={{0,1},{1,0},{2,3},{3,2},{4,5},{5,4},{6,7},{7,6},{8,9},{9,8},{10,11... | collective-permute-start | bytes 24584 | tf_op jit(solution)/shard_map/ppermute | solution.py:22
  107.9 1.7 %collective-permute-start.7 = (f32[2048]{0:T(1024)S(1)}, f32[2048]{0:T(1024)S(1)}, u32[]{:S(2)}, u32[]{:S(2)}) collective-permute-start(f32[2048]{0:T(1024)S(1)} %get-tuple-element.16), channel_id=1, source_target_pairs={{0,2},{1,3},{2,0},{3,1},{4,6},{5,7},{6,4},{7,5},{8,10},{9,11},{10,... | collective-permute-start | bytes 24584 | tf_op jit(solution)/shard_map/ppermute | solution.py:22
  109.6 1.5 %collective-permute-start.6 = (f32[2048]{0:T(1024)S(1)}, f32[2048]{0:T(1024)S(1)}, u32[]{:S(2)}, u32[]{:S(2)}) collective-permute-start(f32[2048]{0:T(1024)S(1)} %get-tuple-element.16), channel_id=1, source_target_pairs={{0,3},{1,2},{2,1},{3,0},{4,7},{5,6},{6,5},{7,4},{8,11},{9,10},{10,... | collective-permute-start | bytes 24584 | tf_op jit(solution)/shard_map/ppermute | solution.py:22
  111.2 0.0 collective-permute-done.8
  111.2 0.8 collective-permute-done.7
  112.0 2.2 %collective-permute-done.6 = f32[2048]{0:T(1024)S(1)} collective-permute-done((f32[2048]{0:T(1024)S(1)}, f32[2048]{0:T(1024)S(1)}, u32[]{:S(2)}, u32[]{:S(2)}) %collective-permute-start.6) | collective-permute-done | bytes 8224 | tf_op jit(solution)/shard_map/ppermute | solution.py:22
  114.2 0.0 copy-done.1
  114.2 3.6 %fusion.7 = bf16[2048,1024]{0,1:T(8,128)(2,1)} fusion(bf16[2048,1024]{0,1:T(8,128)(2,1)S(1)} %copy-done.1, f32[1024,2048]{1,0:T(8,128)S(1)} %get-tuple-element.17, f32[2048]{0:T(1024)S(1)} %add_add_fusion, f32[2048]{0:T(1024)S(1)} %log_add_fusion), kind=kLoop, calls=%fused_computation.9 | loop fusion | flops 12582912 | bytes 16793600 | tf_op jit(solution)/shard_map/convert_element_type | solution.py:65
  117.8 6.4 %copy.17 = bf16[2048,1024]{1,0:T(8,128)(2,1)} copy(bf16[2048,1024]{0,1:T(8,128)(2,1)} %fusion.7) | data formatting | bytes 8388608
  (8 shorter events, 0.1 us)
Async XLA Ops:
  0.6 22.0 %copy-start = (bf16[2048,512]{1,0:T(8,128)(2,1)S(1)}, bf16[2048,512]{1,0:T(8,128)(2,1)}, u32[]{:S(2)}) copy-start(bf16[2048,512]{1,0:T(8,128)(2,1)} %param.4) | copy-start | bytes 6291460
  13.7 6.6 %collective-permute-start.2 = (f32[2048]{0:T(1024)S(1)}, f32[2048]{0:T(1024)S(1)}, u32[]{:S(2)}, u32[]{:S(2)}) collective-permute-start(f32[2048]{0:T(1024)S(1)} %log_add_fusion.1), channel_id=1, source_target_pairs={{0,1},{1,0},{2,3},{3,2},{4,5},{5,4},{6,7},{7,6},{8,9},{9,8},{10,11... | collective-permute-start | bytes 24584 | tf_op jit(solution)/shard_map/ppermute | solution.py:22
  17.0 4.0 %collective-permute-start.1 = (f32[2048]{0:T(1024)S(1)}, f32[2048]{0:T(1024)S(1)}, u32[]{:S(2)}, u32[]{:S(2)}) collective-permute-start(f32[2048]{0:T(1024)S(1)} %log_add_fusion.1), channel_id=1, source_target_pairs={{0,2},{1,3},{2,0},{3,1},{4,6},{5,7},{6,4},{7,5},{8,10},{9,11},{10,... | collective-permute-start | bytes 24584 | tf_op jit(solution)/shard_map/ppermute | solution.py:22
  18.0 4.6 %collective-permute-start = (f32[2048]{0:T(1024)S(1)}, f32[2048]{0:T(1024)S(1)}, u32[]{:S(2)}, u32[]{:S(2)}) collective-permute-start(f32[2048]{0:T(1024)S(1)} %log_add_fusion.1), channel_id=1, source_target_pairs={{0,3},{1,2},{2,1},{3,0},{4,7},{5,6},{6,5},{7,4},{8,11},{9,10},{10,... | collective-permute-start | bytes 24584 | tf_op jit(solution)/shard_map/ppermute | solution.py:22
  22.6 39.8 %copy-start.2 = (f32[8,1024]{1,0:T(8,128)S(1)}, f32[8,1024]{1,0:T(8,128)}, u32[]{:S(2)}) copy-start(f32[8,1024]{1,0:T(8,128)} %param.5) | copy-start | bytes 98308
  62.6 6.5 %collective-permute-start.5 = (f32[3,8]{1,0:T(4,128)S(1)}, f32[3,8]{1,0:T(4,128)S(1)}, u32[]{:S(2)}, u32[]{:S(2)}) collective-permute-start(f32[3,8]{1,0:T(4,128)S(1)} %pad_maximum_fusion), channel_id=1, source_target_pairs={{0,1},{1,0},{2,3},{3,2},{4,5},{5,4},{6,7},{7,6},{8,9},{9,8},{10,11... | collective-permute-start | bytes 296 | tf_op jit(solution)/shard_map/ppermute | solution.py:22
  65.8 4.0 %collective-permute-start.4 = (f32[3,8]{1,0:T(4,128)S(1)}, f32[3,8]{1,0:T(4,128)S(1)}, u32[]{:S(2)}, u32[]{:S(2)}) collective-permute-start(f32[3,8]{1,0:T(4,128)S(1)} %pad_maximum_fusion), channel_id=1, source_target_pairs={{0,2},{1,3},{2,0},{3,1},{4,6},{5,7},{6,4},{7,5},{8,10},{9,11},{10,... | collective-permute-start | bytes 296 | tf_op jit(solution)/shard_map/ppermute | solution.py:22
  67.6 4.5 %collective-permute-start.3 = (f32[3,8]{1,0:T(4,128)S(1)}, f32[3,8]{1,0:T(4,128)S(1)}, u32[]{:S(2)}, u32[]{:S(2)}) collective-permute-start(f32[3,8]{1,0:T(4,128)S(1)} %pad_maximum_fusion), channel_id=1, source_target_pairs={{0,3},{1,2},{2,1},{3,0},{4,7},{5,6},{6,5},{7,4},{8,11},{9,10},{10,... | collective-permute-start | bytes 296 | tf_op jit(solution)/shard_map/ppermute | solution.py:22
  100.3 13.9 %copy-start.1 = (bf16[2048,1024]{0,1:T(8,128)(2,1)S(1)}, bf16[2048,1024]{0,1:T(8,128)(2,1)}, u32[]{:S(2)}) copy-start(bf16[2048,1024]{0,1:T(8,128)(2,1)} %copy.14) | copy-start | bytes 12582916
  105.3 5.8 %collective-permute-start.8 = (f32[2048]{0:T(1024)S(1)}, f32[2048]{0:T(1024)S(1)}, u32[]{:S(2)}, u32[]{:S(2)}) collective-permute-start(f32[2048]{0:T(1024)S(1)} %get-tuple-element.16), channel_id=1, source_target_pairs={{0,1},{1,0},{2,3},{3,2},{4,5},{5,4},{6,7},{7,6},{8,9},{9,8},{10,11... | collective-permute-start | bytes 24584 | tf_op jit(solution)/shard_map/ppermute | solution.py:22
  107.9 4.0 %collective-permute-start.7 = (f32[2048]{0:T(1024)S(1)}, f32[2048]{0:T(1024)S(1)}, u32[]{:S(2)}, u32[]{:S(2)}) collective-permute-start(f32[2048]{0:T(1024)S(1)} %get-tuple-element.16), channel_id=1, source_target_pairs={{0,2},{1,3},{2,0},{3,1},{4,6},{5,7},{6,4},{7,5},{8,10},{9,11},{10,... | collective-permute-start | bytes 24584 | tf_op jit(solution)/shard_map/ppermute | solution.py:22
  109.6 4.6 %collective-permute-start.6 = (f32[2048]{0:T(1024)S(1)}, f32[2048]{0:T(1024)S(1)}, u32[]{:S(2)}, u32[]{:S(2)}) collective-permute-start(f32[2048]{0:T(1024)S(1)} %get-tuple-element.16), channel_id=1, source_target_pairs={{0,3},{1,2},{2,1},{3,0},{4,7},{5,6},{6,5},{7,4},{8,11},{9,10},{10,... | collective-permute-start | bytes 24584 | tf_op jit(solution)/shard_map/ppermute | solution.py:22

commit v2 on v1

v2 whole, which is shorter than its diff:
```python
import functools

import jax
import jax.numpy as jnp
from jax import lax
from jax.experimental import pallas as pl
from jax.experimental.pallas import tpu as pltpu
from jax.sharding import PartitionSpec as P

Y, Z, X, R = 4, 8, 2, 8
LANES = 128
ROWS = 256
MIB = 1 << 20


def wide_index(y, z, x):
    return (y * Z + z) * X + x


YX_GROUPS = [[wide_index(y, z, x) for y in range(Y) for x in range(X)] for z in range(Z)]
Z_GROUPS = [[wide_index(y, z, x) for z in range(Z)] for y in range(Y) for x in range(X)]


def swap(v, groups):
    return lax.all_to_all(v, "wide", 0, 0, axis_index_groups=groups)


def narrow_peers(v):
    return [lax.ppermute(v, "narrow", [(i, i ^ d) for i in range(4)]) for d in (3, 2, 1)]


def fold(parts, op):
    parts = list(parts)
    while len(parts) > 1:
        parts = [op(a, b) for a, b in zip(parts[::2], parts[1::2])]
    return parts[0]


def lane_groups(width):
    return [slice(k, k + LANES) for k in range(0, width, LANES)]


def as_row(column_sums):
    return jnp.sum(column_sums.T, axis=0, keepdims=True)


def as_column(row):
    return jnp.broadcast_to(row, (LANES, row.shape[1])).T


def stats_kernel(x_ref, out_ref):
    step = pl.program_id(0)
    groups = lane_groups(x_ref.shape[1])
    top = fold([x_ref[:, g] for g in groups], jnp.maximum).astype(jnp.float32)
    top = jnp.broadcast_to(jnp.max(top, axis=1, keepdims=True), top.shape)
    total = fold([jnp.exp(x_ref[:, g].astype(jnp.float32) - top) for g in groups], jnp.add)
    out_ref[pl.ds(step, 1), :] = top.T[:1] + jnp.log(as_row(total))


def forward_kernel(x_ref, e_ref, log_ref, out_ref, low, acc):
    step = pl.program_id(0)
    log_total = as_column(log_ref[pl.ds(step, 1), :])
    for g in lane_groups(x_ref.shape[1]):
        low[:, g] = jnp.exp(x_ref[:, g].astype(jnp.float32) - log_total).astype(jnp.bfloat16)
    part = lax.dot_general(
        e_ref[...], low[...], (((0,), (0,)), ((), ())), preferred_element_type=jnp.float32
    )

    @pl.when(step == 0)
    def _():
        acc[...] = part

    @pl.when(step > 0)
    def _():
        acc[...] += part

    @pl.when(step == pl.num_programs(0) - 1)
    def _():
        out_ref[...] = acc[...].astype(jnp.bfloat16)


def backward_kernel(x_ref, e_ref, d_ref, log_ref, probs_ref, dprobs_ref, dot_ref):
    step = pl.program_id(0)
    log_total = as_column(log_ref[pl.ds(step, 1), :])
    dprobs_ref[...] = jnp.dot(e_ref[...], d_ref[...], preferred_element_type=jnp.float32)
    parts = []
    for g in lane_groups(x_ref.shape[1]):
        probs = jnp.exp(x_ref[:, g].astype(jnp.float32) - log_total)
        probs_ref[:, g] = probs
        parts.append(probs * dprobs_ref[:, g])
    dot_ref[pl.ds(step, 1), :] = as_row(fold(parts, jnp.add))


def gradient_kernel(scale, probs_ref, dprobs_ref, dot_ref, out_ref):
    step = pl.program_id(0)
    row_dot = as_column(dot_ref[pl.ds(step, 1), :])
    for g in lane_groups(probs_ref.shape[1]):
        out_ref[:, g] = (scale * probs_ref[:, g] * (dprobs_ref[:, g] - row_dot)).astype(jnp.bfloat16)


def row_block(width):
    return pl.BlockSpec((ROWS, width), lambda i: (i, 0))


def whole(*shape):
    return pl.BlockSpec(shape, lambda i: (0,) * len(shape))


def params(mib):
    return pltpu.CompilerParams(dimension_semantics=("arbitrary",), vmem_limit_bytes=mib * MIB)


def local_log_sum(logits):
    cells, spots = logits.shape
    steps = cells // ROWS
    return pl.pallas_call(
        stats_kernel,
        grid=(steps,),
        in_specs=[row_block(spots)],
        out_specs=whole(steps, ROWS),
        out_shape=jax.ShapeDtypeStruct((steps, ROWS), jnp.float32),
        compiler_params=params(8),
        name="stats",
    )(logits)


def partial_predicted(logits, expression, log_total):
    cells, spots = logits.shape
    genes = expression.shape[1]
    steps = cells // ROWS
    return pl.pallas_call(
        forward_kernel,
        grid=(steps,),
        in_specs=[row_block(spots), row_block(genes), whole(steps, ROWS)],
        out_specs=whole(genes, spots),
        out_shape=jax.ShapeDtypeStruct((genes, spots), jnp.bfloat16),
        scratch_shapes=[
            pltpu.VMEM((ROWS, spots), jnp.bfloat16),
            pltpu.VMEM((genes, spots), jnp.float32),
        ],
        compiler_params=params(16),
        name="forward",
    )(logits, expression, log_total)


def backward(logits, expression, d_pred, log_total):
    cells, spots = logits.shape
    genes = expression.shape[1]
    steps = cells // ROWS
    return pl.pallas_call(
        backward_kernel,
        grid=(steps,),
        in_specs=[row_block(spots), row_block(genes), whole(genes, spots), whole(steps, ROWS)],
        out_specs=[row_block(spots), row_block(spots), whole(steps, ROWS)],
        out_shape=[
            jax.ShapeDtypeStruct((cells, spots), jnp.float32),
            jax.ShapeDtypeStruct((cells, spots), jnp.float32),
            jax.ShapeDtypeStruct((steps, ROWS), jnp.float32),
        ],
        compiler_params=params(16),
        name="backward",
    )(logits, expression, d_pred, log_total)


def gradient(probs, d_probs, row_dot, scale):
    cells, spots = probs.shape
    steps = cells // ROWS
    return pl.pallas_call(
        functools.partial(gradient_kernel, scale),
        grid=(steps,),
        in_specs=[row_block(spots), row_block(spots), whole(steps, ROWS)],
        out_specs=row_block(spots),
        out_shape=jax.ShapeDtypeStruct((cells, spots), jnp.bfloat16),
        compiler_params=params(16),
        name="gradient",
    )(probs, d_probs, row_dot)


def body(logits, expression, measured):
    spots = logits.shape[1]
    local_log = local_log_sum(logits)
    logs = [local_log] + narrow_peers(local_log)
    top = fold(logs, jnp.maximum)
    log_total = top + jnp.log(fold([jnp.exp(v - top) for v in logs], jnp.add))
    part = partial_predicted(logits, expression, log_total)
    part = part.reshape(Y, Z, X, R, spots).transpose(0, 2, 1, 3, 4).reshape(Y * X, Z * R, spots)
    part = swap(part, YX_GROUPS).astype(jnp.float32).sum(0).astype(jnp.bfloat16)
    part = swap(part.reshape(Z, R, spots), Z_GROUPS)
    predicted = part.astype(jnp.float32).sum(0)
    sums = jnp.stack(
        [
            jnp.sum(predicted * measured, axis=1),
            jnp.sum(predicted * predicted, axis=1),
            jnp.sum(measured * measured, axis=1),
        ]
    )
    sums = sums + fold([jnp.zeros_like(sums)] + narrow_peers(sums), jnp.add)
    inner, pred_sq, meas_sq = sums[0], sums[1], sums[2]
    norm_p = jnp.sqrt(pred_sq + 1e-06)
    norm_m = jnp.sqrt(meas_sq + 1e-06)
    similarity = inner / (norm_p * norm_m)
    share = (
        -measured / (norm_p * norm_m)[:, None]
        + (inner / (norm_p**3 * norm_m))[:, None] * predicted
    ).astype(jnp.bfloat16)
    share = swap(jnp.broadcast_to(share[None], (Z, R, spots)), Z_GROUPS).reshape(Z * R, spots)
    share = swap(jnp.broadcast_to(share[None], (Y * X, Z * R, spots)), YX_GROUPS)
    d_pred = share.reshape(Y, X, Z, R, spots).transpose(0, 2, 1, 3, 4).reshape(Y * X * Z * R, spots)
    probs, d_probs, row_dot = backward(logits, expression, d_pred, log_total)
    row_dot = fold([row_dot] + narrow_peers(row_dot), jnp.add)
    grad = gradient(probs, d_probs, row_dot, float(spots * lax.axis_size("narrow")))
    return (grad, similarity)


def solution(mesh):
    placed = (P("wide", "narrow"), P("wide", None), P("wide", "narrow"))
    return jax.shard_map(
        body,
        mesh=mesh,
        in_specs=placed,
        out_specs=(P("wide", "narrow"), P("wide")),
        check_vma=False,
    )
```

time: 125 us -> 115 us (0.920)
  Pallas kernels: 0 us -> 18.7 us
  other arithmetic: 11 us -> 1.02 us
  matrix products: 9.57 us -> 0 us
  local copies, waits for them, and re-layouts: 13.3 us -> 4.06 us
    pallas_call x0 -> x4, Pallas kernels: none -> 18.7 us  [the longest x1 7.05 us: partial_predicted(): pl.pallas_call(forward_kernel, grid=(steps,), in_specs=[row_block(spots),...]
    dot_general x2 -> x0, matrix products: 9.57 us -> none  [the longest x1 4.99 us: body(): d_probs = jnp.dot(expression, d_pred, preferred_element_type=jnp.float32)]
    unnamed x8 -> x12, local copies, waits for them, and re-layouts: 13 us -> 3.79 us
    reduce_sum x1 -> x0, other arithmetic: 3.59 us -> none  [body(): jnp.sum(jnp.exp(values - local_top[:, None]), axis=1)]
    convert_element_type x1 -> x0, other arithmetic: 3.58 us -> none  [body(): (total_spots * probs * (d_probs - row_dot[:, None])).astype(jnp.bfloat16)]
    reduce_max x2 -> x0, other arithmetic: 2.84 us -> none  [body(): local_top = jnp.max(values, axis=1)]
where the time goes in v2:
time: 115 us; the launch traced here: 114 us
  blocking collectives  62.5 us (54%)
  starting transfers between devices  18.9 us (16%)
  Pallas kernels  18.7 us (16%)
  waiting for transfers between devices  8.38 us (7%)
  local copies, waits for them, and re-layouts  4.06 us (4%)
    all_to_all x4, blocking collectives, swap(): return lax.all_to_all(v, 'wide', 0, 0, axis_index_groups=groups)  62.5 us
    ppermute x9, starting transfers between devices, narrow_peers(): lax.ppermute(v, 'narrow', [(i, i ^ d) for i in range(4)])  18.9 us
    ppermute x9, waiting for transfers between devices, narrow_peers(): lax.ppermute(v, 'narrow', [(i, i ^ d) for i in range(4)])  8.38 us
    pallas_call x1, Pallas kernels, partial_predicted(): pl.pallas_call(forward_kernel, grid=(steps,), in_specs=[row_block(spots),...  7.05 us
    pallas_call x1, Pallas kernels, backward(): pl.pallas_call(backward_kernel, grid=(steps,), in_specs=[row_block(spots)...  4.53 us
    pallas_call x1, Pallas kernels, gradient(): pl.pallas_call(functools.partial(gradient_kernel, scale), grid=(steps,),...  4.4 us
    unnamed x12, local copies, waits for them, and re-layouts  3.79 us
    pallas_call x1, Pallas kernels, local_log_sum(): pl.pallas_call(stats_kernel, grid=(steps,), in_specs=[row_block(spots)],...  2.75 us
  transfers between devices with their start and end apart: 9, of which 6 were waited for; matrix products, arithmetic and copies ran while one was open for 0% of the time, Pallas kernels for 0%

profile of v2, /device:TPU:1, one launch (start us, length us, event | category | flops | bytes accessed | tf_op | source)
XLA Modules:
  0.0 114.3 jit_solution(5596345744134543470)
XLA Ops:
  0.6 0.0 copy-start
  0.6 2.2 %copy-done = bf16[2048,1024]{1,0:T(8,128)(2,1)S(1)} copy-done((bf16[2048,1024]{1,0:T(8,128)(2,1)S(1)}, bf16[2048,1024]{1,0:T(8,128)(2,1)}, u32[]{:S(2)}) %copy-start) | copy-done | bytes 4194328
  2.8 0.0 copy-start.1
  2.8 2.7 %stats.1 = f32[8,256]{1,0:T(8,128)S(1)} custom-call(bf16[2048,1024]{1,0:T(8,128)(2,1)S(1)} %copy-done), custom_call_target="tpu_custom_call" | custom-call | tf_op jit(solution)/shard_map/stats/pallas_call | solution.py:116
  5.6 3.3 %collective-permute-start.2 = (f32[8,256]{1,0:T(8,128)S(1)}, f32[8,256]{1,0:T(8,128)S(1)}, u32[]{:S(2)}, u32[]{:S(2)}) collective-permute-start(f32[8,256]{1,0:T(8,128)S(1)} %stats.1), channel_id=1, source_target_pairs={{0,1},{1,0},{2,3},{3,2},{4,5},{5,4},{6,7},{7,6},{8,9},{9,8},{10,11... | collective-permute-start | bytes 24584 | tf_op jit(solution)/shard_map/ppermute | solution.py:29
  8.9 1.0 collective-permute-start.1
  9.9 2.2 %collective-permute-start = (f32[8,256]{1,0:T(8,128)S(1)}, f32[8,256]{1,0:T(8,128)S(1)}, u32[]{:S(2)}, u32[]{:S(2)}) collective-permute-start(f32[8,256]{1,0:T(8,128)S(1)} %stats.1), channel_id=1, source_target_pairs={{0,3},{1,2},{2,1},{3,0},{4,7},{5,6},{6,5},{7,4},{8,11},{9,10},{10,... | collective-permute-start | bytes 24584 | tf_op jit(solution)/shard_map/ppermute | solution.py:29
  12.1 0.0 collective-permute-done.2
  12.1 0.8 collective-permute-done.1
  12.9 1.6 %collective-permute-done = f32[8,256]{1,0:T(8,128)S(1)} collective-permute-done((f32[8,256]{1,0:T(8,128)S(1)}, f32[8,256]{1,0:T(8,128)S(1)}, u32[]{:S(2)}, u32[]{:S(2)}) %collective-permute-start) | collective-permute-done | bytes 8224 | tf_op jit(solution)/shard_map/ppermute | solution.py:29
  14.5 0.0 copy-done.1
  14.6 0.0 copy-start.3
  14.6 1.6 %copy-done.3 = bf16[2048,512]{1,0:T(8,128)(2,1)S(1)} copy-done((bf16[2048,512]{1,0:T(8,128)(2,1)S(1)}, bf16[2048,512]{1,0:T(8,128)(2,1)}, u32[]{:S(2)}) %copy-start.3) | copy-done | bytes 2097176
  16.1 7.1 %forward.1 = bf16[512,1024]{1,0:T(8,128)(2,1)S(1)} custom-call(bf16[2048,1024]{1,0:T(8,128)(2,1)S(1)} %copy-done.1, bf16[2048,512]{1,0:T(8,128)(2,1)S(1)} %copy-done.3, f32[8,256]{1,0:T(8,128)S(1)} %log_add_fusion.log_ref), custom_call_target="tpu_custom_call" | custom-call | tf_op jit(solution)/shard_map/forward/pallas_call | solution.py:131
  23.2 0.0 copy-start.5
  23.2 0.1 copy.7
  23.3 18.9 %all_to_all.20 = bf16[8,64,1024]{2,1,0:T(8,128)(2,1)S(1)} all-to-all(bf16[8,64,1024]{2,1,0:T(8,128)(2,1)S(1)} %bitcast.26), channel_id=1, replica_groups={{0,4,64,68,128,132,192,196},{8,12,72,76,136,140,200,204},{16,20,80,84,1..., dimensions={0} | all-to-all | bytes 2097152 | tf_op jit(solution)/shard_map/all_to_all | solution.py:25
  42.1 0.0 copy-start.4
  42.1 0.2 reduce_sum.48
  42.3 0.0 copy-start.2
  42.3 16.3 %all_to_all.21 = bf16[8,8,1024]{2,1,0:T(8,128)(2,1)S(1)} all-to-all(bf16[8,8,1024]{2,1,0:T(8,128)(2,1)S(1)} %bitcast.28), channel_id=1, replica_groups={{0,8,16,24,32,40,48,56},{4,12,20,28,36,44,52,60},{64,72,80,88,96,104,11..., dimensions={0} | all-to-all | bytes 262144 | tf_op jit(solution)/shard_map/all_to_all | solution.py:25
  58.7 0.0 copy-done.5
  58.7 0.2 multiply_reduce_fusion.2
  58.8 3.2 %collective-permute-start.5 = (f32[3,8]{1,0:T(4,128)S(1)}, f32[3,8]{1,0:T(4,128)S(1)}, u32[]{:S(2)}, u32[]{:S(2)}) collective-permute-start(f32[3,8]{1,0:T(4,128)S(1)} %pad_maximum_fusion), channel_id=1, source_target_pairs={{0,1},{1,0},{2,3},{3,2},{4,5},{5,4},{6,7},{7,6},{8,9},{9,8},{10,11... | collective-permute-start | bytes 296 | tf_op jit(solution)/shard_map/ppermute | solution.py:29
  62.1 1.7 %collective-permute-start.4 = (f32[3,8]{1,0:T(4,128)S(1)}, f32[3,8]{1,0:T(4,128)S(1)}, u32[]{:S(2)}, u32[]{:S(2)}) collective-permute-start(f32[3,8]{1,0:T(4,128)S(1)} %pad_maximum_fusion), channel_id=1, source_target_pairs={{0,2},{1,3},{2,0},{3,1},{4,6},{5,7},{6,4},{7,5},{8,10},{9,11},{10,... | collective-permute-start | bytes 296 | tf_op jit(solution)/shard_map/ppermute | solution.py:29
  63.8 1.5 %collective-permute-start.3 = (f32[3,8]{1,0:T(4,128)S(1)}, f32[3,8]{1,0:T(4,128)S(1)}, u32[]{:S(2)}, u32[]{:S(2)}) collective-permute-start(f32[3,8]{1,0:T(4,128)S(1)} %pad_maximum_fusion), channel_id=1, source_target_pairs={{0,3},{1,2},{2,1},{3,0},{4,7},{5,6},{6,5},{7,4},{8,11},{9,10},{10,... | collective-permute-start | bytes 296 | tf_op jit(solution)/shard_map/ppermute | solution.py:29
  65.3 0.0 collective-permute-done.5
  65.3 0.7 collective-permute-done.4
  66.0 2.3 %collective-permute-done.3 = f32[3,8]{1,0:T(4,128)S(1)} collective-permute-done((f32[3,8]{1,0:T(4,128)S(1)}, f32[3,8]{1,0:T(4,128)S(1)}, u32[]{:S(2)}, u32[]{:S(2)}) %collective-permute-start.3) | collective-permute-done | bytes 128 | tf_op jit(solution)/shard_map/ppermute | solution.py:29
  68.3 0.5 bitcast_divide_fusion
  68.9 0.1 add_convert_fusion
  69.0 10.8 %all_to_all.22 = bf16[8,8,1024]{2,1,0:T(8,128)(2,1)S(1)} all-to-all(bf16[8,8,1024]{2,1,0:T(8,128)(2,1)S(1)} %broadcast_in_dim.6), channel_id=1, replica_groups={{0,8,16,24,32,40,48,56},{4,12,20,28,36,44,52,60},{64,72,80,88,96,104,11..., dimensions={0} | all-to-all | bytes 262144 | tf_op jit(solution)/shard_map/all_to_all | solution.py:25
  79.8 0.1 broadcast_in_dim.8
  79.9 16.6 %all_to_all.23 = bf16[8,64,1024]{2,1,0:T(8,128)(2,1)S(1)} all-to-all(bf16[8,64,1024]{2,1,0:T(8,128)(2,1)S(1)} %broadcast_in_dim.8), channel_id=1, replica_groups={{0,4,64,68,128,132,192,196},{8,12,72,76,136,140,200,204},{16,20,80,84,1..., dimensions={0} | all-to-all | bytes 2097152 | tf_op jit(solution)/shard_map/all_to_all | solution.py:25
  96.5 0.1 copy.8
  96.5 0.0 copy-done.4
  96.5 0.0 copy-done.2
  96.5 4.5 %backward.1 = (f32[2048,1024]{1,0:T(8,128)S(1)}, f32[2048,1024]{1,0:T(8,128)S(1)}, f32[8,256]{1,0:T(8,128)S(1)}) custom-call(bf16[2048,1024]{1,0:T(8,128)(2,1)S(1)} %copy-done.2, bf16[2048,512]{1,0:T(8,128)(2,1)S(1)} %copy-done.4, bf16[512,1024]{1,0:T(8,128)(2,1)S(1)} %bitcast.24, f32[8,256]{1,0:T(8,128)S(1)} %log_add_fusion.log_ref), custom_call_target="tpu_custom_call" | custom-call | tf_op jit(solution)/shard_map/backward/pallas_call | solution.py:150
  101.1 2.6 %collective-permute-start.8 = (f32[8,256]{1,0:T(8,128)S(1)}, f32[8,256]{1,0:T(8,128)S(1)}, u32[]{:S(2)}, u32[]{:S(2)}) collective-permute-start(f32[8,256]{1,0:T(8,128)S(1)} %get-tuple-element.7), channel_id=1, source_target_pairs={{0,1},{1,0},{2,3},{3,2},{4,5},{5,4},{6,7},{7,6},{8,9},{9,8},{10,11... | collective-permute-start | bytes 24584 | tf_op jit(solution)/shard_map/ppermute | solution.py:29
  103.7 1.6 %collective-permute-start.7 = (f32[8,256]{1,0:T(8,128)S(1)}, f32[8,256]{1,0:T(8,128)S(1)}, u32[]{:S(2)}, u32[]{:S(2)}) collective-permute-start(f32[8,256]{1,0:T(8,128)S(1)} %get-tuple-element.7), channel_id=1, source_target_pairs={{0,2},{1,3},{2,0},{3,1},{4,6},{5,7},{6,4},{7,5},{8,10},{9,11},{10,... | collective-permute-start | bytes 24584 | tf_op jit(solution)/shard_map/ppermute | solution.py:29
  105.3 1.6 %collective-permute-start.6 = (f32[8,256]{1,0:T(8,128)S(1)}, f32[8,256]{1,0:T(8,128)S(1)}, u32[]{:S(2)}, u32[]{:S(2)}) collective-permute-start(f32[8,256]{1,0:T(8,128)S(1)} %get-tuple-element.7), channel_id=1, source_target_pairs={{0,3},{1,2},{2,1},{3,0},{4,7},{5,6},{6,5},{7,4},{8,11},{9,10},{10,... | collective-permute-start | bytes 24584 | tf_op jit(solution)/shard_map/ppermute | solution.py:29
  106.9 0.0 collective-permute-done.8
  106.9 0.8 collective-permute-done.7
  107.7 2.2 %collective-permute-done.6 = f32[8,256]{1,0:T(8,128)S(1)} collective-permute-done((f32[8,256]{1,0:T(8,128)S(1)}, f32[8,256]{1,0:T(8,128)S(1)}, u32[]{:S(2)}, u32[]{:S(2)}) %collective-permute-start.6) | collective-permute-done | bytes 8224 | tf_op jit(solution)/shard_map/ppermute | solution.py:29
  109.9 4.4 %gradient.1 = bf16[2048,1024]{1,0:T(8,128)(2,1)} custom-call(f32[2048,1024]{1,0:T(8,128)S(1)} %get-tuple-element.5.probs_ref, f32[2048,1024]{1,0:T(8,128)S(1)} %get-tuple-element.6.dprobs_ref, f32[8,256]{1,0:T(8,128)S(1)} %add_add_fusion.dot_ref), custom_call_target="tpu_custom_call" | custom-call | tf_op jit(solution)/shard_map/gradient/pallas_call | solution.py:168
  (6 shorter events, 0.1 us)
Async XLA Ops:
  0.6 2.2 %copy-start = (bf16[2048,1024]{1,0:T(8,128)(2,1)S(1)}, bf16[2048,1024]{1,0:T(8,128)(2,1)}, u32[]{:S(2)}) copy-start(bf16[2048,1024]{1,0:T(8,128)(2,1)} %x_ref.5) | copy-start | bytes 12582916
  2.8 11.7 %copy-start.1 = (bf16[2048,1024]{1,0:T(8,128)(2,1)S(1)}, bf16[2048,1024]{1,0:T(8,128)(2,1)}, u32[]{:S(2)}) copy-start(bf16[2048,1024]{1,0:T(8,128)(2,1)} %x_ref.5) | copy-start | bytes 12582916
  5.6 6.6 %collective-permute-start.2 = (f32[8,256]{1,0:T(8,128)S(1)}, f32[8,256]{1,0:T(8,128)S(1)}, u32[]{:S(2)}, u32[]{:S(2)}) collective-permute-start(f32[8,256]{1,0:T(8,128)S(1)} %stats.1), channel_id=1, source_target_pairs={{0,1},{1,0},{2,3},{3,2},{4,5},{5,4},{6,7},{7,6},{8,9},{9,8},{10,11... | collective-permute-start | bytes 24584 | tf_op jit(solution)/shard_map/ppermute | solution.py:29
  8.9 4.0 %collective-permute-start.1 = (f32[8,256]{1,0:T(8,128)S(1)}, f32[8,256]{1,0:T(8,128)S(1)}, u32[]{:S(2)}, u32[]{:S(2)}) collective-permute-start(f32[8,256]{1,0:T(8,128)S(1)} %stats.1), channel_id=1, source_target_pairs={{0,2},{1,3},{2,0},{3,1},{4,6},{5,7},{6,4},{7,5},{8,10},{9,11},{10,... | collective-permute-start | bytes 24584 | tf_op jit(solution)/shard_map/ppermute | solution.py:29
  9.9 4.6 %collective-permute-start = (f32[8,256]{1,0:T(8,128)S(1)}, f32[8,256]{1,0:T(8,128)S(1)}, u32[]{:S(2)}, u32[]{:S(2)}) collective-permute-start(f32[8,256]{1,0:T(8,128)S(1)} %stats.1), channel_id=1, source_target_pairs={{0,3},{1,2},{2,1},{3,0},{4,7},{5,6},{6,5},{7,4},{8,11},{9,10},{10,... | collective-permute-start | bytes 24584 | tf_op jit(solution)/shard_map/ppermute | solution.py:29
  14.6 1.6 %copy-start.3 = (bf16[2048,512]{1,0:T(8,128)(2,1)S(1)}, bf16[2048,512]{1,0:T(8,128)(2,1)}, u32[]{:S(2)}) copy-start(bf16[2048,512]{1,0:T(8,128)(2,1)} %e_ref.3) | copy-start | bytes 6291460
  23.2 35.5 %copy-start.5 = (f32[8,1024]{1,0:T(8,128)S(1)}, f32[8,1024]{1,0:T(8,128)}, u32[]{:S(2)}) copy-start(f32[8,1024]{1,0:T(8,128)} %param.5) | copy-start | bytes 98308
  42.1 54.4 %copy-start.4 = (bf16[2048,512]{1,0:T(8,128)(2,1)S(1)}, bf16[2048,512]{1,0:T(8,128)(2,1)}, u32[]{:S(2)}) copy-start(bf16[2048,512]{1,0:T(8,128)(2,1)} %e_ref.3) | copy-start | bytes 6291460
  42.3 54.2 %copy-start.2 = (bf16[2048,1024]{1,0:T(8,128)(2,1)S(1)}, bf16[2048,1024]{1,0:T(8,128)(2,1)}, u32[]{:S(2)}) copy-start(bf16[2048,1024]{1,0:T(8,128)(2,1)} %x_ref.5) | copy-start | bytes 12582916
  58.8 6.5 %collective-permute-start.5 = (f32[3,8]{1,0:T(4,128)S(1)}, f32[3,8]{1,0:T(4,128)S(1)}, u32[]{:S(2)}, u32[]{:S(2)}) collective-permute-start(f32[3,8]{1,0:T(4,128)S(1)} %pad_maximum_fusion), channel_id=1, source_target_pairs={{0,1},{1,0},{2,3},{3,2},{4,5},{5,4},{6,7},{7,6},{8,9},{9,8},{10,11... | collective-permute-start | bytes 296 | tf_op jit(solution)/shard_map/ppermute | solution.py:29
  62.1 4.0 %collective-permute-start.4 = (f32[3,8]{1,0:T(4,128)S(1)}, f32[3,8]{1,0:T(4,128)S(1)}, u32[]{:S(2)}, u32[]{:S(2)}) collective-permute-start(f32[3,8]{1,0:T(4,128)S(1)} %pad_maximum_fusion), channel_id=1, source_target_pairs={{0,2},{1,3},{2,0},{3,1},{4,6},{5,7},{6,4},{7,5},{8,10},{9,11},{10,... | collective-permute-start | bytes 296 | tf_op jit(solution)/shard_map/ppermute | solution.py:29
  63.8 4.5 %collective-permute-start.3 = (f32[3,8]{1,0:T(4,128)S(1)}, f32[3,8]{1,0:T(4,128)S(1)}, u32[]{:S(2)}, u32[]{:S(2)}) collective-permute-start(f32[3,8]{1,0:T(4,128)S(1)} %pad_maximum_fusion), channel_id=1, source_target_pairs={{0,3},{1,2},{2,1},{3,0},{4,7},{5,6},{6,5},{7,4},{8,11},{9,10},{10,... | collective-permute-start | bytes 296 | tf_op jit(solution)/shard_map/ppermute | solution.py:29
  101.1 5.8 %collective-permute-start.8 = (f32[8,256]{1,0:T(8,128)S(1)}, f32[8,256]{1,0:T(8,128)S(1)}, u32[]{:S(2)}, u32[]{:S(2)}) collective-permute-start(f32[8,256]{1,0:T(8,128)S(1)} %get-tuple-element.7), channel_id=1, source_target_pairs={{0,1},{1,0},{2,3},{3,2},{4,5},{5,4},{6,7},{7,6},{8,9},{9,8},{10,11... | collective-permute-start | bytes 24584 | tf_op jit(solution)/shard_map/ppermute | solution.py:29
  103.7 4.0 %collective-permute-start.7 = (f32[8,256]{1,0:T(8,128)S(1)}, f32[8,256]{1,0:T(8,128)S(1)}, u32[]{:S(2)}, u32[]{:S(2)}) collective-permute-start(f32[8,256]{1,0:T(8,128)S(1)} %get-tuple-element.7), channel_id=1, source_target_pairs={{0,2},{1,3},{2,0},{3,1},{4,6},{5,7},{6,4},{7,5},{8,10},{9,11},{10,... | collective-permute-start | bytes 24584 | tf_op jit(solution)/shard_map/ppermute | solution.py:29
  105.3 4.6 %collective-permute-start.6 = (f32[8,256]{1,0:T(8,128)S(1)}, f32[8,256]{1,0:T(8,128)S(1)}, u32[]{:S(2)}, u32[]{:S(2)}) collective-permute-start(f32[8,256]{1,0:T(8,128)S(1)} %get-tuple-element.7), channel_id=1, source_target_pairs={{0,3},{1,2},{2,1},{3,0},{4,7},{5,6},{6,5},{7,4},{8,11},{9,10},{10,... | collective-permute-start | bytes 24584 | tf_op jit(solution)/shard_map/ppermute | solution.py:29

commit v3 on v1

v3 whole, which is shorter than its diff:
```python
import functools

import jax
import jax.numpy as jnp
from jax import lax
from jax.experimental import pallas as pl
from jax.experimental.pallas import tpu as pltpu
from jax.sharding import PartitionSpec as P

Y, Z, X, R = 4, 8, 2, 8
LANES = 128
ROWS = 256
STATS_MIB = 58
MIB = 1 << 20


def wide_index(y, z, x):
    return (y * Z + z) * X + x


YX_GROUPS = [[wide_index(y, z, x) for y in range(Y) for x in range(X)] for z in range(Z)]
Z_GROUPS = [[wide_index(y, z, x) for z in range(Z)] for y in range(Y) for x in range(X)]


def swap(v, groups):
    return lax.all_to_all(v, "wide", 0, 0, axis_index_groups=groups)


def narrow_peers(v):
    return [lax.ppermute(v, "narrow", [(i, i ^ d) for i in range(4)]) for d in (3, 2, 1)]


def fold(parts, op):
    parts = list(parts)
    while len(parts) > 1:
        parts = [op(a, b) for a, b in zip(parts[::2], parts[1::2])]
    return parts[0]


def lane_groups(width):
    return [slice(k, k + LANES) for k in range(0, width, LANES)]


def as_row(column_sums):
    return jnp.sum(column_sums.T, axis=0, keepdims=True)


def as_column(row):
    return jnp.broadcast_to(row, (LANES, row.shape[1])).T


def block(i):
    return pl.ds(pl.multiple_of(i * ROWS, ROWS), ROWS)


def stats_kernel(x_hbm, out_ref, x_ref, sems):
    cells, spots = x_ref.shape
    steps = cells // ROWS
    groups = lane_groups(spots)

    def copy(i):
        return pltpu.make_async_copy(x_hbm.at[block(i), :], x_ref.at[block(i), :], sems.at[i])

    for i in range(steps):
        copy(i).start()

    @pl.loop(0, steps)
    def _(i):
        copy(i).wait()
        rows = block(i)
        top = fold([x_ref[rows, g] for g in groups], jnp.maximum).astype(jnp.float32)
        total = fold([jnp.exp(x_ref[rows, g].astype(jnp.float32) - top) for g in groups], jnp.add)
        top, total = top.T, total.T
        row_top = jnp.max(top, axis=0, keepdims=True)
        row_total = jnp.sum(total * jnp.exp(top - row_top), axis=0, keepdims=True)
        out_ref[pl.ds(i, 1), :] = row_top + jnp.log(row_total)


def transpose_kernel(e_ref, out_ref):
    @pl.loop(0, e_ref.shape[0] // ROWS)
    def _(i):
        out_ref[:, block(i)] = e_ref[block(i), :].T


def forward_kernel(tile, x_ref, et_ref, log_ref, part_ref, probs_ref, low, column):
    cells, spots = x_ref.shape

    @pl.loop(0, cells // ROWS)
    def _(i):
        column[block(i), :] = as_column(log_ref[pl.ds(i, 1), :])

    tiles = [slice(k, k + tile) for k in range(0, spots, tile)]

    def fill(cols):
        for k in range(cols.start, cols.stop, LANES):
            g = slice(k, k + LANES)
            probs = jnp.exp(x_ref[:, g].astype(jnp.float32) - column[...])
            probs_ref[:, g] = probs
            low[:, g] = probs.astype(jnp.bfloat16)

    fill(tiles[0])
    for cols, later in zip(tiles, tiles[1:] + [None]):
        part = jnp.dot(et_ref[...], low[:, cols], preferred_element_type=jnp.float32)
        part_ref[:, cols] = part.astype(jnp.bfloat16)
        if later is not None:
            fill(later)


def backward_kernel(size, probs_ref, e_ref, d_ref, dprobs_ref, dot_ref):
    cells, spots = probs_ref.shape

    def row_dots(first):
        for k in range(first, first + size, ROWS):
            rows = slice(k, k + ROWS)
            parts = [probs_ref[rows, g] * dprobs_ref[rows, g] for g in lane_groups(spots)]
            dot_ref[k // ROWS : k // ROWS + 1, :] = as_row(fold(parts, jnp.add))

    for first in range(0, cells, size):
        rows = slice(first, first + size)
        dprobs_ref[rows, :] = jnp.dot(e_ref[rows, :], d_ref[...], preferred_element_type=jnp.float32)
        if first:
            row_dots(first - size)
    row_dots(cells - size)


def gradient_kernel(scale, size, probs_ref, dprobs_ref, dot_ref, out_hbm, buf, sems):
    cells, spots = probs_ref.shape
    steps = cells // size
    inner = size // ROWS

    def copy(i):
        rows = pl.ds(pl.multiple_of(i * size, size), size)
        return pltpu.make_async_copy(buf.at[rows, :], out_hbm.at[rows, :], sems.at[i])

    @pl.loop(0, steps)
    def _(i):
        for h in range(inner):
            rows = block(i * inner + h)
            row_dot = as_column(dot_ref[pl.ds(i * inner + h, 1), :])
            for g in lane_groups(spots):
                grad = scale * probs_ref[rows, g] * (dprobs_ref[rows, g] - row_dot)
                buf[rows, g] = grad.astype(jnp.bfloat16)
        copy(i).start()

    for i in range(steps):
        copy(i).wait()


VMEM = pl.BlockSpec(memory_space=pltpu.VMEM)
HBM = pl.BlockSpec(memory_space=pltpu.HBM)


def params(mib):
    return pltpu.CompilerParams(vmem_limit_bytes=mib * MIB)


def cost(flops, moved, transcendentals=0):
    return pl.CostEstimate(flops=flops, bytes_accessed=moved, transcendentals=transcendentals)


def local_log_sum(logits):
    cells, spots = logits.shape
    steps = cells // ROWS
    return pl.pallas_call(
        stats_kernel,
        in_specs=[HBM],
        out_specs=VMEM,
        out_shape=jax.ShapeDtypeStruct((steps, ROWS), jnp.float32),
        scratch_shapes=[
            pltpu.VMEM((cells, spots), logits.dtype),
            pltpu.SemaphoreType.DMA((steps,)),
        ],
        compiler_params=params(STATS_MIB),
        cost_estimate=cost(cells * spots * 6, cells * spots * 2, cells * spots),
        name="stats",
    )(logits)


def transposed(expression):
    cells, genes = expression.shape
    return pl.pallas_call(
        transpose_kernel,
        in_specs=[VMEM],
        out_specs=VMEM,
        out_shape=jax.ShapeDtypeStruct((genes, cells), expression.dtype),
        compiler_params=params(8),
        cost_estimate=cost(0, cells * genes * 4),
        name="transpose",
    )(expression)


def partial_predicted(logits, expression_t, log_total):
    cells, spots = logits.shape
    genes = expression_t.shape[0]
    return pl.pallas_call(
        functools.partial(forward_kernel, 256),
        in_specs=[VMEM] * 3,
        out_specs=[VMEM] * 2,
        out_shape=[
            jax.ShapeDtypeStruct((genes, spots), jnp.bfloat16),
            jax.ShapeDtypeStruct((cells, spots), jnp.float32),
        ],
        scratch_shapes=[
            pltpu.VMEM((cells, spots), jnp.bfloat16),
            pltpu.VMEM((cells, LANES), jnp.float32),
        ],
        compiler_params=params(24),
        cost_estimate=cost(2 * cells * spots * genes, cells * spots * 4, cells * spots),
        name="forward",
    )(logits, expression_t, log_total)


def backward(probs, expression, d_pred):
    cells, spots = probs.shape
    genes = expression.shape[1]
    return pl.pallas_call(
        functools.partial(backward_kernel, 512),
        in_specs=[VMEM] * 3,
        out_specs=[VMEM] * 2,
        out_shape=[
            jax.ShapeDtypeStruct((cells, spots), jnp.float32),
            jax.ShapeDtypeStruct((cells // ROWS, ROWS), jnp.float32),
        ],
        compiler_params=params(12),
        cost_estimate=cost(2 * cells * spots * genes, cells * spots * 4),
        name="backward",
    )(probs, expression, d_pred)


def gradient(probs, d_probs, row_dot, scale):
    cells, spots = probs.shape
    size = 512
    return pl.pallas_call(
        functools.partial(gradient_kernel, scale, size),
        in_specs=[VMEM] * 3,
        out_specs=HBM,
        out_shape=jax.ShapeDtypeStruct((cells, spots), jnp.bfloat16),
        scratch_shapes=[
            pltpu.VMEM((cells, spots), jnp.bfloat16),
            pltpu.SemaphoreType.DMA((cells // size,)),
        ],
        compiler_params=params(12),
        cost_estimate=cost(cells * spots * 3, cells * spots * 4),
        name="gradient",
    )(probs, d_probs, row_dot)


def body(logits, expression, measured):
    spots = logits.shape[1]
    local_log = local_log_sum(logits)
    expression_t = transposed(expression)
    logs = [local_log] + narrow_peers(local_log)
    top = fold(logs, jnp.maximum)
    log_total = top + jnp.log(fold([jnp.exp(v - top) for v in logs], jnp.add))
    part, probs = partial_predicted(logits, expression_t, log_total)
    part = part.reshape(Y, Z, X, R, spots).transpose(0, 2, 1, 3, 4).reshape(Y * X, Z * R, spots)
    part = swap(part, YX_GROUPS).astype(jnp.float32).sum(0).astype(jnp.bfloat16)
    part = swap(part.reshape(Z, R, spots), Z_GROUPS)
    predicted = part.astype(jnp.float32).sum(0)
    sums = jnp.stack(
        [
            jnp.sum(predicted * measured, axis=1),
            jnp.sum(predicted * predicted, axis=1),
            jnp.sum(measured * measured, axis=1),
        ]
    )
    sums = sums + fold([jnp.zeros_like(sums)] + narrow_peers(sums), jnp.add)
    inner, pred_sq, meas_sq = sums[0], sums[1], sums[2]
    norm_p = jnp.sqrt(pred_sq + 1e-06)
    norm_m = jnp.sqrt(meas_sq + 1e-06)
    similarity = inner / (norm_p * norm_m)
    share = (
        -measured / (norm_p * norm_m)[:, None]
        + (inner / (norm_p**3 * norm_m))[:, None] * predicted
    ).astype(jnp.bfloat16)
    share = swap(jnp.broadcast_to(share[None], (Z, R, spots)), Z_GROUPS).reshape(Z * R, spots)
    share = swap(jnp.broadcast_to(share[None], (Y * X, Z * R, spots)), YX_GROUPS)
    d_pred = share.reshape(Y, X, Z, R, spots).transpose(0, 2, 1, 3, 4).reshape(Y * X * Z * R, spots)
    d_probs, row_dot = backward(probs, expression, d_pred)
    row_dot = fold([row_dot] + narrow_peers(row_dot), jnp.add)
    grad = gradient(probs, d_probs, row_dot, float(spots * lax.axis_size("narrow")))
    return (grad, similarity)


def solution(mesh):
    placed = (P("wide", "narrow"), P("wide", None), P("wide", "narrow"))
    return jax.shard_map(
        body,
        mesh=mesh,
        in_specs=placed,
        out_specs=(P("wide", "narrow"), P("wide")),
        check_vma=False,
    )
```

time: 125 us -> 116 us (0.928)
  Pallas kernels: 0 us -> 14 us
  matrix products: 9.57 us -> 0 us
  other arithmetic: 11 us -> 1.71 us
  local copies, waits for them, and re-layouts: 13.3 us -> 10.3 us
    pallas_call x0 -> x5, Pallas kernels: none -> 14 us  [the longest x1 4.26 us: local_log_sum(): pl.pallas_call(stats_kernel, in_specs=[HBM], out_specs=VMEM, out_shape=ja...]
    dot_general x2 -> x0, matrix products: 9.57 us -> none  [the longest x1 4.99 us: body(): d_probs = jnp.dot(expression, d_pred, preferred_element_type=jnp.float32)]
    reduce_sum x1 -> x0, other arithmetic: 3.59 us -> none  [body(): jnp.sum(jnp.exp(values - local_top[:, None]), axis=1)]
    convert_element_type x1 -> x0, other arithmetic: 3.58 us -> none  [body(): (total_spots * probs * (d_probs - row_dot[:, None])).astype(jnp.bfloat16)]
    unnamed x8 -> x12, local copies, waits for them, and re-layouts: 13 us -> 9.98 us
    reduce_max x2 -> x0, other arithmetic: 2.84 us -> none  [body(): local_top = jnp.max(values, axis=1)]
  transfers between devices with their start and end apart: 9 -> 9, of which waited for: 6 -> 5; matrix products, arithmetic and copies ran while one was open for 0% -> 0% of each run, Pallas kernels for 0% -> 1%
where the time goes in v3:
time: 116 us; the launch traced here: 115 us
  blocking collectives  62.2 us (54%)
  starting transfers between devices  18.9 us (16%)
  Pallas kernels  14 us (12%)
  local copies, waits for them, and re-layouts  10.3 us (9%)
  waiting for transfers between devices  7.61 us (7%)
  other arithmetic  1.71 us (1%)
    all_to_all x4, blocking collectives, swap(): return lax.all_to_all(v, 'wide', 0, 0, axis_index_groups=groups)  62.2 us
    ppermute x9, starting transfers between devices, narrow_peers(): lax.ppermute(v, 'narrow', [(i, i ^ d) for i in range(4)])  18.9 us
    unnamed x12, local copies, waits for them, and re-layouts  9.98 us
    ppermute x9, waiting for transfers between devices, narrow_peers(): lax.ppermute(v, 'narrow', [(i, i ^ d) for i in range(4)])  7.61 us
    pallas_call x1, Pallas kernels, local_log_sum(): pl.pallas_call(stats_kernel, in_specs=[HBM], out_specs=VMEM, out_shape=ja...  4.26 us
    pallas_call x1, Pallas kernels, partial_predicted(): pl.pallas_call(functools.partial(forward_kernel, 256), in_specs=[VMEM] *...  3.65 us
    pallas_call x1, Pallas kernels, backward(): pl.pallas_call(functools.partial(backward_kernel, 512), in_specs=[VMEM] *...  2.67 us
    pallas_call x1, Pallas kernels, gradient(): pl.pallas_call(functools.partial(gradient_kernel, scale, size), in_specs=...  2.38 us
  transfers between devices with their start and end apart: 9, of which 5 were waited for; matrix products, arithmetic and copies ran while one was open for 0% of the time, Pallas kernels for 1%

profile of v3, /device:TPU:1, one launch (start us, length us, event | category | flops | bytes accessed | tf_op | source)
XLA Modules:
  0.0 115.4 jit_solution(8790878529290586482)
XLA Ops:
  0.6 0.0 copy-start.3
  0.6 4.3 %stats.1 = f32[8,256]{1,0:T(8,128)} custom-call(bf16[2048,1024]{1,0:T(8,128)(2,1)} %x_ref.1), custom_call_target="tpu_custom_call" | custom-call | flops 12582912 | bytes 4194304 | tf_op jit(solution)/shard_map/stats/pallas_call | solution.py:164
  4.9 0.0 copy-start.4
  4.9 3.3 %collective-permute-start.2 = (f32[8,256]{1,0:T(8,128)}, f32[8,256]{1,0:T(8,128)S(1)}, u32[]{:S(2)}, u32[]{:S(2)}) collective-permute-start(f32[8,256]{1,0:T(8,128)} %stats.1), channel_id=1, source_target_pairs={{0,1},{1,0},{2,3},{3,2},{4,5},{5,4},{6,7},{7,6},{8,9},{9,8},{10,11... | collective-permute-start | bytes 24584 | tf_op jit(solution)/shard_map/ppermute | solution.py:30
  8.3 1.0 collective-permute-start.1
  9.3 2.2 %collective-permute-start = (f32[8,256]{1,0:T(8,128)}, f32[8,256]{1,0:T(8,128)S(1)}, u32[]{:S(2)}, u32[]{:S(2)}) collective-permute-start(f32[8,256]{1,0:T(8,128)} %stats.1), channel_id=1, source_target_pairs={{0,3},{1,2},{2,1},{3,0},{4,7},{5,6},{6,5},{7,4},{8,11},{9,10},{10,... | collective-permute-start | bytes 24584 | tf_op jit(solution)/shard_map/ppermute | solution.py:30
  11.5 0.0 copy-done.3
  11.5 1.0 transpose.13.et_ref
  12.5 0.0 collective-permute-done.2
  12.5 0.0 collective-permute-done.1
  12.5 1.5 %collective-permute-done = f32[8,256]{1,0:T(8,128)S(1)} collective-permute-done((f32[8,256]{1,0:T(8,128)}, f32[8,256]{1,0:T(8,128)S(1)}, u32[]{:S(2)}, u32[]{:S(2)}) %collective-permute-start) | collective-permute-done | bytes 8224 | tf_op jit(solution)/shard_map/ppermute | solution.py:30
  14.1 0.7 log_add_fusion.log_ref
  14.8 0.0 copy-done.4
  14.8 3.6 %forward.1 = (bf16[512,1024]{1,0:T(8,128)(2,1)S(1)}, f32[2048,1024]{1,0:T(8,128)S(1)}) custom-call(bf16[2048,1024]{1,0:T(8,128)(2,1)S(1)} %copy-done.4, bf16[512,2048]{1,0:T(8,128)(2,1)S(1)} %transpose.13.et_ref, f32[8,256]{1,0:T(8,128)S(1)} %log_add_fusion.log_ref), custom_call_target="tpu_custom_call" | custom-call | flops 2147483648 | bytes 8388608 | tf_op jit(solution)/shard_map/forward/pallas_call | solution.py:195
  18.5 0.0 copy-start
  18.5 3.2 %copy-done = f32[2048,1024]{1,0:T(8,128)} copy-done((f32[2048,1024]{1,0:T(8,128)}, f32[2048,1024]{1,0:T(8,128)S(1)}, u32[]{:S(2)}) %copy-start) | copy-done | bytes 8388632
  21.7 0.0 copy-start.5
  21.7 0.1 copy.7
  21.8 18.9 %all_to_all.20 = bf16[8,64,1024]{2,1,0:T(8,128)(2,1)S(1)} all-to-all(bf16[8,64,1024]{2,1,0:T(8,128)(2,1)S(1)} %bitcast.26), channel_id=1, replica_groups={{0,4,64,68,128,132,192,196},{8,12,72,76,136,140,200,204},{16,20,80,84,1..., dimensions={0} | all-to-all | bytes 2097152 | tf_op jit(solution)/shard_map/all_to_all | solution.py:26
  40.6 0.2 reduce_sum.48
  40.8 16.0 %all_to_all.21 = bf16[8,8,1024]{2,1,0:T(8,128)(2,1)S(1)} all-to-all(bf16[8,8,1024]{2,1,0:T(8,128)(2,1)S(1)} %bitcast.28), channel_id=1, replica_groups={{0,8,16,24,32,40,48,56},{4,12,20,28,36,44,52,60},{64,72,80,88,96,104,11..., dimensions={0} | all-to-all | bytes 262144 | tf_op jit(solution)/shard_map/all_to_all | solution.py:26
  56.8 0.0 copy-done.5
  56.9 0.2 multiply_reduce_fusion.2
  57.0 3.2 %collective-permute-start.5 = (f32[3,8]{1,0:T(4,128)S(1)}, f32[3,8]{1,0:T(4,128)S(1)}, u32[]{:S(2)}, u32[]{:S(2)}) collective-permute-start(f32[3,8]{1,0:T(4,128)S(1)} %pad_maximum_fusion), channel_id=1, source_target_pairs={{0,1},{1,0},{2,3},{3,2},{4,5},{5,4},{6,7},{7,6},{8,9},{9,8},{10,11... | collective-permute-start | bytes 296 | tf_op jit(solution)/shard_map/ppermute | solution.py:30
  60.2 1.7 %collective-permute-start.4 = (f32[3,8]{1,0:T(4,128)S(1)}, f32[3,8]{1,0:T(4,128)S(1)}, u32[]{:S(2)}, u32[]{:S(2)}) collective-permute-start(f32[3,8]{1,0:T(4,128)S(1)} %pad_maximum_fusion), channel_id=1, source_target_pairs={{0,2},{1,3},{2,0},{3,1},{4,6},{5,7},{6,4},{7,5},{8,10},{9,11},{10,... | collective-permute-start | bytes 296 | tf_op jit(solution)/shard_map/ppermute | solution.py:30
  62.0 1.5 %collective-permute-start.3 = (f32[3,8]{1,0:T(4,128)S(1)}, f32[3,8]{1,0:T(4,128)S(1)}, u32[]{:S(2)}, u32[]{:S(2)}) collective-permute-start(f32[3,8]{1,0:T(4,128)S(1)} %pad_maximum_fusion), channel_id=1, source_target_pairs={{0,3},{1,2},{2,1},{3,0},{4,7},{5,6},{6,5},{7,4},{8,11},{9,10},{10,... | collective-permute-start | bytes 296 | tf_op jit(solution)/shard_map/ppermute | solution.py:30
  63.5 0.0 collective-permute-done.5
  63.5 0.7 collective-permute-done.4
  64.2 2.3 %collective-permute-done.3 = f32[3,8]{1,0:T(4,128)S(1)} collective-permute-done((f32[3,8]{1,0:T(4,128)S(1)}, f32[3,8]{1,0:T(4,128)S(1)}, u32[]{:S(2)}, u32[]{:S(2)}) %collective-permute-start.3) | collective-permute-done | bytes 128 | tf_op jit(solution)/shard_map/ppermute | solution.py:30
  66.5 0.5 bitcast_divide_fusion
  67.1 0.1 add_convert_fusion
  67.1 10.8 %all_to_all.22 = bf16[8,8,1024]{2,1,0:T(8,128)(2,1)S(1)} all-to-all(bf16[8,8,1024]{2,1,0:T(8,128)(2,1)S(1)} %broadcast_in_dim.6), channel_id=1, replica_groups={{0,8,16,24,32,40,48,56},{4,12,20,28,36,44,52,60},{64,72,80,88,96,104,11..., dimensions={0} | all-to-all | bytes 262144 | tf_op jit(solution)/shard_map/all_to_all | solution.py:26
  78.0 0.1 broadcast_in_dim.8
  78.1 16.6 %all_to_all.23 = bf16[8,64,1024]{2,1,0:T(8,128)(2,1)S(1)} all-to-all(bf16[8,64,1024]{2,1,0:T(8,128)(2,1)S(1)} %broadcast_in_dim.8), channel_id=1, replica_groups={{0,4,64,68,128,132,192,196},{8,12,72,76,136,140,200,204},{16,20,80,84,1..., dimensions={0} | all-to-all | bytes 2097152 | tf_op jit(solution)/shard_map/all_to_all | solution.py:26
  94.6 0.1 copy.8
  94.7 0.0 copy-start.1
  94.7 3.4 %copy-done.1 = f32[2048,1024]{1,0:T(8,128)S(1)} copy-done((f32[2048,1024]{1,0:T(8,128)S(1)}, f32[2048,1024]{1,0:T(8,128)}, u32[]{:S(2)}) %copy-start.1) | copy-done | bytes 8388632
  98.1 2.7 %backward.1 = (f32[2048,1024]{1,0:T(8,128)S(1)}, f32[8,256]{1,0:T(8,128)S(1)}) custom-call(f32[2048,1024]{1,0:T(8,128)S(1)} %copy-done.1, bf16[2048,512]{1,0:T(8,128)(2,1)S(1)} %copy-done.3, bf16[512,1024]{1,0:T(8,128)(2,1)S(1)} %bitcast.24), custom_call_target="tpu_custom_call" | custom-call | flops 2147483648 | bytes 8388608 | tf_op jit(solution)/shard_map/backward/pallas_call | solution.py:216
  100.8 2.6 %collective-permute-start.8 = (f32[8,256]{1,0:T(8,128)S(1)}, f32[8,256]{1,0:T(8,128)S(1)}, u32[]{:S(2)}, u32[]{:S(2)}) collective-permute-start(f32[8,256]{1,0:T(8,128)S(1)} %get-tuple-element.9), channel_id=1, source_target_pairs={{0,1},{1,0},{2,3},{3,2},{4,5},{5,4},{6,7},{7,6},{8,9},{9,8},{10,11... | collective-permute-start | bytes 24584 | tf_op jit(solution)/shard_map/ppermute | solution.py:30
  103.4 1.7 %collective-permute-start.7 = (f32[8,256]{1,0:T(8,128)S(1)}, f32[8,256]{1,0:T(8,128)S(1)}, u32[]{:S(2)}, u32[]{:S(2)}) collective-permute-start(f32[8,256]{1,0:T(8,128)S(1)} %get-tuple-element.9), channel_id=1, source_target_pairs={{0,2},{1,3},{2,0},{3,1},{4,6},{5,7},{6,4},{7,5},{8,10},{9,11},{10,... | collective-permute-start | bytes 24584 | tf_op jit(solution)/shard_map/ppermute | solution.py:30
  105.1 1.5 %collective-permute-start.6 = (f32[8,256]{1,0:T(8,128)S(1)}, f32[8,256]{1,0:T(8,128)S(1)}, u32[]{:S(2)}, u32[]{:S(2)}) collective-permute-start(f32[8,256]{1,0:T(8,128)S(1)} %get-tuple-element.9), channel_id=1, source_target_pairs={{0,3},{1,2},{2,1},{3,0},{4,7},{5,6},{6,5},{7,4},{8,11},{9,10},{10,... | collective-permute-start | bytes 24584 | tf_op jit(solution)/shard_map/ppermute | solution.py:30
  106.6 0.0 collective-permute-done.8
  106.6 0.8 collective-permute-done.7
  107.4 2.2 %collective-permute-done.6 = f32[8,256]{1,0:T(8,128)S(1)} collective-permute-done((f32[8,256]{1,0:T(8,128)S(1)}, f32[8,256]{1,0:T(8,128)S(1)}, u32[]{:S(2)}, u32[]{:S(2)}) %collective-permute-start.6) | collective-permute-done | bytes 8224 | tf_op jit(solution)/shard_map/ppermute | solution.py:30
  109.6 0.0 copy-start.2
  109.6 3.4 %copy-done.2 = f32[2048,1024]{1,0:T(8,128)S(1)} copy-done((f32[2048,1024]{1,0:T(8,128)S(1)}, f32[2048,1024]{1,0:T(8,128)}, u32[]{:S(2)}) %copy-start.2) | copy-done | bytes 8388632
  113.0 2.4 %gradient.1 = bf16[2048,1024]{1,0:T(8,128)(2,1)} custom-call(f32[2048,1024]{1,0:T(8,128)S(1)} %copy-done.2, f32[2048,1024]{1,0:T(8,128)S(1)} %get-tuple-element.8.dprobs_ref, f32[8,256]{1,0:T(8,128)S(1)} %add_add_fusion.dot_ref), custom_call_target="tpu_custom_call" | custom-call | flops 6291456 | bytes 8388608 | tf_op jit(solution)/shard_map/gradient/pallas_call | solution.py:233
  (5 shorter events, 0.1 us)
Async XLA Ops:
  0.6 10.9 %copy-start.3 = (bf16[2048,512]{1,0:T(8,128)(2,1)S(1)}, bf16[2048,512]{1,0:T(8,128)(2,1)}, u32[]{:S(2)}) copy-start(bf16[2048,512]{1,0:T(8,128)(2,1)} %e_ref.3) | copy-start | bytes 6291460
  4.9 9.9 %copy-start.4 = (bf16[2048,1024]{1,0:T(8,128)(2,1)S(1)}, bf16[2048,1024]{1,0:T(8,128)(2,1)}, u32[]{:S(2)}) copy-start(bf16[2048,1024]{1,0:T(8,128)(2,1)} %x_ref.1) | copy-start | bytes 12582916
  4.9 7.6 %collective-permute-start.2 = (f32[8,256]{1,0:T(8,128)}, f32[8,256]{1,0:T(8,128)S(1)}, u32[]{:S(2)}, u32[]{:S(2)}) collective-permute-start(f32[8,256]{1,0:T(8,128)} %stats.1), channel_id=1, source_target_pairs={{0,1},{1,0},{2,3},{3,2},{4,5},{5,4},{6,7},{7,6},{8,9},{9,8},{10,11... | collective-permute-start | bytes 24584 | tf_op jit(solution)/shard_map/ppermute | solution.py:30
  8.3 4.3 %collective-permute-start.1 = (f32[8,256]{1,0:T(8,128)}, f32[8,256]{1,0:T(8,128)S(1)}, u32[]{:S(2)}, u32[]{:S(2)}) collective-permute-start(f32[8,256]{1,0:T(8,128)} %stats.1), channel_id=1, source_target_pairs={{0,2},{1,3},{2,0},{3,1},{4,6},{5,7},{6,4},{7,5},{8,10},{9,11},{10,... | collective-permute-start | bytes 24584 | tf_op jit(solution)/shard_map/ppermute | solution.py:30
  9.3 4.8 %collective-permute-start = (f32[8,256]{1,0:T(8,128)}, f32[8,256]{1,0:T(8,128)S(1)}, u32[]{:S(2)}, u32[]{:S(2)}) collective-permute-start(f32[8,256]{1,0:T(8,128)} %stats.1), channel_id=1, source_target_pairs={{0,3},{1,2},{2,1},{3,0},{4,7},{5,6},{6,5},{7,4},{8,11},{9,10},{10,... | collective-permute-start | bytes 24584 | tf_op jit(solution)/shard_map/ppermute | solution.py:30
  18.5 3.2 %copy-start = (f32[2048,1024]{1,0:T(8,128)}, f32[2048,1024]{1,0:T(8,128)S(1)}, u32[]{:S(2)}) copy-start(f32[2048,1024]{1,0:T(8,128)S(1)} %get-tuple-element.6.probs_ref) | copy-start | bytes 25165828
  21.7 35.2 %copy-start.5 = (f32[8,1024]{1,0:T(8,128)S(1)}, f32[8,1024]{1,0:T(8,128)}, u32[]{:S(2)}) copy-start(f32[8,1024]{1,0:T(8,128)} %param.5) | copy-start | bytes 98308
  57.0 6.5 %collective-permute-start.5 = (f32[3,8]{1,0:T(4,128)S(1)}, f32[3,8]{1,0:T(4,128)S(1)}, u32[]{:S(2)}, u32[]{:S(2)}) collective-permute-start(f32[3,8]{1,0:T(4,128)S(1)} %pad_maximum_fusion), channel_id=1, source_target_pairs={{0,1},{1,0},{2,3},{3,2},{4,5},{5,4},{6,7},{7,6},{8,9},{9,8},{10,11... | collective-permute-start | bytes 296 | tf_op jit(solution)/shard_map/ppermute | solution.py:30
  60.2 4.0 %collective-permute-start.4 = (f32[3,8]{1,0:T(4,128)S(1)}, f32[3,8]{1,0:T(4,128)S(1)}, u32[]{:S(2)}, u32[]{:S(2)}) collective-permute-start(f32[3,8]{1,0:T(4,128)S(1)} %pad_maximum_fusion), channel_id=1, source_target_pairs={{0,2},{1,3},{2,0},{3,1},{4,6},{5,7},{6,4},{7,5},{8,10},{9,11},{10,... | collective-permute-start | bytes 296 | tf_op jit(solution)/shard_map/ppermute | solution.py:30
  62.0 4.5 %collective-permute-start.3 = (f32[3,8]{1,0:T(4,128)S(1)}, f32[3,8]{1,0:T(4,128)S(1)}, u32[]{:S(2)}, u32[]{:S(2)}) collective-permute-start(f32[3,8]{1,0:T(4,128)S(1)} %pad_maximum_fusion), channel_id=1, source_target_pairs={{0,3},{1,2},{2,1},{3,0},{4,7},{5,6},{6,5},{7,4},{8,11},{9,10},{10,... | collective-permute-start | bytes 296 | tf_op jit(solution)/shard_map/ppermute | solution.py:30
  94.7 3.4 %copy-start.1 = (f32[2048,1024]{1,0:T(8,128)S(1)}, f32[2048,1024]{1,0:T(8,128)}, u32[]{:S(2)}) copy-start(f32[2048,1024]{1,0:T(8,128)} %copy-done) | copy-start | bytes 25165828
  100.8 5.8 %collective-permute-start.8 = (f32[8,256]{1,0:T(8,128)S(1)}, f32[8,256]{1,0:T(8,128)S(1)}, u32[]{:S(2)}, u32[]{:S(2)}) collective-permute-start(f32[8,256]{1,0:T(8,128)S(1)} %get-tuple-element.9), channel_id=1, source_target_pairs={{0,1},{1,0},{2,3},{3,2},{4,5},{5,4},{6,7},{7,6},{8,9},{9,8},{10,11... | collective-permute-start | bytes 24584 | tf_op jit(solution)/shard_map/ppermute | solution.py:30
  103.4 4.0 %collective-permute-start.7 = (f32[8,256]{1,0:T(8,128)S(1)}, f32[8,256]{1,0:T(8,128)S(1)}, u32[]{:S(2)}, u32[]{:S(2)}) collective-permute-start(f32[8,256]{1,0:T(8,128)S(1)} %get-tuple-element.9), channel_id=1, source_target_pairs={{0,2},{1,3},{2,0},{3,1},{4,6},{5,7},{6,4},{7,5},{8,10},{9,11},{10,... | collective-permute-start | bytes 24584 | tf_op jit(solution)/shard_map/ppermute | solution.py:30
  105.1 4.6 %collective-permute-start.6 = (f32[8,256]{1,0:T(8,128)S(1)}, f32[8,256]{1,0:T(8,128)S(1)}, u32[]{:S(2)}, u32[]{:S(2)}) collective-permute-start(f32[8,256]{1,0:T(8,128)S(1)} %get-tuple-element.9), channel_id=1, source_target_pairs={{0,3},{1,2},{2,1},{3,0},{4,7},{5,6},{6,5},{7,4},{8,11},{9,10},{10,... | collective-permute-start | bytes 24584 | tf_op jit(solution)/shard_map/ppermute | solution.py:30
  109.6 3.4 %copy-start.2 = (f32[2048,1024]{1,0:T(8,128)S(1)}, f32[2048,1024]{1,0:T(8,128)}, u32[]{:S(2)}) copy-start(f32[2048,1024]{1,0:T(8,128)} %copy-done) | copy-start | bytes 25165828

commit v4 on v3

--- a/solution.py
+++ b/solution.py
@@ -10,7 +10,7 @@
 Y, Z, X, R = 4, 8, 2, 8
 LANES = 128
 ROWS = 256
-STATS_MIB = 58
+STATS_MIB = 60
 MIB = 1 << 20
 
 
@@ -26,8 +26,15 @@
     return lax.all_to_all(v, "wide", 0, 0, axis_index_groups=groups)
 
 
-def narrow_peers(v):
-    return [lax.ppermute(v, "narrow", [(i, i ^ d) for i in range(4)]) for d in (3, 2, 1)]
+def narrow_combine(v, op):
+    for d in (1, 2):
+        v = op(v, lax.ppermute(v, "narrow", [(i, i ^ d) for i in range(4)]))
+    return v
+
+
+def log_add(a, b):
+    top = jnp.maximum(a, b)
+    return top + jnp.log(jnp.exp(a - top) + jnp.exp(b - top))
 
 
 def fold(parts, op):
@@ -82,7 +89,7 @@
         out_ref[:, block(i)] = e_ref[block(i), :].T
 
 
-def forward_kernel(tile, x_ref, et_ref, log_ref, part_ref, probs_ref, low, column):
+def forward_kernel(tile, x_ref, et_ref, log_ref, part_ref, low, column):
     cells, spots = x_ref.shape
 
     @pl.loop(0, cells // ROWS)
@@ -95,7 +102,6 @@
         for k in range(cols.start, cols.stop, LANES):
             g = slice(k, k + LANES)
             probs = jnp.exp(x_ref[:, g].astype(jnp.float32) - column[...])
-            probs_ref[:, g] = probs
             low[:, g] = probs.astype(jnp.bfloat16)
 
     fill(tiles[0])
@@ -106,8 +112,15 @@
             fill(later)
 
 
-def backward_kernel(size, probs_ref, e_ref, d_ref, dprobs_ref, dot_ref):
+def backward_kernel(size, x_ref, e_ref, d_ref, log_ref, probs_ref, dprobs_ref, dot_ref):
     cells, spots = probs_ref.shape
+
+    def fill(first):
+        for k in range(first, first + size, ROWS):
+            rows = slice(k, k + ROWS)
+            log_total = as_column(log_ref[k // ROWS : k // ROWS + 1, :])
+            for g in lane_groups(spots):
+                probs_ref[rows, g] = jnp.exp(x_ref[rows, g].astype(jnp.float32) - log_total)
 
     def row_dots(first):
         for k in range(first, first + size, ROWS):
@@ -118,6 +131,7 @@
     for first in range(0, cells, size):
         rows = slice(first, first + size)
         dprobs_ref[rows, :] = jnp.dot(e_ref[rows, :], d_ref[...], preferred_element_type=jnp.float32)
+        fill(first)
         if first:
             row_dots(first - size)
     row_dots(cells - size)
@@ -195,36 +209,34 @@
     return pl.pallas_call(
         functools.partial(forward_kernel, 256),
         in_specs=[VMEM] * 3,
-        out_specs=[VMEM] * 2,
-        out_shape=[
-            jax.ShapeDtypeStruct((genes, spots), jnp.bfloat16),
-            jax.ShapeDtypeStruct((cells, spots), jnp.float32),
-        ],
+        out_specs=VMEM,
+        out_shape=jax.ShapeDtypeStruct((genes, spots), jnp.bfloat16),
         scratch_shapes=[
             pltpu.VMEM((cells, spots), jnp.bfloat16),
             pltpu.VMEM((cells, LANES), jnp.float32),
         ],
-        compiler_params=params(24),
+        compiler_params=params(16),
         cost_estimate=cost(2 * cells * spots * genes, cells * spots * 4, cells * spots),
         name="forward",
     )(logits, expression_t, log_total)
 
 
-def backward(probs, expression, d_pred):
-    cells, spots = probs.shape
+def backward(logits, expression, d_pred, log_total):
+    cells, spots = logits.shape
     genes = expression.shape[1]
     return pl.pallas_call(
         functools.partial(backward_kernel, 512),
-        in_specs=[VMEM] * 3,
-        out_specs=[VMEM] * 2,
+        in_specs=[VMEM] * 4,
+        out_specs=[VMEM] * 3,
         out_shape=[
+            jax.ShapeDtypeStruct((cells, spots), jnp.float32),
             jax.ShapeDtypeStruct((cells, spots), jnp.float32),
             jax.ShapeDtypeStruct((cells // ROWS, ROWS), jnp.float32),
         ],
         compiler_params=params(12),
-        cost_estimate=cost(2 * cells * spots * genes, cells * spots * 4),
+        cost_estimate=cost(2 * cells * spots * genes, cells * spots * 4, cells * spots),
         name="backward",
-    )(probs, expression, d_pred)
+    )(logits, expression, d_pred, log_total)
 
 
 def gradient(probs, d_probs, row_dot, scale):
@@ -249,10 +261,8 @@
     spots = logits.shape[1]
     local_log = local_log_sum(logits)
     expression_t = transposed(expression)
-    logs = [local_log] + narrow_peers(local_log)
-    top = fold(logs, jnp.maximum)
-    log_total = top + jnp.log(fold([jnp.exp(v - top) for v in logs], jnp.add))
-    part, probs = partial_predicted(logits, expression_t, log_total)
+    log_total = narrow_combine(local_log, log_add)
+    part = partial_predicted(logits, expression_t, log_total)
     part = part.reshape(Y, Z, X, R, spots).transpose(0, 2, 1, 3, 4).reshape(Y * X, Z * R, spots)
     part = swap(part, YX_GROUPS).astype(jnp.float32).sum(0).astype(jnp.bfloat16)
     part = swap(part.reshape(Z, R, spots), Z_GROUPS)
@@ -264,7 +274,7 @@
             jnp.sum(measured * measured, axis=1),
         ]
     )
-    sums = sums + fold([jnp.zeros_like(sums)] + narrow_peers(sums), jnp.add)
+    sums = narrow_combine(sums, jnp.add)
     inner, pred_sq, meas_sq = sums[0], sums[1], sums[2]
     norm_p = jnp.sqrt(pred_sq + 1e-06)
     norm_m = jnp.sqrt(meas_sq + 1e-06)
@@ -276,8 +286,8 @@
     share = swap(jnp.broadcast_to(share[None], (Z, R, spots)), Z_GROUPS).reshape(Z * R, spots)
     share = swap(jnp.broadcast_to(share[None], (Y * X, Z * R, spots)), YX_GROUPS)
     d_pred = share.reshape(Y, X, Z, R, spots).transpose(0, 2, 1, 3, 4).reshape(Y * X * Z * R, spots)
-    d_probs, row_dot = backward(probs, expression, d_pred)
-    row_dot = fold([row_dot] + narrow_peers(row_dot), jnp.add)
+    probs, d_probs, row_dot = backward(logits, expression, d_pred, log_total)
+    row_dot = narrow_combine(row_dot, jnp.add)
     grad = gradient(probs, d_probs, row_dot, float(spots * lax.axis_size("narrow")))
     return (grad, similarity)
 

time: 116 us -> 102 us (0.88)
  local copies, waits for them, and re-layouts: 10.3 us -> 0.29 us
  blocking collectives: 62.2 us -> 59.1 us
  starting transfers between devices: 18.9 us -> 17.3 us
    unnamed x12 -> x8, local copies, waits for them, and re-layouts: 9.98 us -> 0.02 us
    all_to_all x4, blocking collectives: 62.2 us -> 59.1 us  [swap(): return lax.all_to_all(v, 'wide', 0, 0, axis_index_groups=groups)]
    ppermute x9 -> x6, starting transfers between devices: 18.9 us -> 17.3 us  [narrow_combine(): v = op(v, lax.ppermute(v, 'narrow', [(i, i ^ d) for i in range(4)]))]
    ppermute x9 -> x6, waiting for transfers between devices: 7.61 us -> 7.72 us  [narrow_combine(): v = op(v, lax.ppermute(v, 'narrow', [(i, i ^ d) for i in range(4)]))]
  transfers between devices with their start and end apart: 9 -> 6, of which waited for: 5 -> 6; matrix products, arithmetic and copies ran while one was open for 0% -> 0% of each run, Pallas kernels for 1% -> 1%
where the time goes in v4:
time: 102 us
  blocking collectives  59.1 us (58%)
  starting transfers between devices  17.3 us (17%)
  Pallas kernels  15 us (15%)
  waiting for transfers between devices  7.72 us (8%)
  other arithmetic  1.74 us (2%)
    all_to_all x4, blocking collectives, swap(): return lax.all_to_all(v, 'wide', 0, 0, axis_index_groups=groups)  59.1 us
    ppermute x6, starting transfers between devices, narrow_combine(): v = op(v, lax.ppermute(v, 'narrow', [(i, i ^ d) for i in range(4)]))  17.3 us
    ppermute x6, waiting for transfers between devices, narrow_combine(): v = op(v, lax.ppermute(v, 'narrow', [(i, i ^ d) for i in range(4)]))  7.72 us
    pallas_call x1, Pallas kernels, local_log_sum(): pl.pallas_call(stats_kernel, in_specs=[HBM], out_specs=VMEM, out_shape=ja...  4.26 us
    pallas_call x1, Pallas kernels, partial_predicted(): pl.pallas_call(functools.partial(forward_kernel, 256), in_specs=[VMEM] *...  3.6 us
    pallas_call x1, Pallas kernels, backward(): pl.pallas_call(functools.partial(backward_kernel, 512), in_specs=[VMEM] *...  3.48 us
    pallas_call x1, Pallas kernels, gradient(): pl.pallas_call(functools.partial(gradient_kernel, scale, size), in_specs=...  2.65 us
  transfers between devices with their start and end apart: 6, of which 6 were waited for; matrix products, arithmetic and copies ran while one was open for 0% of the time, Pallas kernels for 1%

profile of v4, /device:TPU:1, one launch (start us, length us, event | category | flops | bytes accessed | tf_op | source)
XLA Modules:
  0.0 101.9 jit_solution(978367710811340664)
XLA Ops:
  0.6 0.0 copy-start.2
  0.6 4.3 %stats.1 = f32[8,256]{1,0:T(8,128)} custom-call(bf16[2048,1024]{1,0:T(8,128)(2,1)} %x_ref.3), custom_call_target="tpu_custom_call" | custom-call | flops 12582912 | bytes 4194304 | tf_op jit(solution)/shard_map/stats/pallas_call | solution.py:178
  4.9 0.0 copy-start
  4.9 3.3 %collective-permute-start = (f32[8,256]{1,0:T(8,128)}, f32[8,256]{1,0:T(8,128)S(1)}, u32[]{:S(2)}, u32[]{:S(2)}) collective-permute-start(f32[8,256]{1,0:T(8,128)} %stats.1), channel_id=1, source_target_pairs={{0,1},{1,0},{2,3},{3,2},{4,5},{5,4},{6,7},{7,6},{8,9},{9,8},{10,11... | collective-permute-start | bytes 24584 | tf_op jit(solution)/shard_map/ppermute | solution.py:31
  8.3 1.0 %collective-permute-done = f32[8,256]{1,0:T(8,128)S(1)} collective-permute-done((f32[8,256]{1,0:T(8,128)}, f32[8,256]{1,0:T(8,128)S(1)}, u32[]{:S(2)}, u32[]{:S(2)}) %collective-permute-start) | collective-permute-done | bytes 8224 | tf_op jit(solution)/shard_map/ppermute | solution.py:31
  9.3 0.7 log_add_fusion.1
  10.0 1.1 %collective-permute-start.1 = (f32[8,256]{1,0:T(8,128)S(1)}, f32[8,256]{1,0:T(8,128)S(1)}, u32[]{:S(2)}, u32[]{:S(2)}) collective-permute-start(f32[8,256]{1,0:T(8,128)S(1)} %log_add_fusion.1), channel_id=1, source_target_pairs={{0,2},{1,3},{2,0},{3,1},{4,6},{5,7},{6,4},{7,5},{8,10},{9,11},{10,... | collective-permute-start | bytes 24584 | tf_op jit(solution)/shard_map/ppermute | solution.py:31
  11.1 0.0 copy-done.2
  11.1 1.0 transpose.13.et_ref
  12.1 2.0 %collective-permute-done.1 = f32[8,256]{1,0:T(8,128)S(1)} collective-permute-done((f32[8,256]{1,0:T(8,128)S(1)}, f32[8,256]{1,0:T(8,128)S(1)}, u32[]{:S(2)}, u32[]{:S(2)}) %collective-permute-start.1) | collective-permute-done | bytes 8224 | tf_op jit(solution)/shard_map/ppermute | solution.py:31
  14.1 0.0 copy-done
  14.1 3.6 %forward.1 = bf16[512,1024]{1,0:T(8,128)(2,1)S(1)} custom-call(bf16[2048,1024]{1,0:T(8,128)(2,1)S(1)} %copy-done, bf16[512,2048]{1,0:T(8,128)(2,1)S(1)} %transpose.13.et_ref, f32[8,256]{1,0:T(8,128)S(1)} %log_add_fusion.log_ref), custom_call_target="tpu_custom_call" | custom-call | flops 2147483648 | bytes 8388608 | tf_op jit(solution)/shard_map/forward/pallas_call | solution.py:209
  17.7 0.0 copy-start.3
  17.7 0.1 copy.7
  17.8 17.1 %all_to_all.20 = bf16[8,64,1024]{2,1,0:T(8,128)(2,1)S(1)} all-to-all(bf16[8,64,1024]{2,1,0:T(8,128)(2,1)S(1)} %bitcast.26), channel_id=1, replica_groups={{0,4,64,68,128,132,192,196},{8,12,72,76,136,140,200,204},{16,20,80,84,1..., dimensions={0} | all-to-all | bytes 2097152 | tf_op jit(solution)/shard_map/all_to_all | solution.py:26
  35.0 0.2 reduce_sum.48
  35.1 0.0 copy-start.1
  35.2 16.2 %all_to_all.21 = bf16[8,8,1024]{2,1,0:T(8,128)(2,1)S(1)} all-to-all(bf16[8,8,1024]{2,1,0:T(8,128)(2,1)S(1)} %bitcast.28), channel_id=1, replica_groups={{0,8,16,24,32,40,48,56},{4,12,20,28,36,44,52,60},{64,72,80,88,96,104,11..., dimensions={0} | all-to-all | bytes 262144 | tf_op jit(solution)/shard_map/all_to_all | solution.py:26
  51.4 0.0 copy-done.3
  51.4 0.2 multiply_reduce_fusion.2
  51.6 4.2 %collective-permute-start.2 = (f32[3,8]{1,0:T(4,128)S(1)}, f32[3,8]{1,0:T(4,128)S(1)}, u32[]{:S(2)}, u32[]{:S(2)}) collective-permute-start(f32[3,8]{1,0:T(4,128)S(1)} %pad_maximum_fusion), channel_id=1, source_target_pairs={{0,1},{1,0},{2,3},{3,2},{4,5},{5,4},{6,7},{7,6},{8,9},{9,8},{10,11... | collective-permute-start | bytes 296 | tf_op jit(solution)/shard_map/ppermute | solution.py:31
  55.7 0.8 collective-permute-done.2
  56.6 2.5 %collective-permute-start.3 = (f32[3,8]{1,0:T(4,128)S(1)}, f32[3,8]{1,0:T(4,128)S(1)}, u32[]{:S(2)}, u32[]{:S(2)}) collective-permute-start(f32[3,8]{1,0:T(4,128)S(1)} %fusion.4), channel_id=1, source_target_pairs={{0,2},{1,3},{2,0},{3,1},{4,6},{5,7},{6,4},{7,5},{8,10},{9,11},{10,... | collective-permute-start | bytes 296 | tf_op jit(solution)/shard_map/ppermute | solution.py:31
  59.1 1.5 %collective-permute-done.3 = f32[3,8]{1,0:T(4,128)S(1)} collective-permute-done((f32[3,8]{1,0:T(4,128)S(1)}, f32[3,8]{1,0:T(4,128)S(1)}, u32[]{:S(2)}, u32[]{:S(2)}) %collective-permute-start.3) | collective-permute-done | bytes 128 | tf_op jit(solution)/shard_map/ppermute | solution.py:31
  60.6 0.5 bitcast_divide_fusion
  61.1 0.1 add_convert_fusion
  61.2 10.3 %all_to_all.22 = bf16[8,8,1024]{2,1,0:T(8,128)(2,1)S(1)} all-to-all(bf16[8,8,1024]{2,1,0:T(8,128)(2,1)S(1)} %broadcast_in_dim.6), channel_id=1, replica_groups={{0,8,16,24,32,40,48,56},{4,12,20,28,36,44,52,60},{64,72,80,88,96,104,11..., dimensions={0} | all-to-all | bytes 262144 | tf_op jit(solution)/shard_map/all_to_all | solution.py:26
  71.6 0.1 broadcast_in_dim.8
  71.7 15.4 %all_to_all.23 = bf16[8,64,1024]{2,1,0:T(8,128)(2,1)S(1)} all-to-all(bf16[8,64,1024]{2,1,0:T(8,128)(2,1)S(1)} %broadcast_in_dim.8), channel_id=1, replica_groups={{0,4,64,68,128,132,192,196},{8,12,72,76,136,140,200,204},{16,20,80,84,1..., dimensions={0} | all-to-all | bytes 2097152 | tf_op jit(solution)/shard_map/all_to_all | solution.py:26
  87.1 0.1 copy.8
  87.2 0.0 copy-done.1
  87.2 3.5 %backward.1 = (f32[2048,1024]{1,0:T(8,128)S(1)}, f32[2048,1024]{1,0:T(8,128)S(1)}, f32[8,256]{1,0:T(8,128)S(1)}) custom-call(bf16[2048,1024]{1,0:T(8,128)(2,1)S(1)} %copy-done.1, bf16[2048,512]{1,0:T(8,128)(2,1)S(1)} %copy-done.2, bf16[512,1024]{1,0:T(8,128)(2,1)S(1)} %bitcast.24, f32[8,256]{1,0:T(8,128)S(1)} %log_add_fusion.log_ref), custom_call_target="tpu_custom_call" | custom-call | flops 2147483648 | bytes 8388608 | tf_op jit(solution)/shard_map/backward/pallas_call | solution.py:227
  90.7 3.7 %collective-permute-start.4 = (f32[8,256]{1,0:T(8,128)S(1)}, f32[8,256]{1,0:T(8,128)S(1)}, u32[]{:S(2)}, u32[]{:S(2)}) collective-permute-start(f32[8,256]{1,0:T(8,128)S(1)} %get-tuple-element.7), channel_id=1, source_target_pairs={{0,1},{1,0},{2,3},{3,2},{4,5},{5,4},{6,7},{7,6},{8,9},{9,8},{10,11... | collective-permute-start | bytes 24584 | tf_op jit(solution)/shard_map/ppermute | solution.py:31
  94.4 0.8 collective-permute-done.4
  95.3 2.4 %collective-permute-start.5 = (f32[8,256]{1,0:T(8,128)S(1)}, f32[8,256]{1,0:T(8,128)S(1)}, u32[]{:S(2)}, u32[]{:S(2)}) collective-permute-start(f32[8,256]{1,0:T(8,128)S(1)} %add.58), channel_id=1, source_target_pairs={{0,2},{1,3},{2,0},{3,1},{4,6},{5,7},{6,4},{7,5},{8,10},{9,11},{10,... | collective-permute-start | bytes 24584 | tf_op jit(solution)/shard_map/ppermute | solution.py:31
  97.7 1.6 %collective-permute-done.5 = f32[8,256]{1,0:T(8,128)S(1)} collective-permute-done((f32[8,256]{1,0:T(8,128)S(1)}, f32[8,256]{1,0:T(8,128)S(1)}, u32[]{:S(2)}, u32[]{:S(2)}) %collective-permute-start.5) | collective-permute-done | bytes 8224 | tf_op jit(solution)/shard_map/ppermute | solution.py:31
  99.3 2.7 %gradient.1 = bf16[2048,1024]{1,0:T(8,128)(2,1)} custom-call(f32[2048,1024]{1,0:T(8,128)S(1)} %get-tuple-element.5.probs_ref, f32[2048,1024]{1,0:T(8,128)S(1)} %get-tuple-element.6.dprobs_ref, f32[8,256]{1,0:T(8,128)S(1)} %add.59.dot_ref), custom_call_target="tpu_custom_call" | custom-call | flops 6291456 | bytes 8388608 | tf_op jit(solution)/shard_map/gradient/pallas_call | solution.py:245
  (8 shorter events, 0.1 us)
Async XLA Ops:
  0.6 10.5 %copy-start.2 = (bf16[2048,512]{1,0:T(8,128)(2,1)S(1)}, bf16[2048,512]{1,0:T(8,128)(2,1)}, u32[]{:S(2)}) copy-start(bf16[2048,512]{1,0:T(8,128)(2,1)} %e_ref.3) | copy-start | bytes 6291460
  4.9 9.2 %copy-start = (bf16[2048,1024]{1,0:T(8,128)(2,1)S(1)}, bf16[2048,1024]{1,0:T(8,128)(2,1)}, u32[]{:S(2)}) copy-start(bf16[2048,1024]{1,0:T(8,128)(2,1)} %x_ref.3) | copy-start | bytes 12582916
  4.9 4.4 %collective-permute-start = (f32[8,256]{1,0:T(8,128)}, f32[8,256]{1,0:T(8,128)S(1)}, u32[]{:S(2)}, u32[]{:S(2)}) collective-permute-start(f32[8,256]{1,0:T(8,128)} %stats.1), channel_id=1, source_target_pairs={{0,1},{1,0},{2,3},{3,2},{4,5},{5,4},{6,7},{7,6},{8,9},{9,8},{10,11... | collective-permute-start | bytes 24584 | tf_op jit(solution)/shard_map/ppermute | solution.py:31
  10.0 4.1 %collective-permute-start.1 = (f32[8,256]{1,0:T(8,128)S(1)}, f32[8,256]{1,0:T(8,128)S(1)}, u32[]{:S(2)}, u32[]{:S(2)}) collective-permute-start(f32[8,256]{1,0:T(8,128)S(1)} %log_add_fusion.1), channel_id=1, source_target_pairs={{0,2},{1,3},{2,0},{3,1},{4,6},{5,7},{6,4},{7,5},{8,10},{9,11},{10,... | collective-permute-start | bytes 24584 | tf_op jit(solution)/shard_map/ppermute | solution.py:31
  17.7 33.7 %copy-start.3 = (f32[8,1024]{1,0:T(8,128)S(1)}, f32[8,1024]{1,0:T(8,128)}, u32[]{:S(2)}) copy-start(f32[8,1024]{1,0:T(8,128)} %param.5) | copy-start | bytes 98308
  35.1 52.1 %copy-start.1 = (bf16[2048,1024]{1,0:T(8,128)(2,1)S(1)}, bf16[2048,1024]{1,0:T(8,128)(2,1)}, u32[]{:S(2)}) copy-start(bf16[2048,1024]{1,0:T(8,128)(2,1)} %x_ref.3) | copy-start | bytes 12582916
  51.6 5.0 %collective-permute-start.2 = (f32[3,8]{1,0:T(4,128)S(1)}, f32[3,8]{1,0:T(4,128)S(1)}, u32[]{:S(2)}, u32[]{:S(2)}) collective-permute-start(f32[3,8]{1,0:T(4,128)S(1)} %pad_maximum_fusion), channel_id=1, source_target_pairs={{0,1},{1,0},{2,3},{3,2},{4,5},{5,4},{6,7},{7,6},{8,9},{9,8},{10,11... | collective-permute-start | bytes 296 | tf_op jit(solution)/shard_map/ppermute | solution.py:31
  56.6 4.0 %collective-permute-start.3 = (f32[3,8]{1,0:T(4,128)S(1)}, f32[3,8]{1,0:T(4,128)S(1)}, u32[]{:S(2)}, u32[]{:S(2)}) collective-permute-start(f32[3,8]{1,0:T(4,128)S(1)} %fusion.4), channel_id=1, source_target_pairs={{0,2},{1,3},{2,0},{3,1},{4,6},{5,7},{6,4},{7,5},{8,10},{9,11},{10,... | collective-permute-start | bytes 296 | tf_op jit(solution)/shard_map/ppermute | solution.py:31
  90.7 4.6 %collective-permute-start.4 = (f32[8,256]{1,0:T(8,128)S(1)}, f32[8,256]{1,0:T(8,128)S(1)}, u32[]{:S(2)}, u32[]{:S(2)}) collective-permute-start(f32[8,256]{1,0:T(8,128)S(1)} %get-tuple-element.7), channel_id=1, source_target_pairs={{0,1},{1,0},{2,3},{3,2},{4,5},{5,4},{6,7},{7,6},{8,9},{9,8},{10,11... | collective-permute-start | bytes 24584 | tf_op jit(solution)/shard_map/ppermute | solution.py:31
  95.3 4.0 %collective-permute-start.5 = (f32[8,256]{1,0:T(8,128)S(1)}, f32[8,256]{1,0:T(8,128)S(1)}, u32[]{:S(2)}, u32[]{:S(2)}) collective-permute-start(f32[8,256]{1,0:T(8,128)S(1)} %add.58), channel_id=1, source_target_pairs={{0,2},{1,3},{2,0},{3,1},{4,6},{5,7},{6,4},{7,5},{8,10},{9,11},{10,... | collective-permute-start | bytes 24584 | tf_op jit(solution)/shard_map/ppermute | solution.py:31

commit v5 on v4

--- a/solution.py
+++ b/solution.py
@@ -7,10 +7,9 @@
 from jax.experimental.pallas import tpu as pltpu
 from jax.sharding import PartitionSpec as P
 
-Y, Z, X, R = 4, 8, 2, 8
+Y, Z, X, R, N = 4, 8, 2, 8, 4
 LANES = 128
 ROWS = 256
-STATS_MIB = 60
 MIB = 1 << 20
 
 
@@ -18,12 +17,28 @@
     return (y * Z + z) * X + x
 
 
-YX_GROUPS = [[wide_index(y, z, x) for y in range(Y) for x in range(X)] for z in range(Z)]
-Z_GROUPS = [[wide_index(y, z, x) for z in range(Z)] for y in range(Y) for x in range(X)]
+def device_index(y, z, x, n):
+    return wide_index(y, z, x) * N + n
+
+
+def yx_groups(n):
+    return [[device_index(y, z, x, n) for y in range(Y) for x in range(X)] for z in range(Z)]
+
+
+def z_groups(n):
+    return [[device_index(y, z, x, n) for z in range(Z)] for y in range(Y) for x in range(X)]
+
+
+WIDE_STAGE = [g for n in range(N) for g in (z_groups(n) if n % 2 else yx_groups(n))]
+SHORT_STAGE = [g for n in range(N) for g in (yx_groups(n) if n % 2 else z_groups(n))]
 
 
 def swap(v, groups):
-    return lax.all_to_all(v, "wide", 0, 0, axis_index_groups=groups)
+    return lax.all_to_all(v, ("wide", "narrow"), 0, 0, axis_index_groups=groups)
+
+
+def by_core(even, odd):
+    return jnp.where(lax.axis_index("narrow") % 2 == 0, even, odd)
 
 
 def narrow_combine(v, op):
@@ -184,7 +199,7 @@
             pltpu.VMEM((cells, spots), logits.dtype),
             pltpu.SemaphoreType.DMA((steps,)),
         ],
-        compiler_params=params(STATS_MIB),
+        compiler_params=params(8),
         cost_estimate=cost(cells * spots * 6, cells * spots * 2, cells * spots),
         name="stats",
     )(logits)
@@ -259,13 +274,17 @@
 
 def body(logits, expression, measured):
     spots = logits.shape[1]
-    local_log = local_log_sum(logits)
+    local_log = local_log_sum(pltpu.with_memory_space_constraint(logits, pltpu.HBM))
     expression_t = transposed(expression)
     log_total = narrow_combine(local_log, log_add)
     part = partial_predicted(logits, expression_t, log_total)
-    part = part.reshape(Y, Z, X, R, spots).transpose(0, 2, 1, 3, 4).reshape(Y * X, Z * R, spots)
-    part = swap(part, YX_GROUPS).astype(jnp.float32).sum(0).astype(jnp.bfloat16)
-    part = swap(part.reshape(Z, R, spots), Z_GROUPS)
+    part = part.reshape(Y, Z, X, R, spots)
+    part = by_core(
+        part.transpose(0, 2, 1, 3, 4).reshape(8, Z * R, spots),
+        part.transpose(1, 0, 2, 3, 4).reshape(8, Y * X * R, spots),
+    )
+    part = swap(part, WIDE_STAGE).astype(jnp.float32).sum(0).astype(jnp.bfloat16)
+    part = swap(part.reshape(8, R, spots), SHORT_STAGE)
     predicted = part.astype(jnp.float32).sum(0)
     sums = jnp.stack(
         [
@@ -276,16 +295,18 @@
     )
     sums = narrow_combine(sums, jnp.add)
     inner, pred_sq, meas_sq = sums[0], sums[1], sums[2]
-    norm_p = jnp.sqrt(pred_sq + 1e-06)
-    norm_m = jnp.sqrt(meas_sq + 1e-06)
-    similarity = inner / (norm_p * norm_m)
+    inv_p = lax.rsqrt(pred_sq + 1e-06)
+    inv_m = lax.rsqrt(meas_sq + 1e-06)
+    similarity = inner * (inv_p * inv_m)
     share = (
-        -measured / (norm_p * norm_m)[:, None]
-        + (inner / (norm_p**3 * norm_m))[:, None] * predicted
+        (similarity * inv_p * inv_p)[:, None] * predicted - (inv_p * inv_m)[:, None] * measured
     ).astype(jnp.bfloat16)
-    share = swap(jnp.broadcast_to(share[None], (Z, R, spots)), Z_GROUPS).reshape(Z * R, spots)
-    share = swap(jnp.broadcast_to(share[None], (Y * X, Z * R, spots)), YX_GROUPS)
-    d_pred = share.reshape(Y, X, Z, R, spots).transpose(0, 2, 1, 3, 4).reshape(Y * X * Z * R, spots)
+    share = swap(jnp.broadcast_to(share[None], (8, R, spots)), SHORT_STAGE).reshape(8 * R, spots)
+    share = swap(jnp.broadcast_to(share[None], (8, 8 * R, spots)), WIDE_STAGE)
+    d_pred = by_core(
+        share.reshape(Y, X, Z, R, spots).transpose(0, 2, 1, 3, 4),
+        share.reshape(Z, Y, X, R, spots).transpose(1, 0, 2, 3, 4),
+    ).reshape(Y * Z * X * R, spots)
     probs, d_probs, row_dot = backward(logits, expression, d_pred, log_total)
     row_dot = narrow_combine(row_dot, jnp.add)
     grad = gradient(probs, d_probs, row_dot, float(spots * lax.axis_size("narrow")))

time: 102 us -> 97.8 us (0.959)
  starting transfers between devices: 17.3 us -> 9.6 us
  blocking collectives: 59.1 us -> 62.8 us
    ppermute x6, starting transfers between devices: 17.3 us -> 9.6 us  [narrow_combine(): v = op(v, lax.ppermute(v, 'narrow', [(i, i ^ d) for i in range(4)]))]
    all_to_all x4, blocking collectives: 59.1 us -> 62.8 us  [swap(): return lax.all_to_all(v, ('wide', 'narrow'), 0, 0, axis_index_groups=groups)]
where the time goes in v5:
time: 97.8 us; the launch traced here: 97.5 us
  blocking collectives  62.8 us (64%)
  Pallas kernels  14.4 us (15%)
  starting transfers between devices  9.6 us (10%)
  waiting for transfers between devices  8.15 us (8%)
  other arithmetic  1.32 us (1%)
    all_to_all x4, blocking collectives, swap(): return lax.all_to_all(v, ('wide', 'narrow'), 0, 0, axis_index_groups=groups)  62.8 us
    ppermute x6, starting transfers between devices, narrow_combine(): v = op(v, lax.ppermute(v, 'narrow', [(i, i ^ d) for i in range(4)]))  9.6 us
    ppermute x6, waiting for transfers between devices, narrow_combine(): v = op(v, lax.ppermute(v, 'narrow', [(i, i ^ d) for i in range(4)]))  8.15 us
    pallas_call x1, Pallas kernels, local_log_sum(): pl.pallas_call(stats_kernel, in_specs=[HBM], out_specs=VMEM, out_shape=ja...  3.67 us
    pallas_call x1, Pallas kernels, partial_predicted(): pl.pallas_call(functools.partial(forward_kernel, 256), in_specs=[VMEM] *...  3.6 us
    pallas_call x1, Pallas kernels, backward(): pl.pallas_call(functools.partial(backward_kernel, 512), in_specs=[VMEM] *...  3.47 us
    pallas_call x1, Pallas kernels, gradient(): pl.pallas_call(functools.partial(gradient_kernel, scale, size), in_specs=...  2.65 us
  transfers between devices with their start and end apart: 6, of which 6 were waited for; matrix products, arithmetic and copies ran while one was open for 0% of the time, Pallas kernels for 1%

profile of v5, /device:TPU:1, one launch (start us, length us, event | category | flops | bytes accessed | tf_op | source)
XLA Modules:
  0.0 97.5 jit_solution(16735797376012730159)
XLA Ops:
  0.6 0.0 copy-start.2
  0.6 3.7 %stats.1 = f32[8,256]{1,0:T(8,128)S(1)} custom-call(bf16[2048,1024]{1,0:T(8,128)(2,1)} %x_ref.3), custom_call_target="tpu_custom_call" | custom-call | flops 12582912 | bytes 4194304 | tf_op jit(solution)/shard_map/stats/pallas_call | solution.py:193
  4.3 3.3 %collective-permute-start = (f32[8,256]{1,0:T(8,128)S(1)}, f32[8,256]{1,0:T(8,128)S(1)}, u32[]{:S(2)}, u32[]{:S(2)}) collective-permute-start(f32[8,256]{1,0:T(8,128)S(1)} %stats.1), channel_id=1, source_target_pairs={{0,1},{1,0},{2,3},{3,2},{4,5},{5,4},{6,7},{7,6},{8,9},{9,8},{10,11... | collective-permute-start | bytes 24584 | tf_op jit(solution)/shard_map/ppermute | solution.py:46
  7.6 0.8 collective-permute-done
  8.5 1.1 %collective-permute-start.1 = (f32[8,256]{1,0:T(8,128)S(1)}, f32[8,256]{1,0:T(8,128)S(1)}, u32[]{:S(2)}, u32[]{:S(2)}) collective-permute-start(f32[8,256]{1,0:T(8,128)S(1)} %log_add_fusion.1), channel_id=1, source_target_pairs={{0,2},{1,3},{2,0},{3,1},{4,6},{5,7},{6,4},{7,5},{8,10},{9,11},{10,... | collective-permute-start | bytes 24584 | tf_op jit(solution)/shard_map/ppermute | solution.py:46
  9.6 0.0 copy-done.2
  9.6 0.0 copy-start
  9.6 1.0 %transpose.22.et_ref = bf16[512,2048]{1,0:T(8,128)(2,1)S(1)} custom-call(bf16[2048,512]{1,0:T(8,128)(2,1)S(1)} %copy-done.2), custom_call_target="tpu_custom_call" | custom-call | bytes 4194304 | tf_op jit(solution)/shard_map/transpose/pallas_call | solution.py:210
  10.6 2.0 %collective-permute-done.1 = f32[8,256]{1,0:T(8,128)S(1)} collective-permute-done((f32[8,256]{1,0:T(8,128)S(1)}, f32[8,256]{1,0:T(8,128)S(1)}, u32[]{:S(2)}, u32[]{:S(2)}) %collective-permute-start.1) | collective-permute-done | bytes 8224 | tf_op jit(solution)/shard_map/ppermute | solution.py:46
  12.6 0.0 copy-done
  12.6 3.6 %forward.1 = bf16[512,1024]{1,0:T(8,128)(2,1)S(1)} custom-call(bf16[2048,1024]{1,0:T(8,128)(2,1)S(1)} %copy-done, bf16[512,2048]{1,0:T(8,128)(2,1)S(1)} %transpose.22.et_ref, f32[8,256]{1,0:T(8,128)S(1)} %log_add_fusion.log_ref), custom_call_target="tpu_custom_call" | custom-call | flops 2147483648 | bytes 8388608 | tf_op jit(solution)/shard_map/forward/pallas_call | solution.py:224
  16.2 0.1 copy.10
  16.3 0.0 copy-start.3
  16.3 0.1 copy.9
  16.4 0.2 bitcast_select_fusion
  16.6 24.9 %all_to_all.20 = bf16[8,64,1024]{2,1,0:T(8,128)(2,1)S(1)} all-to-all(bf16[8,64,1024]{2,1,0:T(8,128)(2,1)S(1)} %bitcast_select_fusion), channel_id=1, replica_groups={{0,4,64,68,128,132,192,196},{8,12,72,76,136,140,200,204},{16,20,80,84,1..., dimensions={0} | all-to-all | bytes 2097152 | tf_op jit(solution)/shard_map/all_to_all | solution.py:37
  41.5 0.2 reduce_sum.48
  41.7 9.6 %all_to_all.21 = bf16[8,8,1024]{2,1,0:T(8,128)(2,1)S(1)} all-to-all(bf16[8,8,1024]{2,1,0:T(8,128)(2,1)S(1)} %bitcast.36), channel_id=1, replica_groups={{0,8,16,24,32,40,48,56},{4,12,20,28,36,44,52,60},{64,72,80,88,96,104,11..., dimensions={0} | all-to-all | bytes 262144 | tf_op jit(solution)/shard_map/all_to_all | solution.py:37
  51.3 0.0 copy-done.3
  51.3 0.2 multiply_reduce_fusion.2
  51.5 0.1 collective-permute-start.2
  51.6 1.1 %collective-permute-done.2 = f32[3,8]{1,0:T(4,128)S(1)} collective-permute-done((f32[3,8]{1,0:T(4,128)S(1)}, f32[3,8]{1,0:T(4,128)S(1)}, u32[]{:S(2)}, u32[]{:S(2)}) %collective-permute-start.2) | collective-permute-done | bytes 128 | tf_op jit(solution)/shard_map/ppermute | solution.py:46
  52.7 2.5 %collective-permute-start.3 = (f32[3,8]{1,0:T(4,128)S(1)}, f32[3,8]{1,0:T(4,128)S(1)}, u32[]{:S(2)}, u32[]{:S(2)}) collective-permute-start(f32[3,8]{1,0:T(4,128)S(1)} %fusion.2), channel_id=1, source_target_pairs={{0,2},{1,3},{2,0},{3,1},{4,6},{5,7},{6,4},{7,5},{8,10},{9,11},{10,... | collective-permute-start | bytes 296 | tf_op jit(solution)/shard_map/ppermute | solution.py:46
  55.3 1.5 %collective-permute-done.3 = f32[3,8]{1,0:T(4,128)S(1)} collective-permute-done((f32[3,8]{1,0:T(4,128)S(1)}, f32[3,8]{1,0:T(4,128)S(1)}, u32[]{:S(2)}, u32[]{:S(2)}) %collective-permute-start.3) | collective-permute-done | bytes 128 | tf_op jit(solution)/shard_map/ppermute | solution.py:46
  56.8 0.5 multiply_multiply_fusion
  57.3 0.1 subtract_convert_fusion
  57.4 7.9 %all_to_all.22 = bf16[8,8,1024]{2,1,0:T(8,128)(2,1)S(1)} all-to-all(bf16[8,8,1024]{2,1,0:T(8,128)(2,1)S(1)} %broadcast_in_dim.6), channel_id=1, replica_groups={{0,8,16,24,32,40,48,56},{4,12,20,28,36,44,52,60},{64,72,80,88,96,104,11..., dimensions={0} | all-to-all | bytes 262144 | tf_op jit(solution)/shard_map/all_to_all | solution.py:37
  65.3 0.0 copy-start.1
  65.3 0.1 broadcast_in_dim.8
  65.4 20.4 %all_to_all.23 = bf16[8,64,1024]{2,1,0:T(8,128)(2,1)S(1)} all-to-all(bf16[8,64,1024]{2,1,0:T(8,128)(2,1)S(1)} %broadcast_in_dim.8), channel_id=1, replica_groups={{0,4,64,68,128,132,192,196},{8,12,72,76,136,140,200,204},{16,20,80,84,1..., dimensions={0} | all-to-all | bytes 2097152 | tf_op jit(solution)/shard_map/all_to_all | solution.py:37
  85.9 0.1 bitcast_select_fusion.1
  86.0 0.1 copy.12
  86.1 0.0 copy-done.1
  86.1 3.5 %backward.1 = (f32[2048,1024]{1,0:T(8,128)S(1)}, f32[2048,1024]{1,0:T(8,128)S(1)}, f32[8,256]{1,0:T(8,128)S(1)}) custom-call(bf16[2048,1024]{1,0:T(8,128)(2,1)S(1)} %copy-done.1, bf16[2048,512]{1,0:T(8,128)(2,1)S(1)} %copy-done.2, bf16[512,1024]{1,0:T(8,128)(2,1)S(1)} %bitcast.32, f32[8,256]{1,0:T(8,128)S(1)} %log_add_fusion.log_ref), custom_call_target="tpu_custom_call" | custom-call | flops 2147483648 | bytes 8388608 | tf_op jit(solution)/shard_map/backward/pallas_call | solution.py:242
  89.6 0.1 collective-permute-start.4
  89.7 1.2 %collective-permute-done.4 = f32[8,256]{1,0:T(8,128)S(1)} collective-permute-done((f32[8,256]{1,0:T(8,128)S(1)}, f32[8,256]{1,0:T(8,128)S(1)}, u32[]{:S(2)}, u32[]{:S(2)}) %collective-permute-start.4) | collective-permute-done | bytes 8224 | tf_op jit(solution)/shard_map/ppermute | solution.py:46
  90.8 2.5 %collective-permute-start.5 = (f32[8,256]{1,0:T(8,128)S(1)}, f32[8,256]{1,0:T(8,128)S(1)}, u32[]{:S(2)}, u32[]{:S(2)}) collective-permute-start(f32[8,256]{1,0:T(8,128)S(1)} %add.60), channel_id=1, source_target_pairs={{0,2},{1,3},{2,0},{3,1},{4,6},{5,7},{6,4},{7,5},{8,10},{9,11},{10,... | collective-permute-start | bytes 24584 | tf_op jit(solution)/shard_map/ppermute | solution.py:46
  93.3 1.5 %collective-permute-done.5 = f32[8,256]{1,0:T(8,128)S(1)} collective-permute-done((f32[8,256]{1,0:T(8,128)S(1)}, f32[8,256]{1,0:T(8,128)S(1)}, u32[]{:S(2)}, u32[]{:S(2)}) %collective-permute-start.5) | collective-permute-done | bytes 8224 | tf_op jit(solution)/shard_map/ppermute | solution.py:46
  94.8 2.7 %gradient.1 = bf16[2048,1024]{1,0:T(8,128)(2,1)} custom-call(f32[2048,1024]{1,0:T(8,128)S(1)} %get-tuple-element.5.probs_ref, f32[2048,1024]{1,0:T(8,128)S(1)} %get-tuple-element.6.dprobs_ref, f32[8,256]{1,0:T(8,128)S(1)} %add.61.dot_ref), custom_call_target="tpu_custom_call" | custom-call | flops 6291456 | bytes 8388608 | tf_op jit(solution)/shard_map/gradient/pallas_call | solution.py:260
  (9 shorter events, 0.1 us)
Async XLA Ops:
  0.6 9.0 %copy-start.2 = (bf16[2048,512]{1,0:T(8,128)(2,1)S(1)}, bf16[2048,512]{1,0:T(8,128)(2,1)}, u32[]{:S(2)}) copy-start(bf16[2048,512]{1,0:T(8,128)(2,1)} %e_ref.3) | copy-start | bytes 6291460
  4.3 4.2 %collective-permute-start = (f32[8,256]{1,0:T(8,128)S(1)}, f32[8,256]{1,0:T(8,128)S(1)}, u32[]{:S(2)}, u32[]{:S(2)}) collective-permute-start(f32[8,256]{1,0:T(8,128)S(1)} %stats.1), channel_id=1, source_target_pairs={{0,1},{1,0},{2,3},{3,2},{4,5},{5,4},{6,7},{7,6},{8,9},{9,8},{10,11... | collective-permute-start | bytes 24584 | tf_op jit(solution)/shard_map/ppermute | solution.py:46
  8.5 4.1 %collective-permute-start.1 = (f32[8,256]{1,0:T(8,128)S(1)}, f32[8,256]{1,0:T(8,128)S(1)}, u32[]{:S(2)}, u32[]{:S(2)}) collective-permute-start(f32[8,256]{1,0:T(8,128)S(1)} %log_add_fusion.1), channel_id=1, source_target_pairs={{0,2},{1,3},{2,0},{3,1},{4,6},{5,7},{6,4},{7,5},{8,10},{9,11},{10,... | collective-permute-start | bytes 24584 | tf_op jit(solution)/shard_map/ppermute | solution.py:46
  9.6 3.0 %copy-start = (bf16[2048,1024]{1,0:T(8,128)(2,1)S(1)}, bf16[2048,1024]{1,0:T(8,128)(2,1)}, u32[]{:S(2)}) copy-start(bf16[2048,1024]{1,0:T(8,128)(2,1)} %x_ref.3) | copy-start | bytes 12582916
  16.3 35.0 %copy-start.3 = (f32[8,1024]{1,0:T(8,128)S(1)}, f32[8,1024]{1,0:T(8,128)}, u32[]{:S(2)}) copy-start(f32[8,1024]{1,0:T(8,128)} %param.5) | copy-start | bytes 98308
  51.5 1.2 %collective-permute-start.2 = (f32[3,8]{1,0:T(4,128)S(1)}, f32[3,8]{1,0:T(4,128)S(1)}, u32[]{:S(2)}, u32[]{:S(2)}) collective-permute-start(f32[3,8]{1,0:T(4,128)S(1)} %pad_maximum_fusion), channel_id=1, source_target_pairs={{0,1},{1,0},{2,3},{3,2},{4,5},{5,4},{6,7},{7,6},{8,9},{9,8},{10,11... | collective-permute-start | bytes 296 | tf_op jit(solution)/shard_map/ppermute | solution.py:46
  52.7 4.0 %collective-permute-start.3 = (f32[3,8]{1,0:T(4,128)S(1)}, f32[3,8]{1,0:T(4,128)S(1)}, u32[]{:S(2)}, u32[]{:S(2)}) collective-permute-start(f32[3,8]{1,0:T(4,128)S(1)} %fusion.2), channel_id=1, source_target_pairs={{0,2},{1,3},{2,0},{3,1},{4,6},{5,7},{6,4},{7,5},{8,10},{9,11},{10,... | collective-permute-start | bytes 296 | tf_op jit(solution)/shard_map/ppermute | solution.py:46
  65.3 20.8 %copy-start.1 = (bf16[2048,1024]{1,0:T(8,128)(2,1)S(1)}, bf16[2048,1024]{1,0:T(8,128)(2,1)}, u32[]{:S(2)}) copy-start(bf16[2048,1024]{1,0:T(8,128)(2,1)} %x_ref.3) | copy-start | bytes 12582916
  89.6 1.3 %collective-permute-start.4 = (f32[8,256]{1,0:T(8,128)S(1)}, f32[8,256]{1,0:T(8,128)S(1)}, u32[]{:S(2)}, u32[]{:S(2)}) collective-permute-start(f32[8,256]{1,0:T(8,128)S(1)} %get-tuple-element.7), channel_id=1, source_target_pairs={{0,1},{1,0},{2,3},{3,2},{4,5},{5,4},{6,7},{7,6},{8,9},{9,8},{10,11... | collective-permute-start | bytes 24584 | tf_op jit(solution)/shard_map/ppermute | solution.py:46
  90.8 4.0 %collective-permute-start.5 = (f32[8,256]{1,0:T(8,128)S(1)}, f32[8,256]{1,0:T(8,128)S(1)}, u32[]{:S(2)}, u32[]{:S(2)}) collective-permute-start(f32[8,256]{1,0:T(8,128)S(1)} %add.60), channel_id=1, source_target_pairs={{0,2},{1,3},{2,0},{3,1},{4,6},{5,7},{6,4},{7,5},{8,10},{9,11},{10,... | collective-permute-start | bytes 24584 | tf_op jit(solution)/shard_map/ppermute | solution.py:46

commit v6 on v5

--- a/solution.py
+++ b/solution.py
@@ -98,9 +98,18 @@
         out_ref[pl.ds(i, 1), :] = row_top + jnp.log(row_total)
 
 
-def transpose_kernel(e_ref, out_ref):
-    @pl.loop(0, e_ref.shape[0] // ROWS)
+def transpose_kernel(e_hbm, out_ref, e_ref, sems):
+    steps = e_ref.shape[0] // ROWS
+
+    def copy(i):
+        return pltpu.make_async_copy(e_hbm.at[block(i), :], e_ref.at[block(i), :], sems.at[i])
+
+    for i in range(steps):
+        copy(i).start()
+
+    @pl.loop(0, steps)
     def _(i):
+        copy(i).wait()
         out_ref[:, block(i)] = e_ref[block(i), :].T
 
 
@@ -175,6 +184,31 @@
         copy(i).wait()
 
 
+def gene_sums_kernel(part_ref, measured_ref, predicted_ref, sums_ref):
+    rows = part_ref.shape[0]
+    pairs = [part_ref[k : k + 2 * R, :].astype(jnp.float32) for k in range(0, rows, 2 * R)]
+    pairs = fold(pairs, jnp.add)
+    predicted = pairs[:R] + pairs[R:]
+    predicted_ref[...] = predicted
+    measured = measured_ref[...]
+    groups = lane_groups(predicted.shape[1])
+    for k, v in enumerate([predicted * measured, predicted * predicted, measured * measured]):
+        sums_ref[k * R : (k + 1) * R, :] = fold([v[:, g] for g in groups], jnp.add)
+
+
+def share_kernel(sums_ref, predicted_ref, measured_ref, share_ref, cosine_ref):
+    sums = jnp.sum(sums_ref[...], axis=1, keepdims=True)
+    inner, pred_sq, meas_sq = sums[:R], sums[R : 2 * R], sums[2 * R :]
+    inv_p = lax.rsqrt(pred_sq + 1e-06)
+    inv_m = lax.rsqrt(meas_sq + 1e-06)
+    cosine = inner * (inv_p * inv_m)
+    cosine_ref[...] = jnp.broadcast_to(cosine, cosine_ref.shape)
+    share = cosine * inv_p * inv_p * predicted_ref[...] - inv_p * inv_m * measured_ref[...]
+    share = jnp.concatenate([share, share]).astype(jnp.bfloat16)
+    for k in range(0, share_ref.shape[0], 2 * R):
+        share_ref[k : k + 2 * R, :] = share
+
+
 VMEM = pl.BlockSpec(memory_space=pltpu.VMEM)
 HBM = pl.BlockSpec(memory_space=pltpu.HBM)
 
@@ -209,9 +243,13 @@
     cells, genes = expression.shape
     return pl.pallas_call(
         transpose_kernel,
-        in_specs=[VMEM],
+        in_specs=[HBM],
         out_specs=VMEM,
         out_shape=jax.ShapeDtypeStruct((genes, cells), expression.dtype),
+        scratch_shapes=[
+            pltpu.VMEM((cells, genes), expression.dtype),
+            pltpu.SemaphoreType.DMA((cells // ROWS,)),
+        ],
         compiler_params=params(8),
         cost_estimate=cost(0, cells * genes * 4),
         name="transpose",
@@ -272,10 +310,40 @@
     )(probs, d_probs, row_dot)
 
 
+def gene_sums(part, measured):
+    rows, spots = part.shape
+    return pl.pallas_call(
+        gene_sums_kernel,
+        in_specs=[VMEM] * 2,
+        out_specs=[VMEM] * 2,
+        out_shape=[
+            jax.ShapeDtypeStruct((R, spots), jnp.float32),
+            jax.ShapeDtypeStruct((3 * R, LANES), jnp.float32),
+        ],
+        compiler_params=params(4),
+        name="gene_sums",
+    )(part, measured)
+
+
+def gradient_share(sums, predicted, measured):
+    spots = predicted.shape[1]
+    return pl.pallas_call(
+        share_kernel,
+        in_specs=[VMEM] * 3,
+        out_specs=[VMEM] * 2,
+        out_shape=[
+            jax.ShapeDtypeStruct((8 * R, spots), jnp.bfloat16),
+            jax.ShapeDtypeStruct((R, LANES), jnp.float32),
+        ],
+        compiler_params=params(4),
+        name="share",
+    )(sums, predicted, measured)
+
+
 def body(logits, expression, measured):
     spots = logits.shape[1]
     local_log = local_log_sum(pltpu.with_memory_space_constraint(logits, pltpu.HBM))
-    expression_t = transposed(expression)
+    expression_t = transposed(pltpu.with_memory_space_constraint(expression, pltpu.HBM))
     log_total = narrow_combine(local_log, log_add)
     part = partial_predicted(logits, expression_t, log_total)
     part = part.reshape(Y, Z, X, R, spots)
@@ -284,24 +352,11 @@
         part.transpose(1, 0, 2, 3, 4).reshape(8, Y * X * R, spots),
     )
     part = swap(part, WIDE_STAGE).astype(jnp.float32).sum(0).astype(jnp.bfloat16)
-    part = swap(part.reshape(8, R, spots), SHORT_STAGE)
-    predicted = part.astype(jnp.float32).sum(0)
-    sums = jnp.stack(
-        [
-            jnp.sum(predicted * measured, axis=1),
-            jnp.sum(predicted * predicted, axis=1),
-            jnp.sum(measured * measured, axis=1),
-        ]
-    )
-    sums = narrow_combine(sums, jnp.add)
-    inner, pred_sq, meas_sq = sums[0], sums[1], sums[2]
-    inv_p = lax.rsqrt(pred_sq + 1e-06)
-    inv_m = lax.rsqrt(meas_sq + 1e-06)
-    similarity = inner * (inv_p * inv_m)
-    share = (
-        (similarity * inv_p * inv_p)[:, None] * predicted - (inv_p * inv_m)[:, None] * measured
-    ).astype(jnp.bfloat16)
-    share = swap(jnp.broadcast_to(share[None], (8, R, spots)), SHORT_STAGE).reshape(8 * R, spots)
+    part = swap(part.reshape(8, R, spots), SHORT_STAGE).reshape(8 * R, spots)
+    predicted, sums = gene_sums(part, measured)
+    share, cosine = gradient_share(narrow_combine(sums, jnp.add), predicted, measured)
+    similarity = cosine[:, 0]
+    share = swap(share.reshape(8, R, spots), SHORT_STAGE).reshape(8 * R, spots)
     share = swap(jnp.broadcast_to(share[None], (8, 8 * R, spots)), WIDE_STAGE)
     d_pred = by_core(
         share.reshape(Y, X, Z, R, spots).transpose(0, 2, 1, 3, 4),

time: 97.8 us -> 97.7 us (level)
  starting transfers between devices: 9.6 us -> 8.25 us
  Pallas kernels: 14.4 us -> 15.6 us
    ppermute x6, starting transfers between devices: 9.6 us -> 8.25 us  [narrow_combine(): v = op(v, lax.ppermute(v, 'narrow', [(i, i ^ d) for i in range(4)]))]
    pallas_call x1 -> x3, Pallas kernels: 1.01 us -> 2.32 us  [the longest x1 2.19 us: transposed(): pl.pallas_call(transpose_kernel, in_specs=[HBM], out_specs=VMEM, out_shap...]
  transfers between devices with their start and end apart: 6 -> 6, of which waited for: 6 -> 6; matrix products, arithmetic and copies ran while one was open for 0% -> 1% of each run, Pallas kernels for 1% -> 2%
where the time goes in v6:
time: 97.7 us; the launch traced here: 97.5 us
  blocking collectives  63.6 us (65%)
  Pallas kernels  15.6 us (16%)
  starting transfers between devices  8.25 us (8%)
  waiting for transfers between devices  7.73 us (8%)
  local copies, waits for them, and re-layouts  1.04 us (1%)
    all_to_all x4, blocking collectives, swap(): return lax.all_to_all(v, ('wide', 'narrow'), 0, 0, axis_index_groups=groups)  63.6 us
    ppermute x6, starting transfers between devices, narrow_combine(): v = op(v, lax.ppermute(v, 'narrow', [(i, i ^ d) for i in range(4)]))  8.25 us
    ppermute x6, waiting for transfers between devices, narrow_combine(): v = op(v, lax.ppermute(v, 'narrow', [(i, i ^ d) for i in range(4)]))  7.73 us
    pallas_call x1, Pallas kernels, partial_predicted(): pl.pallas_call(functools.partial(forward_kernel, 256), in_specs=[VMEM] *...  3.6 us
    pallas_call x1, Pallas kernels, local_log_sum(): pl.pallas_call(stats_kernel, in_specs=[HBM], out_specs=VMEM, out_shape=ja...  3.52 us
    pallas_call x1, Pallas kernels, backward(): pl.pallas_call(functools.partial(backward_kernel, 512), in_specs=[VMEM] *...  3.47 us
    pallas_call x1, Pallas kernels, gradient(): pl.pallas_call(functools.partial(gradient_kernel, scale, size), in_specs=...  2.65 us
    pallas_call x1, Pallas kernels, transposed(): pl.pallas_call(transpose_kernel, in_specs=[HBM], out_specs=VMEM, out_shap...  2.19 us
  transfers between devices with their start and end apart: 6, of which 6 were waited for; matrix products, arithmetic and copies ran while one was open for 1% of the time, Pallas kernels for 2%

profile of v6, /device:TPU:1, one launch (start us, length us, event | category | flops | bytes accessed | tf_op | source)
XLA Modules:
  0.0 97.5 jit_solution(12580422562524722272)
XLA Ops:
  0.6 3.5 %stats.1 = f32[8,256]{1,0:T(8,128)S(1)} custom-call(bf16[2048,1024]{1,0:T(8,128)(2,1)} %x_ref.3), custom_call_target="tpu_custom_call" | custom-call | flops 12582912 | bytes 4194304 | tf_op jit(solution)/shard_map/stats/pallas_call | solution.py:227
  4.2 3.3 %collective-permute-start = (f32[8,256]{1,0:T(8,128)S(1)}, f32[8,256]{1,0:T(8,128)S(1)}, u32[]{:S(2)}, u32[]{:S(2)}) collective-permute-start(f32[8,256]{1,0:T(8,128)S(1)} %stats.1), channel_id=1, source_target_pairs={{0,1},{1,0},{2,3},{3,2},{4,5},{5,4},{6,7},{7,6},{8,9},{9,8},{10,11... | collective-permute-start | bytes 24584 | tf_op jit(solution)/shard_map/ppermute | solution.py:46
  7.5 0.8 collective-permute-done
  8.3 1.1 %collective-permute-start.1 = (f32[8,256]{1,0:T(8,128)S(1)}, f32[8,256]{1,0:T(8,128)S(1)}, u32[]{:S(2)}, u32[]{:S(2)}) collective-permute-start(f32[8,256]{1,0:T(8,128)S(1)} %log_add_fusion.1), channel_id=1, source_target_pairs={{0,2},{1,3},{2,0},{3,1},{4,6},{5,7},{6,4},{7,5},{8,10},{9,11},{10,... | collective-permute-start | bytes 24584 | tf_op jit(solution)/shard_map/ppermute | solution.py:46
  9.4 0.0 copy-start
  9.4 2.2 %transpose.19.et_ref = bf16[512,2048]{1,0:T(8,128)(2,1)S(1)} custom-call(bf16[2048,512]{1,0:T(8,128)(2,1)} %e_ref.1), custom_call_target="tpu_custom_call" | custom-call | bytes 4194304 | tf_op jit(solution)/shard_map/transpose/pallas_call | solution.py:244
  11.6 0.8 collective-permute-done.1
  12.4 0.0 copy-done
  12.4 3.6 %forward.1 = bf16[512,1024]{1,0:T(8,128)(2,1)S(1)} custom-call(bf16[2048,1024]{1,0:T(8,128)(2,1)S(1)} %copy-done, bf16[512,2048]{1,0:T(8,128)(2,1)S(1)} %transpose.19.et_ref, f32[8,256]{1,0:T(8,128)S(1)} %log_add_fusion.log_ref), custom_call_target="tpu_custom_call" | custom-call | flops 2147483648 | bytes 8388608 | tf_op jit(solution)/shard_map/forward/pallas_call | solution.py:262
  16.1 0.1 copy.6
  16.2 0.0 copy-start.3
  16.2 0.1 copy.5
  16.3 0.2 bitcast_select_fusion
  16.5 25.5 %all_to_all.20 = bf16[8,64,1024]{2,1,0:T(8,128)(2,1)S(1)} all-to-all(bf16[8,64,1024]{2,1,0:T(8,128)(2,1)S(1)} %bitcast_select_fusion), channel_id=1, replica_groups={{0,4,64,68,128,132,192,196},{8,12,72,76,136,140,200,204},{16,20,80,84,1..., dimensions={0} | all-to-all | bytes 2097152 | tf_op jit(solution)/shard_map/all_to_all | solution.py:37
  42.0 0.2 reduce_sum.12
  42.2 9.6 %all_to_all.21 = bf16[8,8,1024]{2,1,0:T(8,128)(2,1)S(1)} all-to-all(bf16[8,8,1024]{2,1,0:T(8,128)(2,1)S(1)} %bitcast.27), channel_id=1, replica_groups={{0,8,16,24,32,40,48,56},{4,12,20,28,36,44,52,60},{64,72,80,88,96,104,11..., dimensions={0} | all-to-all | bytes 262144 | tf_op jit(solution)/shard_map/all_to_all | solution.py:37
  51.7 0.0 copy-done.3
  51.8 0.1 collective-permute-start.2
  51.9 1.2 %collective-permute-done.2 = f32[24,128]{1,0:T(8,128)S(1)} collective-permute-done((f32[24,128]{1,0:T(8,128)S(1)}, f32[24,128]{1,0:T(8,128)S(1)}, u32[]{:S(2)}, u32[]{:S(2)}) %collective-permute-start.2) | collective-permute-done | bytes 12320 | tf_op jit(solution)/shard_map/ppermute | solution.py:46
  53.0 1.8 %collective-permute-start.3 = (f32[24,128]{1,0:T(8,128)S(1)}, f32[24,128]{1,0:T(8,128)S(1)}, u32[]{:S(2)}, u32[]{:S(2)}) collective-permute-start(f32[24,128]{1,0:T(8,128)S(1)} %add.34), channel_id=1, source_target_pairs={{0,2},{1,3},{2,0},{3,1},{4,6},{5,7},{6,4},{7,5},{8,10},{9,11},{10,... | collective-permute-start | bytes 36872 | tf_op jit(solution)/shard_map/ppermute | solution.py:46
  54.9 2.2 %collective-permute-done.3 = f32[24,128]{1,0:T(8,128)S(1)} collective-permute-done((f32[24,128]{1,0:T(8,128)S(1)}, f32[24,128]{1,0:T(8,128)S(1)}, u32[]{:S(2)}, u32[]{:S(2)}) %collective-permute-start.3) | collective-permute-done | bytes 12320 | tf_op jit(solution)/shard_map/ppermute | solution.py:46
  57.1 0.1 share.1
  57.2 7.9 %all_to_all.22 = bf16[8,8,1024]{2,1,0:T(8,128)(2,1)S(1)} all-to-all(bf16[8,8,1024]{2,1,0:T(8,128)(2,1)S(1)} %bitcast.23), channel_id=1, replica_groups={{0,8,16,24,32,40,48,56},{4,12,20,28,36,44,52,60},{64,72,80,88,96,104,11..., dimensions={0} | all-to-all | bytes 262144 | tf_op jit(solution)/shard_map/all_to_all | solution.py:37
  65.1 0.0 copy-start.1
  65.1 0.0 copy-start.2
  65.1 0.1 broadcast_in_dim.8
  65.3 20.6 %all_to_all.23 = bf16[8,64,1024]{2,1,0:T(8,128)(2,1)S(1)} all-to-all(bf16[8,64,1024]{2,1,0:T(8,128)(2,1)S(1)} %broadcast_in_dim.8), channel_id=1, replica_groups={{0,4,64,68,128,132,192,196},{8,12,72,76,136,140,200,204},{16,20,80,84,1..., dimensions={0} | all-to-all | bytes 2097152 | tf_op jit(solution)/shard_map/all_to_all | solution.py:37
  85.8 0.1 bitcast_select_fusion.1
  86.0 0.1 copy.8
  86.0 0.0 copy-done.1
  86.1 0.0 copy-done.2
  86.1 3.5 %backward.1 = (f32[2048,1024]{1,0:T(8,128)S(1)}, f32[2048,1024]{1,0:T(8,128)S(1)}, f32[8,256]{1,0:T(8,128)S(1)}) custom-call(bf16[2048,1024]{1,0:T(8,128)(2,1)S(1)} %copy-done.1, bf16[2048,512]{1,0:T(8,128)(2,1)S(1)} %copy-done.2, bf16[512,1024]{1,0:T(8,128)(2,1)S(1)} %bitcast.21, f32[8,256]{1,0:T(8,128)S(1)} %log_add_fusion.log_ref), custom_call_target="tpu_custom_call" | custom-call | flops 2147483648 | bytes 8388608 | tf_op jit(solution)/shard_map/backward/pallas_call | solution.py:280
  89.5 0.1 collective-permute-start.4
  89.6 1.2 %collective-permute-done.4 = f32[8,256]{1,0:T(8,128)S(1)} collective-permute-done((f32[8,256]{1,0:T(8,128)S(1)}, f32[8,256]{1,0:T(8,128)S(1)}, u32[]{:S(2)}, u32[]{:S(2)}) %collective-permute-start.4) | collective-permute-done | bytes 8224 | tf_op jit(solution)/shard_map/ppermute | solution.py:46
  90.8 1.8 %collective-permute-start.5 = (f32[8,256]{1,0:T(8,128)S(1)}, f32[8,256]{1,0:T(8,128)S(1)}, u32[]{:S(2)}, u32[]{:S(2)}) collective-permute-start(f32[8,256]{1,0:T(8,128)S(1)} %add.36), channel_id=1, source_target_pairs={{0,2},{1,3},{2,0},{3,1},{4,6},{5,7},{6,4},{7,5},{8,10},{9,11},{10,... | collective-permute-start | bytes 24584 | tf_op jit(solution)/shard_map/ppermute | solution.py:46
  92.6 0.6 slice_reduce_fusion
  93.2 1.6 %collective-permute-done.5 = f32[8,256]{1,0:T(8,128)S(1)} collective-permute-done((f32[8,256]{1,0:T(8,128)S(1)}, f32[8,256]{1,0:T(8,128)S(1)}, u32[]{:S(2)}, u32[]{:S(2)}) %collective-permute-start.5) | collective-permute-done | bytes 8224 | tf_op jit(solution)/shard_map/ppermute | solution.py:46
  94.8 2.7 %gradient.1 = bf16[2048,1024]{1,0:T(8,128)(2,1)} custom-call(f32[2048,1024]{1,0:T(8,128)S(1)} %get-tuple-element.12.probs_ref, f32[2048,1024]{1,0:T(8,128)S(1)} %get-tuple-element.13.dprobs_ref, f32[8,256]{1,0:T(8,128)S(1)} %add.37.dot_ref), custom_call_target="tpu_custom_call" | custom-call | flops 6291456 | bytes 8388608 | tf_op jit(solution)/shard_map/gradient/pallas_call | solution.py:298
  (7 shorter events, 0.1 us)
Async XLA Ops:
  4.2 4.2 %collective-permute-start = (f32[8,256]{1,0:T(8,128)S(1)}, f32[8,256]{1,0:T(8,128)S(1)}, u32[]{:S(2)}, u32[]{:S(2)}) collective-permute-start(f32[8,256]{1,0:T(8,128)S(1)} %stats.1), channel_id=1, source_target_pairs={{0,1},{1,0},{2,3},{3,2},{4,5},{5,4},{6,7},{7,6},{8,9},{9,8},{10,11... | collective-permute-start | bytes 24584 | tf_op jit(solution)/shard_map/ppermute | solution.py:46
  8.3 4.1 %collective-permute-start.1 = (f32[8,256]{1,0:T(8,128)S(1)}, f32[8,256]{1,0:T(8,128)S(1)}, u32[]{:S(2)}, u32[]{:S(2)}) collective-permute-start(f32[8,256]{1,0:T(8,128)S(1)} %log_add_fusion.1), channel_id=1, source_target_pairs={{0,2},{1,3},{2,0},{3,1},{4,6},{5,7},{6,4},{7,5},{8,10},{9,11},{10,... | collective-permute-start | bytes 24584 | tf_op jit(solution)/shard_map/ppermute | solution.py:46
  9.4 3.0 %copy-start = (bf16[2048,1024]{1,0:T(8,128)(2,1)S(1)}, bf16[2048,1024]{1,0:T(8,128)(2,1)}, u32[]{:S(2)}) copy-start(bf16[2048,1024]{1,0:T(8,128)(2,1)} %x_ref.3) | copy-start | bytes 12582916
  16.2 35.6 %copy-start.3 = (f32[8,1024]{1,0:T(8,128)S(1)}, f32[8,1024]{1,0:T(8,128)}, u32[]{:S(2)}) copy-start(f32[8,1024]{1,0:T(8,128)} %measured_ref.3) | copy-start | bytes 98308
  51.8 1.3 %collective-permute-start.2 = (f32[24,128]{1,0:T(8,128)S(1)}, f32[24,128]{1,0:T(8,128)S(1)}, u32[]{:S(2)}, u32[]{:S(2)}) collective-permute-start(f32[24,128]{1,0:T(8,128)S(1)} %get-tuple-element.9), channel_id=1, source_target_pairs={{0,1},{1,0},{2,3},{3,2},{4,5},{5,4},{6,7},{7,6},{8,9},{9,8},{10,11... | collective-permute-start | bytes 36872 | tf_op jit(solution)/shard_map/ppermute | solution.py:46
  53.0 4.0 %collective-permute-start.3 = (f32[24,128]{1,0:T(8,128)S(1)}, f32[24,128]{1,0:T(8,128)S(1)}, u32[]{:S(2)}, u32[]{:S(2)}) collective-permute-start(f32[24,128]{1,0:T(8,128)S(1)} %add.34), channel_id=1, source_target_pairs={{0,2},{1,3},{2,0},{3,1},{4,6},{5,7},{6,4},{7,5},{8,10},{9,11},{10,... | collective-permute-start | bytes 36872 | tf_op jit(solution)/shard_map/ppermute | solution.py:46
  65.1 20.9 %copy-start.1 = (bf16[2048,1024]{1,0:T(8,128)(2,1)S(1)}, bf16[2048,1024]{1,0:T(8,128)(2,1)}, u32[]{:S(2)}) copy-start(bf16[2048,1024]{1,0:T(8,128)(2,1)} %x_ref.3) | copy-start | bytes 12582916
  65.1 20.9 %copy-start.2 = (bf16[2048,512]{1,0:T(8,128)(2,1)S(1)}, bf16[2048,512]{1,0:T(8,128)(2,1)}, u32[]{:S(2)}) copy-start(bf16[2048,512]{1,0:T(8,128)(2,1)} %e_ref.1) | copy-start | bytes 6291460
  89.5 1.3 %collective-permute-start.4 = (f32[8,256]{1,0:T(8,128)S(1)}, f32[8,256]{1,0:T(8,128)S(1)}, u32[]{:S(2)}, u32[]{:S(2)}) collective-permute-start(f32[8,256]{1,0:T(8,128)S(1)} %get-tuple-element.14), channel_id=1, source_target_pairs={{0,1},{1,0},{2,3},{3,2},{4,5},{5,4},{6,7},{7,6},{8,9},{9,8},{10,11... | collective-permute-start | bytes 24584 | tf_op jit(solution)/shard_map/ppermute | solution.py:46
  90.8 4.0 %collective-permute-start.5 = (f32[8,256]{1,0:T(8,128)S(1)}, f32[8,256]{1,0:T(8,128)S(1)}, u32[]{:S(2)}, u32[]{:S(2)}) collective-permute-start(f32[8,256]{1,0:T(8,128)S(1)} %add.36), channel_id=1, source_target_pairs={{0,2},{1,3},{2,0},{3,1},{4,6},{5,7},{6,4},{7,5},{8,10},{9,11},{10,... | collective-permute-start | bytes 24584 | tf_op jit(solution)/shard_map/ppermute | solution.py:46

commit v7 on v6

--- a/solution.py
+++ b/solution.py
@@ -8,8 +8,11 @@
 from jax.sharding import PartitionSpec as P
 
 Y, Z, X, R, N = 4, 8, 2, 8, 4
+H, L = 4, 2
+FOUR, MEMBERS = 4, 16
 LANES = 128
 ROWS = 256
+FORWARD_TILE = 256
 MIB = 1 << 20
 
 
@@ -21,24 +24,95 @@
     return wide_index(y, z, x) * N + n
 
 
-def yx_groups(n):
-    return [[device_index(y, z, x, n) for y in range(Y) for x in range(X)] for z in range(Z)]
-
-
-def z_groups(n):
-    return [[device_index(y, z, x, n) for z in range(Z)] for y in range(Y) for x in range(X)]
-
-
-WIDE_STAGE = [g for n in range(N) for g in (z_groups(n) if n % 2 else yx_groups(n))]
-SHORT_STAGE = [g for n in range(N) for g in (yx_groups(n) if n % 2 else z_groups(n))]
-
-
-def swap(v, groups):
-    return lax.all_to_all(v, ("wide", "narrow"), 0, 0, axis_index_groups=groups)
+def zx_groups(n):
+    return [[device_index(y, z, x, n) for z in range(Z) for x in range(X)] for y in range(Y)]
+
+
+def yh_groups(n):
+    return [
+        [device_index(y, 2 * h + l, x, n) for y in range(Y) for h in range(H)]
+        for x in range(X)
+        for l in range(L)
+    ]
+
+
+def partner(y, z, x, n, k):
+    if n % 2 == 0:
+        return device_index((y + k) % Y, z, x, n)
+    o = (L * x + z % L) ^ k
+    return device_index(y, z - z % L + o % L, o // L, n)
+
+
+FIRST = {
+    k: [
+        (device_index(y, z, x, n), partner(y, z, x, n, k))
+        for y in range(Y)
+        for z in range(Z)
+        for x in range(X)
+        for n in range(N)
+    ]
+    for k in (1, 2, 3)
+}
+SECOND = [g for n in range(N) for g in (yh_groups(n) if n % 2 else zx_groups(n))]
+ORDER = (2, 1, 3)
+
+
+def send_first(v, k):
+    return lax.ppermute(v, ("wide", "narrow"), FIRST[k])
+
+
+def swap_second(v):
+    return lax.all_to_all(v, ("wide", "narrow"), 0, 0, axis_index_groups=SECOND)
 
 
 def by_core(even, odd):
     return jnp.where(lax.axis_index("narrow") % 2 == 0, even, odd)
+
+
+def own_block():
+    wide = lax.axis_index("wide")
+    return by_core(wide // (Z * X), (wide % X) * L + (wide // X) % L)
+
+
+def reduce_scatter(part):
+    spots = part.shape[1]
+    blocks = by_core(
+        part.reshape(FOUR, -1, spots),
+        part.reshape(Y, H, L, X, R, spots)
+        .transpose(3, 2, 0, 1, 4, 5)
+        .reshape(FOUR, -1, spots),
+    )
+    own = own_block()
+
+    def pick(i):
+        return lax.dynamic_index_in_dim(blocks, i, 0, keepdims=False)
+
+    got = [send_first(pick(by_core((own + k) % FOUR, own ^ k)), k) for k in ORDER]
+    total = fold([v.astype(jnp.float32) for v in [pick(own)] + got], jnp.add)
+    total = total.astype(jnp.bfloat16).reshape(MEMBERS, R, spots)
+    return swap_second(total).reshape(MEMBERS * R, spots)
+
+
+def all_gather_second(share):
+    spots = share.shape[1]
+    return swap_second(share.reshape(MEMBERS, R, spots)).reshape(MEMBERS * R, spots)
+
+
+def all_gather_first(block):
+    spots = block.shape[1]
+    got = {k: send_first(block, k) for k in ORDER}
+    got[0] = block
+    own = own_block()
+    blocks = jnp.stack(
+        [
+            lax.select_n(by_core((own - j) % FOUR, own ^ j), *[got[k] for k in range(FOUR)])
+            for j in range(FOUR)
+        ]
+    )
+    return by_core(
+        blocks.reshape(-1, spots),
+        blocks.reshape(X, L, Y, H, R, spots).transpose(2, 3, 1, 0, 4, 5).reshape(-1, spots),
+    )
 
 
 def narrow_combine(v, op):
@@ -113,16 +187,44 @@
         out_ref[:, block(i)] = e_ref[block(i), :].T
 
 
-def forward_kernel(tile, x_ref, et_ref, log_ref, part_ref, low, column):
+def probs_kernel(x_hbm, e_hbm, log_ref, probs_ref, e_ref, x_ref, sems):
     cells, spots = x_ref.shape
+    steps = cells // ROWS
+
+    def copy(i):
+        return pltpu.make_async_copy(x_hbm.at[block(i), :], x_ref.at[block(i), :], sems.at[i])
+
+    for i in range(steps):
+        copy(i).start()
+    expression = pltpu.make_async_copy(e_hbm, e_ref, sems.at[steps])
+    expression.start()
+
+    @pl.loop(0, steps)
+    def _(i):
+        copy(i).wait()
+        log_total = as_column(log_ref[pl.ds(i, 1), :])
+        for g in lane_groups(spots):
+            probs_ref[block(i), g] = jnp.exp(x_ref[block(i), g].astype(jnp.float32) - log_total)
+
+    expression.wait()
+
+
+def forward_kernel(tile, x_hbm, et_ref, log_ref, part_ref, x_ref, low, column, sems):
+    cells, spots = x_ref.shape
+    tiles = [slice(k, k + tile) for k in range(0, spots, tile)]
+    copies = [
+        pltpu.make_async_copy(x_hbm.at[:, cols], x_ref.at[:, cols], sems.at[k])
+        for k, cols in enumerate(tiles)
+    ]
+    for copy in copies:
+        copy.start()
 
     @pl.loop(0, cells // ROWS)
     def _(i):
         column[block(i), :] = as_column(log_ref[pl.ds(i, 1), :])
 
-    tiles = [slice(k, k + tile) for k in range(0, spots, tile)]
-
     def fill(cols):
+        copies[cols.start // tile].wait()
         for k in range(cols.start, cols.stop, LANES):
             g = slice(k, k + LANES)
             probs = jnp.exp(x_ref[:, g].astype(jnp.float32) - column[...])
@@ -136,15 +238,8 @@
             fill(later)
 
 
-def backward_kernel(size, x_ref, e_ref, d_ref, log_ref, probs_ref, dprobs_ref, dot_ref):
+def backward_kernel(size, probs_ref, e_ref, d_ref, dprobs_ref, dot_ref):
     cells, spots = probs_ref.shape
-
-    def fill(first):
-        for k in range(first, first + size, ROWS):
-            rows = slice(k, k + ROWS)
-            log_total = as_column(log_ref[k // ROWS : k // ROWS + 1, :])
-            for g in lane_groups(spots):
-                probs_ref[rows, g] = jnp.exp(x_ref[rows, g].astype(jnp.float32) - log_total)
 
     def row_dots(first):
         for k in range(first, first + size, ROWS):
@@ -155,7 +250,6 @@
     for first in range(0, cells, size):
         rows = slice(first, first + size)
         dprobs_ref[rows, :] = jnp.dot(e_ref[rows, :], d_ref[...], preferred_element_type=jnp.float32)
-        fill(first)
         if first:
             row_dots(first - size)
     row_dots(cells - size)
@@ -256,17 +350,40 @@
     )(expression)
 
 
+def probabilities(logits, expression, log_total):
+    cells, spots = logits.shape
+    steps = cells // ROWS
+    return pl.pallas_call(
+        probs_kernel,
+        in_specs=[HBM, HBM, VMEM],
+        out_specs=[VMEM, VMEM],
+        out_shape=[
+            jax.ShapeDtypeStruct((cells, spots), jnp.float32),
+            jax.ShapeDtypeStruct(expression.shape, expression.dtype),
+        ],
+        scratch_shapes=[
+            pltpu.VMEM((cells, spots), logits.dtype),
+            pltpu.SemaphoreType.DMA((steps + 1,)),
+        ],
+        compiler_params=params(8),
+        cost_estimate=cost(cells * spots * 4, cells * spots * 4, cells * spots),
+        name="probs",
+    )(logits, expression, log_total)
+
+
 def partial_predicted(logits, expression_t, log_total):
     cells, spots = logits.shape
     genes = expression_t.shape[0]
     return pl.pallas_call(
-        functools.partial(forward_kernel, 256),
-        in_specs=[VMEM] * 3,
+        functools.partial(forward_kernel, FORWARD_TILE),
+        in_specs=[HBM, VMEM, VMEM],
         out_specs=VMEM,
         out_shape=jax.ShapeDtypeStruct((genes, spots), jnp.bfloat16),
         scratch_shapes=[
             pltpu.VMEM((cells, spots), jnp.bfloat16),
+            pltpu.VMEM((cells, spots), jnp.bfloat16),
             pltpu.VMEM((cells, LANES), jnp.float32),
+            pltpu.SemaphoreType.DMA((spots // FORWARD_TILE,)),
         ],
         compiler_params=params(16),
         cost_estimate=cost(2 * cells * spots * genes, cells * spots * 4, cells * spots),
@@ -274,22 +391,21 @@
     )(logits, expression_t, log_total)
 
 
-def backward(logits, expression, d_pred, log_total):
-    cells, spots = logits.shape
+def backward(probs, expression, d_pred):
+    cells, spots = probs.shape
     genes = expression.shape[1]
     return pl.pallas_call(
         functools.partial(backward_kernel, 512),
-        in_specs=[VMEM] * 4,
-        out_specs=[VMEM] * 3,
+        in_specs=[VMEM] * 3,
+        out_specs=[VMEM] * 2,
         out_shape=[
             jax.ShapeDtypeStruct((cells, spots), jnp.float32),
-            jax.ShapeDtypeStruct((cells, spots), jnp.float32),
             jax.ShapeDtypeStruct((cells // ROWS, ROWS), jnp.float32),
         ],
-        compiler_params=params(12),
-        cost_estimate=cost(2 * cells * spots * genes, cells * spots * 4, cells * spots),
+        compiler_params=params(8),
+        cost_estimate=cost(2 * cells * spots * genes, cells * spots * 4),
         name="backward",
-    )(logits, expression, d_pred, log_total)
+    )(probs, expression, d_pred)
 
 
 def gradient(probs, d_probs, row_dot, scale):
@@ -332,7 +448,7 @@
         in_specs=[VMEM] * 3,
         out_specs=[VMEM] * 2,
         out_shape=[
-            jax.ShapeDtypeStruct((8 * R, spots), jnp.bfloat16),
+            jax.ShapeDtypeStruct((MEMBERS * R, spots), jnp.bfloat16),
             jax.ShapeDtypeStruct((R, LANES), jnp.float32),
         ],
         compiler_params=params(4),
@@ -342,27 +458,20 @@
 
 def body(logits, expression, measured):
     spots = logits.shape[1]
-    local_log = local_log_sum(pltpu.with_memory_space_constraint(logits, pltpu.HBM))
-    expression_t = transposed(pltpu.with_memory_space_constraint(expression, pltpu.HBM))
+    far_logits = pltpu.with_memory_space_constraint(logits, pltpu.HBM)
+    far_expression = pltpu.with_memory_space_constraint(expression, pltpu.HBM)
+    local_log = local_log_sum(far_logits)
+    expression_t = transposed(far_expression)
     log_total = narrow_combine(local_log, log_add)
-    part = partial_predicted(logits, expression_t, log_total)
-    part = part.reshape(Y, Z, X, R, spots)
-    part = by_core(
-        part.transpose(0, 2, 1, 3, 4).reshape(8, Z * R, spots),
-        part.transpose(1, 0, 2, 3, 4).reshape(8, Y * X * R, spots),
-    )
-    part = swap(part, WIDE_STAGE).astype(jnp.float32).sum(0).astype(jnp.bfloat16)
-    part = swap(part.reshape(8, R, spots), SHORT_STAGE).reshape(8 * R, spots)
+    part = partial_predicted(far_logits, expression_t, log_total)
+    part = reduce_scatter(part)
     predicted, sums = gene_sums(part, measured)
     share, cosine = gradient_share(narrow_combine(sums, jnp.add), predicted, measured)
     similarity = cosine[:, 0]
-    share = swap(share.reshape(8, R, spots), SHORT_STAGE).reshape(8 * R, spots)
-    share = swap(jnp.broadcast_to(share[None], (8, 8 * R, spots)), WIDE_STAGE)
-    d_pred = by_core(
-        share.reshape(Y, X, Z, R, spots).transpose(0, 2, 1, 3, 4),
-        share.reshape(Z, Y, X, R, spots).transpose(1, 0, 2, 3, 4),
-    ).reshape(Y * Z * X * R, spots)
-    probs, d_probs, row_dot = backward(logits, expression, d_pred, log_total)
+    share, log_total = lax.optimization_barrier((all_gather_second(share), log_total))
+    probs, expression = probabilities(far_logits, far_expression, log_total)
+    d_pred = all_gather_first(share)
+    d_probs, row_dot = backward(probs, expression, d_pred)
     row_dot = narrow_combine(row_dot, jnp.add)
     grad = gradient(probs, d_probs, row_dot, float(spots * lax.axis_size("narrow")))
     return (grad, similarity)

time: 97.7 us -> 97.9 us (level)
  blocking collectives: 63.6 us -> 39 us
  waiting for transfers between devices: 7.73 us -> 17.5 us
  starting transfers between devices: 8.25 us -> 17.8 us
  Pallas kernels: 15.6 us -> 20.8 us
    all_to_all x4 -> x2, blocking collectives: 63.6 us -> 39 us  [swap_second(): return lax.all_to_all(v, ('wide', 'narrow'), 0, 0, axis_index_groups=SECOND)]
    ppermute x0 -> x6, waiting for transfers between devices: none -> 10.4 us  [send_first(): return lax.ppermute(v, ('wide', 'narrow'), FIRST[k])]
    pallas_call x1 -> x2, Pallas kernels: 3.6 us -> 9.84 us  [the longest x1 6.88 us: partial_predicted(): pl.pallas_call(functools.partial(forward_kernel, FORWARD_TILE), in_specs=...]
    ppermute x0 -> x6, starting transfers between devices: none -> 5.52 us  [send_first(): return lax.ppermute(v, ('wide', 'narrow'), FIRST[k])]
    ppermute x6, starting transfers between devices: 8.25 us -> 12.3 us  [narrow_combine(): v = op(v, lax.ppermute(v, 'narrow', [(i, i ^ d) for i in range(4)]))]
  transfers between devices with their start and end apart: 6 -> 12, of which waited for: 6 -> 10; matrix products, arithmetic and copies ran while one was open for 1% -> 1% of each run, Pallas kernels for 2% -> 5%
where the time goes in v7:
time: 97.9 us; the launch traced here: 97.8 us
  blocking collectives  39 us (40%)
  Pallas kernels  20.8 us (21%)
  starting transfers between devices  17.8 us (18%)
  waiting for transfers between devices  17.5 us (18%)
    all_to_all x2, blocking collectives, swap_second(): return lax.all_to_all(v, ('wide', 'narrow'), 0, 0, axis_index_groups=SECOND)  39 us
    ppermute x6, starting transfers between devices, narrow_combine(): v = op(v, lax.ppermute(v, 'narrow', [(i, i ^ d) for i in range(4)]))  12.3 us
    ppermute x6, waiting for transfers between devices, send_first(): return lax.ppermute(v, ('wide', 'narrow'), FIRST[k])  10.4 us
    ppermute x6, waiting for transfers between devices, narrow_combine(): v = op(v, lax.ppermute(v, 'narrow', [(i, i ^ d) for i in range(4)]))  7.15 us
    pallas_call x1, Pallas kernels, partial_predicted(): pl.pallas_call(functools.partial(forward_kernel, FORWARD_TILE), in_specs=...  6.88 us
    ppermute x6, starting transfers between devices, send_first(): return lax.ppermute(v, ('wide', 'narrow'), FIRST[k])  5.52 us
    pallas_call x1, Pallas kernels, local_log_sum(): pl.pallas_call(stats_kernel, in_specs=[HBM], out_specs=VMEM, out_shape=ja...  3.52 us
    pallas_call x1, Pallas kernels, probabilities(): pl.pallas_call(probs_kernel, in_specs=[HBM, HBM, VMEM], out_specs=[VMEM,...  2.96 us
  transfers between devices with their start and end apart: 12, of which 10 were waited for; matrix products, arithmetic and copies ran while one was open for 1% of the time, Pallas kernels for 5%

profile of v7, /device:TPU:1, one launch (start us, length us, event | category | flops | bytes accessed | tf_op | source)
XLA Modules:
  0.0 97.8 jit_solution(15537681064347396684)
XLA Ops:
  0.6 3.5 %stats.1 = f32[8,256]{1,0:T(8,128)S(1)} custom-call(bf16[2048,1024]{1,0:T(8,128)(2,1)} %x_hbm.5), custom_call_target="tpu_custom_call" | custom-call | flops 12582912 | bytes 4194304 | tf_op jit(solution)/shard_map/stats/pallas_call | solution.py:321
  4.2 3.3 %collective-permute-start = (f32[8,256]{1,0:T(8,128)S(1)}, f32[8,256]{1,0:T(8,128)S(1)}, u32[]{:S(2)}, u32[]{:S(2)}) collective-permute-start(f32[8,256]{1,0:T(8,128)S(1)} %stats.1), channel_id=1, source_target_pairs={{0,1},{1,0},{2,3},{3,2},{4,5},{5,4},{6,7},{7,6},{8,9},{9,8},{10,11... | collective-permute-start | bytes 24584 | tf_op jit(solution)/shard_map/ppermute | solution.py:120
  7.5 0.8 collective-permute-done
  8.3 1.1 %collective-permute-start.1 = (f32[8,256]{1,0:T(8,128)S(1)}, f32[8,256]{1,0:T(8,128)S(1)}, u32[]{:S(2)}, u32[]{:S(2)}) collective-permute-start(f32[8,256]{1,0:T(8,128)S(1)} %log_add_fusion.1), channel_id=1, source_target_pairs={{0,2},{1,3},{2,0},{3,1},{4,6},{5,7},{6,4},{7,5},{8,10},{9,11},{10,... | collective-permute-start | bytes 24584 | tf_op jit(solution)/shard_map/ppermute | solution.py:120
  9.4 2.0 %transpose.21.et_ref = bf16[512,2048]{1,0:T(8,128)(2,1)S(1)} custom-call(bf16[2048,512]{1,0:T(8,128)(2,1)} %e_hbm.3), custom_call_target="tpu_custom_call" | custom-call | bytes 4194304 | tf_op jit(solution)/shard_map/transpose/pallas_call | solution.py:338
  11.5 0.9 collective-permute-done.1
  12.4 6.9 %forward.1 = bf16[512,1024]{1,0:T(8,128)(2,1)S(1)} custom-call(bf16[2048,1024]{1,0:T(8,128)(2,1)} %x_hbm.5, bf16[512,2048]{1,0:T(8,128)(2,1)S(1)} %transpose.21.et_ref, f32[8,256]{1,0:T(8,128)S(1)} %log_add_fusion.log_ref), custom_call_target="tpu_custom_call" | custom-call | flops 2147483648 | bytes 8388608 | tf_op jit(solution)/shard_map/forward/pallas_call | solution.py:377
  19.3 0.0 copy-start
  19.3 0.1 copy.5
  19.4 0.1 broadcast_select_fusion
  19.6 0.1 dynamic-slice_bitcast_fusion.2
  19.6 0.1 collective-permute-start.2
  19.7 1.9 %collective-permute-start.4 = (bf16[128,1024]{1,0:T(8,128)(2,1)S(1)}, bf16[128,1024]{1,0:T(8,128)(2,1)S(1)}, u32[]{:S(2)}, u32[]{:S(2)}) collective-permute-start(bf16[128,1024]{1,0:T(8,128)(2,1)S(1)} %get-tuple-element.27), channel_id=1, source_target_pairs={{0,192},{1,13},{2,194},{3,15},{4,196},{5,9},{6,198},{7,11},{8,200}... | collective-permute-start | bytes 786440 | tf_op jit(solution)/shard_map/ppermute | solution.py:61
  21.6 0.7 collective-permute-start.3
  22.4 5.7 %collective-permute-done.2 = bf16[128,1024]{1,0:T(8,128)(2,1)S(1)} collective-permute-done((bf16[128,1024]{1,0:T(8,128)(2,1)S(1)}, bf16[128,1024]{1,0:T(8,128)(2,1)S(1)}, u32[]{:S(2)}, u32[]{:S(2)}) %collective-permute-start.2) | collective-permute-done | bytes 262176 | tf_op jit(solution)/shard_map/ppermute | solution.py:61
  28.0 0.0 collective-permute-done.4
  28.0 1.2 %collective-permute-done.3 = bf16[128,1024]{1,0:T(8,128)(2,1)S(1)} collective-permute-done((bf16[128,1024]{1,0:T(8,128)(2,1)S(1)}, bf16[128,1024]{1,0:T(8,128)(2,1)S(1)}, u32[]{:S(2)}, u32[]{:S(2)}) %collective-permute-start.3) | collective-permute-done | bytes 262176 | tf_op jit(solution)/shard_map/ppermute | solution.py:61
  29.3 0.2 fusion.2
  29.4 22.4 %all_to_all.10 = bf16[16,8,1024]{2,1,0:T(8,128)(2,1)S(1)} all-to-all(bf16[16,8,1024]{2,1,0:T(8,128)(2,1)S(1)} %fusion.2), channel_id=1, replica_groups={{0,4,8,12,16,20,24,28,32,36,40,44,48,52,56,60},{64,68,72,76,80,84,88,92..., dimensions={0} | all-to-all | bytes 524288 | tf_op jit(solution)/shard_map/all_to_all | solution.py:65
  51.9 0.0 copy-done
  51.9 0.1 collective-permute-start.5
  52.0 1.1 %collective-permute-done.5 = f32[24,128]{1,0:T(8,128)S(1)} collective-permute-done((f32[24,128]{1,0:T(8,128)S(1)}, f32[24,128]{1,0:T(8,128)S(1)}, u32[]{:S(2)}, u32[]{:S(2)}) %collective-permute-start.5) | collective-permute-done | bytes 12320 | tf_op jit(solution)/shard_map/ppermute | solution.py:120
  53.2 2.1 %collective-permute-start.6 = (f32[24,128]{1,0:T(8,128)S(1)}, f32[24,128]{1,0:T(8,128)S(1)}, u32[]{:S(2)}, u32[]{:S(2)}) collective-permute-start(f32[24,128]{1,0:T(8,128)S(1)} %add.128), channel_id=1, source_target_pairs={{0,2},{1,3},{2,0},{3,1},{4,6},{5,7},{6,4},{7,5},{8,10},{9,11},{10,... | collective-permute-start | bytes 36872 | tf_op jit(solution)/shard_map/ppermute | solution.py:120
  55.3 1.9 %collective-permute-done.6 = f32[24,128]{1,0:T(8,128)S(1)} collective-permute-done((f32[24,128]{1,0:T(8,128)S(1)}, f32[24,128]{1,0:T(8,128)S(1)}, u32[]{:S(2)}, u32[]{:S(2)}) %collective-permute-start.6) | collective-permute-done | bytes 12320 | tf_op jit(solution)/shard_map/ppermute | solution.py:120
  57.2 0.1 share.1
  57.3 16.6 %all_to_all.11 = bf16[16,8,1024]{2,1,0:T(8,128)(2,1)S(1)} all-to-all(bf16[16,8,1024]{2,1,0:T(8,128)(2,1)S(1)} %bitcast.37), channel_id=1, replica_groups={{0,4,8,12,16,20,24,28,32,36,40,44,48,52,56,60},{64,68,72,76,80,84,88,92..., dimensions={0} | all-to-all | bytes 524288 | tf_op jit(solution)/shard_map/all_to_all | solution.py:65
  73.9 1.7 %collective-permute-start.9 = (bf16[128,1024]{1,0:T(8,128)(2,1)S(1)}, bf16[128,1024]{1,0:T(8,128)(2,1)S(1)}, u32[]{:S(2)}, u32[]{:S(2)}) collective-permute-start(bf16[128,1024]{1,0:T(8,128)(2,1)S(1)} %bitcast.40), channel_id=1, source_target_pairs={{0,192},{1,13},{2,194},{3,15},{4,196},{5,9},{6,198},{7,11},{8,200}... | collective-permute-start | bytes 786440 | tf_op jit(solution)/shard_map/ppermute | solution.py:61
  75.7 1.1 %collective-permute-start.8 = (bf16[128,1024]{1,0:T(8,128)(2,1)S(1)}, bf16[128,1024]{1,0:T(8,128)(2,1)S(1)}, u32[]{:S(2)}, u32[]{:S(2)}) collective-permute-start(bf16[128,1024]{1,0:T(8,128)(2,1)S(1)} %bitcast.41), channel_id=1, source_target_pairs={{0,128},{1,5},{2,130},{3,7},{4,132},{5,1},{6,134},{7,3},{8,136},{9... | collective-permute-start | bytes 786440 | tf_op jit(solution)/shard_map/ppermute | solution.py:61
  76.7 0.0 collective-permute-start.7
  76.7 3.0 %probs.1 = (f32[2048,1024]{1,0:T(8,128)S(1)}, bf16[2048,512]{1,0:T(8,128)(2,1)S(1)}) custom-call(bf16[2048,1024]{1,0:T(8,128)(2,1)} %x_hbm.5, bf16[2048,512]{1,0:T(8,128)(2,1)} %e_hbm.3, f32[8,256]{1,0:T(8,128)S(1)} %log_add_fusion.log_ref), custom_call_target="tpu_custom_call" | custom-call | flops 8388608 | bytes 8388608 | tf_op jit(solution)/shard_map/probs/pallas_call | solution.py:356
  79.7 0.5 collective-permute-done.9
  80.2 3.0 %collective-permute-done.8 = bf16[128,1024]{1,0:T(8,128)(2,1)S(1)} collective-permute-done((bf16[128,1024]{1,0:T(8,128)(2,1)S(1)}, bf16[128,1024]{1,0:T(8,128)(2,1)S(1)}, u32[]{:S(2)}, u32[]{:S(2)}) %collective-permute-start.8) | collective-permute-done | bytes 262176 | tf_op jit(solution)/shard_map/ppermute | solution.py:61
  83.2 0.0 collective-permute-done.7
  83.2 0.1 select_bitcast_fusion.3
  83.3 0.1 pad_maximum_fusion
  83.4 0.1 copy.6
  83.5 0.2 bitcast_select_fusion.d_ref
  83.8 2.7 %backward.1 = (f32[2048,1024]{1,0:T(8,128)S(1)}, f32[8,256]{1,0:T(8,128)S(1)}) custom-call(f32[2048,1024]{1,0:T(8,128)S(1)} %get-tuple-element.16.probs_ref, bf16[2048,512]{1,0:T(8,128)(2,1)S(1)} %get-tuple-element.17.e_ref, bf16[512,1024]{1,0:T(8,128)(2,1)S(1)} %bitcast_select_fusion.d_ref), custom_call_target="tpu_custom_call" | custom-call | flops 2147483648 | bytes 8388608 | tf_op jit(solution)/shard_map/backward/pallas_call | solution.py:397
  86.5 3.8 %collective-permute-start.10 = (f32[8,256]{1,0:T(8,128)S(1)}, f32[8,256]{1,0:T(8,128)S(1)}, u32[]{:S(2)}, u32[]{:S(2)}) collective-permute-start(f32[8,256]{1,0:T(8,128)S(1)} %get-tuple-element.20), channel_id=1, source_target_pairs={{0,1},{1,0},{2,3},{3,2},{4,5},{5,4},{6,7},{7,6},{8,9},{9,8},{10,11... | collective-permute-start | bytes 24584 | tf_op jit(solution)/shard_map/ppermute | solution.py:120
  90.2 0.8 collective-permute-done.10
  91.1 1.9 %collective-permute-start.11 = (f32[8,256]{1,0:T(8,128)S(1)}, f32[8,256]{1,0:T(8,128)S(1)}, u32[]{:S(2)}, u32[]{:S(2)}) collective-permute-start(f32[8,256]{1,0:T(8,128)S(1)} %add.134), channel_id=1, source_target_pairs={{0,2},{1,3},{2,0},{3,1},{4,6},{5,7},{6,4},{7,5},{8,10},{9,11},{10,... | collective-permute-start | bytes 24584 | tf_op jit(solution)/shard_map/ppermute | solution.py:120
  92.9 0.6 slice_reduce_fusion
  93.5 1.5 %collective-permute-done.11 = f32[8,256]{1,0:T(8,128)S(1)} collective-permute-done((f32[8,256]{1,0:T(8,128)S(1)}, f32[8,256]{1,0:T(8,128)S(1)}, u32[]{:S(2)}, u32[]{:S(2)}) %collective-permute-start.11) | collective-permute-done | bytes 8224 | tf_op jit(solution)/shard_map/ppermute | solution.py:120
  95.1 2.5 %gradient.1 = bf16[2048,1024]{1,0:T(8,128)(2,1)} custom-call(f32[2048,1024]{1,0:T(8,128)S(1)} %get-tuple-element.16.probs_ref, f32[2048,1024]{1,0:T(8,128)S(1)} %get-tuple-element.19.dprobs_ref, f32[8,256]{1,0:T(8,128)S(1)} %add.135.dot_ref), custom_call_target="tpu_custom_call" | custom-call | flops 6291456 | bytes 8388608 | tf_op jit(solution)/shard_map/gradient/pallas_call | solution.py:414
  (7 shorter events, 0.1 us)
Async XLA Ops:
  4.2 4.2 %collective-permute-start = (f32[8,256]{1,0:T(8,128)S(1)}, f32[8,256]{1,0:T(8,128)S(1)}, u32[]{:S(2)}, u32[]{:S(2)}) collective-permute-start(f32[8,256]{1,0:T(8,128)S(1)} %stats.1), channel_id=1, source_target_pairs={{0,1},{1,0},{2,3},{3,2},{4,5},{5,4},{6,7},{7,6},{8,9},{9,8},{10,11... | collective-permute-start | bytes 24584 | tf_op jit(solution)/shard_map/ppermute | solution.py:120
  8.3 4.1 %collective-permute-start.1 = (f32[8,256]{1,0:T(8,128)S(1)}, f32[8,256]{1,0:T(8,128)S(1)}, u32[]{:S(2)}, u32[]{:S(2)}) collective-permute-start(f32[8,256]{1,0:T(8,128)S(1)} %log_add_fusion.1), channel_id=1, source_target_pairs={{0,2},{1,3},{2,0},{3,1},{4,6},{5,7},{6,4},{7,5},{8,10},{9,11},{10,... | collective-permute-start | bytes 24584 | tf_op jit(solution)/shard_map/ppermute | solution.py:120
  19.3 32.5 %copy-start = (f32[8,1024]{1,0:T(8,128)S(1)}, f32[8,1024]{1,0:T(8,128)}, u32[]{:S(2)}) copy-start(f32[8,1024]{1,0:T(8,128)} %measured_ref.3) | copy-start | bytes 98308
  19.6 8.4 %collective-permute-start.2 = (bf16[128,1024]{1,0:T(8,128)(2,1)S(1)}, bf16[128,1024]{1,0:T(8,128)(2,1)S(1)}, u32[]{:S(2)}, u32[]{:S(2)}) collective-permute-start(bf16[128,1024]{1,0:T(8,128)(2,1)S(1)} %get-tuple-element.26), channel_id=1, source_target_pairs={{0,128},{1,5},{2,130},{3,7},{4,132},{5,1},{6,134},{7,3},{8,136},{9... | collective-permute-start | bytes 786440 | tf_op jit(solution)/shard_map/ppermute | solution.py:61
  19.7 8.3 %collective-permute-start.4 = (bf16[128,1024]{1,0:T(8,128)(2,1)S(1)}, bf16[128,1024]{1,0:T(8,128)(2,1)S(1)}, u32[]{:S(2)}, u32[]{:S(2)}) collective-permute-start(bf16[128,1024]{1,0:T(8,128)(2,1)S(1)} %get-tuple-element.27), channel_id=1, source_target_pairs={{0,192},{1,13},{2,194},{3,15},{4,196},{5,9},{6,198},{7,11},{8,200}... | collective-permute-start | bytes 786440 | tf_op jit(solution)/shard_map/ppermute | solution.py:61
  21.6 7.6 %collective-permute-start.3 = (bf16[128,1024]{1,0:T(8,128)(2,1)S(1)}, bf16[128,1024]{1,0:T(8,128)(2,1)S(1)}, u32[]{:S(2)}, u32[]{:S(2)}) collective-permute-start(bf16[128,1024]{1,0:T(8,128)(2,1)S(1)} %get-tuple-element.28), channel_id=1, source_target_pairs={{0,64},{1,9},{2,66},{3,11},{4,68},{5,13},{6,70},{7,15},{8,72},{9,1... | collective-permute-start | bytes 786440 | tf_op jit(solution)/shard_map/ppermute | solution.py:61
  51.9 1.3 %collective-permute-start.5 = (f32[24,128]{1,0:T(8,128)S(1)}, f32[24,128]{1,0:T(8,128)S(1)}, u32[]{:S(2)}, u32[]{:S(2)}) collective-permute-start(f32[24,128]{1,0:T(8,128)S(1)} %get-tuple-element.12), channel_id=1, source_target_pairs={{0,1},{1,0},{2,3},{3,2},{4,5},{5,4},{6,7},{7,6},{8,9},{9,8},{10,11... | collective-permute-start | bytes 36872 | tf_op jit(solution)/shard_map/ppermute | solution.py:120
  53.2 4.0 %collective-permute-start.6 = (f32[24,128]{1,0:T(8,128)S(1)}, f32[24,128]{1,0:T(8,128)S(1)}, u32[]{:S(2)}, u32[]{:S(2)}) collective-permute-start(f32[24,128]{1,0:T(8,128)S(1)} %add.128), channel_id=1, source_target_pairs={{0,2},{1,3},{2,0},{3,1},{4,6},{5,7},{6,4},{7,5},{8,10},{9,11},{10,... | collective-permute-start | bytes 36872 | tf_op jit(solution)/shard_map/ppermute | solution.py:120
  73.9 6.2 %collective-permute-start.9 = (bf16[128,1024]{1,0:T(8,128)(2,1)S(1)}, bf16[128,1024]{1,0:T(8,128)(2,1)S(1)}, u32[]{:S(2)}, u32[]{:S(2)}) collective-permute-start(bf16[128,1024]{1,0:T(8,128)(2,1)S(1)} %bitcast.40), channel_id=1, source_target_pairs={{0,192},{1,13},{2,194},{3,15},{4,196},{5,9},{6,198},{7,11},{8,200}... | collective-permute-start | bytes 786440 | tf_op jit(solution)/shard_map/ppermute | solution.py:61
  75.7 7.5 %collective-permute-start.8 = (bf16[128,1024]{1,0:T(8,128)(2,1)S(1)}, bf16[128,1024]{1,0:T(8,128)(2,1)S(1)}, u32[]{:S(2)}, u32[]{:S(2)}) collective-permute-start(bf16[128,1024]{1,0:T(8,128)(2,1)S(1)} %bitcast.41), channel_id=1, source_target_pairs={{0,128},{1,5},{2,130},{3,7},{4,132},{5,1},{6,134},{7,3},{8,136},{9... | collective-permute-start | bytes 786440 | tf_op jit(solution)/shard_map/ppermute | solution.py:61
  76.7 6.4 %collective-permute-start.7 = (bf16[128,1024]{1,0:T(8,128)(2,1)S(1)}, bf16[128,1024]{1,0:T(8,128)(2,1)S(1)}, u32[]{:S(2)}, u32[]{:S(2)}) collective-permute-start(bf16[128,1024]{1,0:T(8,128)(2,1)S(1)} %bitcast.42), channel_id=1, source_target_pairs={{0,64},{1,9},{2,66},{3,11},{4,68},{5,13},{6,70},{7,15},{8,72},{9,1... | collective-permute-start | bytes 786440 | tf_op jit(solution)/shard_map/ppermute | solution.py:61
  86.5 4.6 %collective-permute-start.10 = (f32[8,256]{1,0:T(8,128)S(1)}, f32[8,256]{1,0:T(8,128)S(1)}, u32[]{:S(2)}, u32[]{:S(2)}) collective-permute-start(f32[8,256]{1,0:T(8,128)S(1)} %get-tuple-element.20), channel_id=1, source_target_pairs={{0,1},{1,0},{2,3},{3,2},{4,5},{5,4},{6,7},{7,6},{8,9},{9,8},{10,11... | collective-permute-start | bytes 24584 | tf_op jit(solution)/shard_map/ppermute | solution.py:120
  91.1 4.0 %collective-permute-start.11 = (f32[8,256]{1,0:T(8,128)S(1)}, f32[8,256]{1,0:T(8,128)S(1)}, u32[]{:S(2)}, u32[]{:S(2)}) collective-permute-start(f32[8,256]{1,0:T(8,128)S(1)} %add.134), channel_id=1, source_target_pairs={{0,2},{1,3},{2,0},{3,1},{4,6},{5,7},{6,4},{7,5},{8,10},{9,11},{10,... | collective-permute-start | bytes 24584 | tf_op jit(solution)/shard_map/ppermute | solution.py:120

commit v8 on v7

--- a/solution.py
+++ b/solution.py
@@ -12,7 +12,6 @@
 FOUR, MEMBERS = 4, 16
 LANES = 128
 ROWS = 256
-FORWARD_TILE = 256
 MIB = 1 << 20
 
 
@@ -209,33 +208,26 @@
     expression.wait()
 
 
-def forward_kernel(tile, x_hbm, et_ref, log_ref, part_ref, x_ref, low, column, sems):
+def forward_kernel(x_hbm, et_ref, log_ref, part_ref, x_ref, low, sems):
     cells, spots = x_ref.shape
-    tiles = [slice(k, k + tile) for k in range(0, spots, tile)]
-    copies = [
-        pltpu.make_async_copy(x_hbm.at[:, cols], x_ref.at[:, cols], sems.at[k])
-        for k, cols in enumerate(tiles)
-    ]
-    for copy in copies:
-        copy.start()
-
-    @pl.loop(0, cells // ROWS)
+    steps = cells // ROWS
+
+    def copy(i):
+        return pltpu.make_async_copy(x_hbm.at[block(i), :], x_ref.at[block(i), :], sems.at[i])
+
+    for i in range(steps):
+        copy(i).start()
+
+    @pl.loop(0, steps)
     def _(i):
-        column[block(i), :] = as_column(log_ref[pl.ds(i, 1), :])
-
-    def fill(cols):
-        copies[cols.start // tile].wait()
-        for k in range(cols.start, cols.stop, LANES):
-            g = slice(k, k + LANES)
-            probs = jnp.exp(x_ref[:, g].astype(jnp.float32) - column[...])
-            low[:, g] = probs.astype(jnp.bfloat16)
-
-    fill(tiles[0])
-    for cols, later in zip(tiles, tiles[1:] + [None]):
-        part = jnp.dot(et_ref[...], low[:, cols], preferred_element_type=jnp.float32)
-        part_ref[:, cols] = part.astype(jnp.bfloat16)
-        if later is not None:
-            fill(later)
+        copy(i).wait()
+        log_total = as_column(log_ref[pl.ds(i, 1), :])
+        for g in lane_groups(spots):
+            probs = jnp.exp(x_ref[block(i), g].astype(jnp.float32) - log_total)
+            low[block(i), g] = probs.astype(jnp.bfloat16)
+
+    part = jnp.dot(et_ref[...], low[...], preferred_element_type=jnp.float32)
+    part_ref[...] = part.astype(jnp.bfloat16)
 
 
 def backward_kernel(size, probs_ref, e_ref, d_ref, dprobs_ref, dot_ref):
@@ -375,15 +367,14 @@
     cells, spots = logits.shape
     genes = expression_t.shape[0]
     return pl.pallas_call(
-        functools.partial(forward_kernel, FORWARD_TILE),
+        forward_kernel,
         in_specs=[HBM, VMEM, VMEM],
         out_specs=VMEM,
         out_shape=jax.ShapeDtypeStruct((genes, spots), jnp.bfloat16),
         scratch_shapes=[
             pltpu.VMEM((cells, spots), jnp.bfloat16),
             pltpu.VMEM((cells, spots), jnp.bfloat16),
-            pltpu.VMEM((cells, LANES), jnp.float32),
-            pltpu.SemaphoreType.DMA((spots // FORWARD_TILE,)),
+            pltpu.SemaphoreType.DMA((cells // ROWS,)),
         ],
         compiler_params=params(16),
         cost_estimate=cost(2 * cells * spots * genes, cells * spots * 4, cells * spots),

time: 97.9 us -> 96.3 us (0.984)
  Pallas kernels: 20.8 us -> 19.2 us
    pallas_call x1, Pallas kernels: 6.88 us -> 5.29 us  [partial_predicted(): pl.pallas_call(forward_kernel, in_specs=[HBM, VMEM, VMEM], out_specs=VMEM...]
where the time goes in v8:
time: 96.3 us; the launch traced here: 96.2 us
  blocking collectives  39 us (40%)
  Pallas kernels  19.2 us (20%)
  starting transfers between devices  17.8 us (18%)
  waiting for transfers between devices  17.5 us (18%)
    all_to_all x2, blocking collectives, swap_second(): return lax.all_to_all(v, ('wide', 'narrow'), 0, 0, axis_index_groups=SECOND)  39 us
    ppermute x6, starting transfers between devices, narrow_combine(): v = op(v, lax.ppermute(v, 'narrow', [(i, i ^ d) for i in range(4)]))  12.3 us
    ppermute x6, waiting for transfers between devices, send_first(): return lax.ppermute(v, ('wide', 'narrow'), FIRST[k])  10.4 us
    ppermute x6, waiting for transfers between devices, narrow_combine(): v = op(v, lax.ppermute(v, 'narrow', [(i, i ^ d) for i in range(4)]))  7.15 us
    ppermute x6, starting transfers between devices, send_first(): return lax.ppermute(v, ('wide', 'narrow'), FIRST[k])  5.52 us
    pallas_call x1, Pallas kernels, partial_predicted(): pl.pallas_call(forward_kernel, in_specs=[HBM, VMEM, VMEM], out_specs=VMEM...  5.29 us
    pallas_call x1, Pallas kernels, local_log_sum(): pl.pallas_call(stats_kernel, in_specs=[HBM], out_specs=VMEM, out_shape=ja...  3.52 us
    pallas_call x1, Pallas kernels, probabilities(): pl.pallas_call(probs_kernel, in_specs=[HBM, HBM, VMEM], out_specs=[VMEM,...  2.96 us
  transfers between devices with their start and end apart: 12, of which 10 were waited for; matrix products, arithmetic and copies ran while one was open for 1% of the time, Pallas kernels for 5%

profile of v8, /device:TPU:1, one launch (start us, length us, event | category | flops | bytes accessed | tf_op | source)
XLA Modules:
  0.0 96.2 jit_solution(1890214872994594634)
XLA Ops:
  0.6 3.5 %stats.1 = f32[8,256]{1,0:T(8,128)S(1)} custom-call(bf16[2048,1024]{1,0:T(8,128)(2,1)} %x_hbm.5), custom_call_target="tpu_custom_call" | custom-call | flops 12582912 | bytes 4194304 | tf_op jit(solution)/shard_map/stats/pallas_call | solution.py:313
  4.2 3.3 %collective-permute-start = (f32[8,256]{1,0:T(8,128)S(1)}, f32[8,256]{1,0:T(8,128)S(1)}, u32[]{:S(2)}, u32[]{:S(2)}) collective-permute-start(f32[8,256]{1,0:T(8,128)S(1)} %stats.1), channel_id=1, source_target_pairs={{0,1},{1,0},{2,3},{3,2},{4,5},{5,4},{6,7},{7,6},{8,9},{9,8},{10,11... | collective-permute-start | bytes 24584 | tf_op jit(solution)/shard_map/ppermute | solution.py:119
  7.5 0.8 collective-permute-done
  8.3 1.1 %collective-permute-start.1 = (f32[8,256]{1,0:T(8,128)S(1)}, f32[8,256]{1,0:T(8,128)S(1)}, u32[]{:S(2)}, u32[]{:S(2)}) collective-permute-start(f32[8,256]{1,0:T(8,128)S(1)} %log_add_fusion.1), channel_id=1, source_target_pairs={{0,2},{1,3},{2,0},{3,1},{4,6},{5,7},{6,4},{7,5},{8,10},{9,11},{10,... | collective-permute-start | bytes 24584 | tf_op jit(solution)/shard_map/ppermute | solution.py:119
  9.4 2.0 %transpose.21.et_ref = bf16[512,2048]{1,0:T(8,128)(2,1)S(1)} custom-call(bf16[2048,512]{1,0:T(8,128)(2,1)} %e_hbm.3), custom_call_target="tpu_custom_call" | custom-call | bytes 4194304 | tf_op jit(solution)/shard_map/transpose/pallas_call | solution.py:330
  11.5 0.9 collective-permute-done.1
  12.4 5.3 %forward.1 = bf16[512,1024]{1,0:T(8,128)(2,1)S(1)} custom-call(bf16[2048,1024]{1,0:T(8,128)(2,1)} %x_hbm.5, bf16[512,2048]{1,0:T(8,128)(2,1)S(1)} %transpose.21.et_ref, f32[8,256]{1,0:T(8,128)S(1)} %log_add_fusion.log_ref), custom_call_target="tpu_custom_call" | custom-call | flops 2147483648 | bytes 8388608 | tf_op jit(solution)/shard_map/forward/pallas_call | solution.py:369
  17.7 0.0 copy-start
  17.7 0.1 copy.5
  17.8 0.1 broadcast_select_fusion
  18.0 0.1 dynamic-slice_bitcast_fusion.2
  18.0 0.1 collective-permute-start.2
  18.1 1.9 %collective-permute-start.4 = (bf16[128,1024]{1,0:T(8,128)(2,1)S(1)}, bf16[128,1024]{1,0:T(8,128)(2,1)S(1)}, u32[]{:S(2)}, u32[]{:S(2)}) collective-permute-start(bf16[128,1024]{1,0:T(8,128)(2,1)S(1)} %get-tuple-element.27), channel_id=1, source_target_pairs={{0,192},{1,13},{2,194},{3,15},{4,196},{5,9},{6,198},{7,11},{8,200}... | collective-permute-start | bytes 786440 | tf_op jit(solution)/shard_map/ppermute | solution.py:60
  20.0 0.7 collective-permute-start.3
  20.8 5.7 %collective-permute-done.2 = bf16[128,1024]{1,0:T(8,128)(2,1)S(1)} collective-permute-done((bf16[128,1024]{1,0:T(8,128)(2,1)S(1)}, bf16[128,1024]{1,0:T(8,128)(2,1)S(1)}, u32[]{:S(2)}, u32[]{:S(2)}) %collective-permute-start.2) | collective-permute-done | bytes 262176 | tf_op jit(solution)/shard_map/ppermute | solution.py:60
  26.4 0.0 collective-permute-done.4
  26.4 1.2 %collective-permute-done.3 = bf16[128,1024]{1,0:T(8,128)(2,1)S(1)} collective-permute-done((bf16[128,1024]{1,0:T(8,128)(2,1)S(1)}, bf16[128,1024]{1,0:T(8,128)(2,1)S(1)}, u32[]{:S(2)}, u32[]{:S(2)}) %collective-permute-start.3) | collective-permute-done | bytes 262176 | tf_op jit(solution)/shard_map/ppermute | solution.py:60
  27.7 0.2 fusion.2
  27.8 22.4 %all_to_all.10 = bf16[16,8,1024]{2,1,0:T(8,128)(2,1)S(1)} all-to-all(bf16[16,8,1024]{2,1,0:T(8,128)(2,1)S(1)} %fusion.2), channel_id=1, replica_groups={{0,4,8,12,16,20,24,28,32,36,40,44,48,52,56,60},{64,68,72,76,80,84,88,92..., dimensions={0} | all-to-all | bytes 524288 | tf_op jit(solution)/shard_map/all_to_all | solution.py:64
  50.3 0.0 copy-done
  50.3 0.1 collective-permute-start.5
  50.4 1.1 %collective-permute-done.5 = f32[24,128]{1,0:T(8,128)S(1)} collective-permute-done((f32[24,128]{1,0:T(8,128)S(1)}, f32[24,128]{1,0:T(8,128)S(1)}, u32[]{:S(2)}, u32[]{:S(2)}) %collective-permute-start.5) | collective-permute-done | bytes 12320 | tf_op jit(solution)/shard_map/ppermute | solution.py:119
  51.6 2.1 %collective-permute-start.6 = (f32[24,128]{1,0:T(8,128)S(1)}, f32[24,128]{1,0:T(8,128)S(1)}, u32[]{:S(2)}, u32[]{:S(2)}) collective-permute-start(f32[24,128]{1,0:T(8,128)S(1)} %add.128), channel_id=1, source_target_pairs={{0,2},{1,3},{2,0},{3,1},{4,6},{5,7},{6,4},{7,5},{8,10},{9,11},{10,... | collective-permute-start | bytes 36872 | tf_op jit(solution)/shard_map/ppermute | solution.py:119
  53.7 1.9 %collective-permute-done.6 = f32[24,128]{1,0:T(8,128)S(1)} collective-permute-done((f32[24,128]{1,0:T(8,128)S(1)}, f32[24,128]{1,0:T(8,128)S(1)}, u32[]{:S(2)}, u32[]{:S(2)}) %collective-permute-start.6) | collective-permute-done | bytes 12320 | tf_op jit(solution)/shard_map/ppermute | solution.py:119
  55.6 0.1 share.1
  55.7 16.6 %all_to_all.11 = bf16[16,8,1024]{2,1,0:T(8,128)(2,1)S(1)} all-to-all(bf16[16,8,1024]{2,1,0:T(8,128)(2,1)S(1)} %bitcast.37), channel_id=1, replica_groups={{0,4,8,12,16,20,24,28,32,36,40,44,48,52,56,60},{64,68,72,76,80,84,88,92..., dimensions={0} | all-to-all | bytes 524288 | tf_op jit(solution)/shard_map/all_to_all | solution.py:64
  72.3 1.7 %collective-permute-start.9 = (bf16[128,1024]{1,0:T(8,128)(2,1)S(1)}, bf16[128,1024]{1,0:T(8,128)(2,1)S(1)}, u32[]{:S(2)}, u32[]{:S(2)}) collective-permute-start(bf16[128,1024]{1,0:T(8,128)(2,1)S(1)} %bitcast.40), channel_id=1, source_target_pairs={{0,192},{1,13},{2,194},{3,15},{4,196},{5,9},{6,198},{7,11},{8,200}... | collective-permute-start | bytes 786440 | tf_op jit(solution)/shard_map/ppermute | solution.py:60
  74.1 1.1 %collective-permute-start.8 = (bf16[128,1024]{1,0:T(8,128)(2,1)S(1)}, bf16[128,1024]{1,0:T(8,128)(2,1)S(1)}, u32[]{:S(2)}, u32[]{:S(2)}) collective-permute-start(bf16[128,1024]{1,0:T(8,128)(2,1)S(1)} %bitcast.41), channel_id=1, source_target_pairs={{0,128},{1,5},{2,130},{3,7},{4,132},{5,1},{6,134},{7,3},{8,136},{9... | collective-permute-start | bytes 786440 | tf_op jit(solution)/shard_map/ppermute | solution.py:60
  75.1 0.0 collective-permute-start.7
  75.1 3.0 %probs.1 = (f32[2048,1024]{1,0:T(8,128)S(1)}, bf16[2048,512]{1,0:T(8,128)(2,1)S(1)}) custom-call(bf16[2048,1024]{1,0:T(8,128)(2,1)} %x_hbm.5, bf16[2048,512]{1,0:T(8,128)(2,1)} %e_hbm.3, f32[8,256]{1,0:T(8,128)S(1)} %log_add_fusion.log_ref), custom_call_target="tpu_custom_call" | custom-call | flops 8388608 | bytes 8388608 | tf_op jit(solution)/shard_map/probs/pallas_call | solution.py:348
  78.1 0.5 collective-permute-done.9
  78.6 3.0 %collective-permute-done.8 = bf16[128,1024]{1,0:T(8,128)(2,1)S(1)} collective-permute-done((bf16[128,1024]{1,0:T(8,128)(2,1)S(1)}, bf16[128,1024]{1,0:T(8,128)(2,1)S(1)}, u32[]{:S(2)}, u32[]{:S(2)}) %collective-permute-start.8) | collective-permute-done | bytes 262176 | tf_op jit(solution)/shard_map/ppermute | solution.py:60
  81.6 0.0 collective-permute-done.7
  81.6 0.1 select_bitcast_fusion.3
  81.7 0.1 pad_maximum_fusion
  81.8 0.1 copy.6
  81.9 0.2 bitcast_select_fusion.d_ref
  82.2 2.7 %backward.1 = (f32[2048,1024]{1,0:T(8,128)S(1)}, f32[8,256]{1,0:T(8,128)S(1)}) custom-call(f32[2048,1024]{1,0:T(8,128)S(1)} %get-tuple-element.16.probs_ref, bf16[2048,512]{1,0:T(8,128)(2,1)S(1)} %get-tuple-element.17.e_ref, bf16[512,1024]{1,0:T(8,128)(2,1)S(1)} %bitcast_select_fusion.d_ref), custom_call_target="tpu_custom_call" | custom-call | flops 2147483648 | bytes 8388608 | tf_op jit(solution)/shard_map/backward/pallas_call | solution.py:388
  84.9 3.8 %collective-permute-start.10 = (f32[8,256]{1,0:T(8,128)S(1)}, f32[8,256]{1,0:T(8,128)S(1)}, u32[]{:S(2)}, u32[]{:S(2)}) collective-permute-start(f32[8,256]{1,0:T(8,128)S(1)} %get-tuple-element.20), channel_id=1, source_target_pairs={{0,1},{1,0},{2,3},{3,2},{4,5},{5,4},{6,7},{7,6},{8,9},{9,8},{10,11... | collective-permute-start | bytes 24584 | tf_op jit(solution)/shard_map/ppermute | solution.py:119
  88.6 0.8 collective-permute-done.10
  89.5 1.9 %collective-permute-start.11 = (f32[8,256]{1,0:T(8,128)S(1)}, f32[8,256]{1,0:T(8,128)S(1)}, u32[]{:S(2)}, u32[]{:S(2)}) collective-permute-start(f32[8,256]{1,0:T(8,128)S(1)} %add.134), channel_id=1, source_target_pairs={{0,2},{1,3},{2,0},{3,1},{4,6},{5,7},{6,4},{7,5},{8,10},{9,11},{10,... | collective-permute-start | bytes 24584 | tf_op jit(solution)/shard_map/ppermute | solution.py:119
  91.3 0.6 slice_reduce_fusion
  92.0 1.5 %collective-permute-done.11 = f32[8,256]{1,0:T(8,128)S(1)} collective-permute-done((f32[8,256]{1,0:T(8,128)S(1)}, f32[8,256]{1,0:T(8,128)S(1)}, u32[]{:S(2)}, u32[]{:S(2)}) %collective-permute-start.11) | collective-permute-done | bytes 8224 | tf_op jit(solution)/shard_map/ppermute | solution.py:119
  93.5 2.5 %gradient.1 = bf16[2048,1024]{1,0:T(8,128)(2,1)} custom-call(f32[2048,1024]{1,0:T(8,128)S(1)} %get-tuple-element.16.probs_ref, f32[2048,1024]{1,0:T(8,128)S(1)} %get-tuple-element.19.dprobs_ref, f32[8,256]{1,0:T(8,128)S(1)} %add.135.dot_ref), custom_call_target="tpu_custom_call" | custom-call | flops 6291456 | bytes 8388608 | tf_op jit(solution)/shard_map/gradient/pallas_call | solution.py:405
  (7 shorter events, 0.1 us)
Async XLA Ops:
  4.2 4.2 %collective-permute-start = (f32[8,256]{1,0:T(8,128)S(1)}, f32[8,256]{1,0:T(8,128)S(1)}, u32[]{:S(2)}, u32[]{:S(2)}) collective-permute-start(f32[8,256]{1,0:T(8,128)S(1)} %stats.1), channel_id=1, source_target_pairs={{0,1},{1,0},{2,3},{3,2},{4,5},{5,4},{6,7},{7,6},{8,9},{9,8},{10,11... | collective-permute-start | bytes 24584 | tf_op jit(solution)/shard_map/ppermute | solution.py:119
  8.3 4.1 %collective-permute-start.1 = (f32[8,256]{1,0:T(8,128)S(1)}, f32[8,256]{1,0:T(8,128)S(1)}, u32[]{:S(2)}, u32[]{:S(2)}) collective-permute-start(f32[8,256]{1,0:T(8,128)S(1)} %log_add_fusion.1), channel_id=1, source_target_pairs={{0,2},{1,3},{2,0},{3,1},{4,6},{5,7},{6,4},{7,5},{8,10},{9,11},{10,... | collective-permute-start | bytes 24584 | tf_op jit(solution)/shard_map/ppermute | solution.py:119
  17.7 32.5 %copy-start = (f32[8,1024]{1,0:T(8,128)S(1)}, f32[8,1024]{1,0:T(8,128)}, u32[]{:S(2)}) copy-start(f32[8,1024]{1,0:T(8,128)} %measured_ref.3) | copy-start | bytes 98308
  18.0 8.4 %collective-permute-start.2 = (bf16[128,1024]{1,0:T(8,128)(2,1)S(1)}, bf16[128,1024]{1,0:T(8,128)(2,1)S(1)}, u32[]{:S(2)}, u32[]{:S(2)}) collective-permute-start(bf16[128,1024]{1,0:T(8,128)(2,1)S(1)} %get-tuple-element.26), channel_id=1, source_target_pairs={{0,128},{1,5},{2,130},{3,7},{4,132},{5,1},{6,134},{7,3},{8,136},{9... | collective-permute-start | bytes 786440 | tf_op jit(solution)/shard_map/ppermute | solution.py:60
  18.1 8.3 %collective-permute-start.4 = (bf16[128,1024]{1,0:T(8,128)(2,1)S(1)}, bf16[128,1024]{1,0:T(8,128)(2,1)S(1)}, u32[]{:S(2)}, u32[]{:S(2)}) collective-permute-start(bf16[128,1024]{1,0:T(8,128)(2,1)S(1)} %get-tuple-element.27), channel_id=1, source_target_pairs={{0,192},{1,13},{2,194},{3,15},{4,196},{5,9},{6,198},{7,11},{8,200}... | collective-permute-start | bytes 786440 | tf_op jit(solution)/shard_map/ppermute | solution.py:60
  20.0 7.6 %collective-permute-start.3 = (bf16[128,1024]{1,0:T(8,128)(2,1)S(1)}, bf16[128,1024]{1,0:T(8,128)(2,1)S(1)}, u32[]{:S(2)}, u32[]{:S(2)}) collective-permute-start(bf16[128,1024]{1,0:T(8,128)(2,1)S(1)} %get-tuple-element.28), channel_id=1, source_target_pairs={{0,64},{1,9},{2,66},{3,11},{4,68},{5,13},{6,70},{7,15},{8,72},{9,1... | collective-permute-start | bytes 786440 | tf_op jit(solution)/shard_map/ppermute | solution.py:60
  50.3 1.3 %collective-permute-start.5 = (f32[24,128]{1,0:T(8,128)S(1)}, f32[24,128]{1,0:T(8,128)S(1)}, u32[]{:S(2)}, u32[]{:S(2)}) collective-permute-start(f32[24,128]{1,0:T(8,128)S(1)} %get-tuple-element.12), channel_id=1, source_target_pairs={{0,1},{1,0},{2,3},{3,2},{4,5},{5,4},{6,7},{7,6},{8,9},{9,8},{10,11... | collective-permute-start | bytes 36872 | tf_op jit(solution)/shard_map/ppermute | solution.py:119
  51.6 4.0 %collective-permute-start.6 = (f32[24,128]{1,0:T(8,128)S(1)}, f32[24,128]{1,0:T(8,128)S(1)}, u32[]{:S(2)}, u32[]{:S(2)}) collective-permute-start(f32[24,128]{1,0:T(8,128)S(1)} %add.128), channel_id=1, source_target_pairs={{0,2},{1,3},{2,0},{3,1},{4,6},{5,7},{6,4},{7,5},{8,10},{9,11},{10,... | collective-permute-start | bytes 36872 | tf_op jit(solution)/shard_map/ppermute | solution.py:119
  72.3 6.2 %collective-permute-start.9 = (bf16[128,1024]{1,0:T(8,128)(2,1)S(1)}, bf16[128,1024]{1,0:T(8,128)(2,1)S(1)}, u32[]{:S(2)}, u32[]{:S(2)}) collective-permute-start(bf16[128,1024]{1,0:T(8,128)(2,1)S(1)} %bitcast.40), channel_id=1, source_target_pairs={{0,192},{1,13},{2,194},{3,15},{4,196},{5,9},{6,198},{7,11},{8,200}... | collective-permute-start | bytes 786440 | tf_op jit(solution)/shard_map/ppermute | solution.py:60
  74.1 7.5 %collective-permute-start.8 = (bf16[128,1024]{1,0:T(8,128)(2,1)S(1)}, bf16[128,1024]{1,0:T(8,128)(2,1)S(1)}, u32[]{:S(2)}, u32[]{:S(2)}) collective-permute-start(bf16[128,1024]{1,0:T(8,128)(2,1)S(1)} %bitcast.41), channel_id=1, source_target_pairs={{0,128},{1,5},{2,130},{3,7},{4,132},{5,1},{6,134},{7,3},{8,136},{9... | collective-permute-start | bytes 786440 | tf_op jit(solution)/shard_map/ppermute | solution.py:60
  75.1 6.4 %collective-permute-start.7 = (bf16[128,1024]{1,0:T(8,128)(2,1)S(1)}, bf16[128,1024]{1,0:T(8,128)(2,1)S(1)}, u32[]{:S(2)}, u32[]{:S(2)}) collective-permute-start(bf16[128,1024]{1,0:T(8,128)(2,1)S(1)} %bitcast.42), channel_id=1, source_target_pairs={{0,64},{1,9},{2,66},{3,11},{4,68},{5,13},{6,70},{7,15},{8,72},{9,1... | collective-permute-start | bytes 786440 | tf_op jit(solution)/shard_map/ppermute | solution.py:60
  84.9 4.6 %collective-permute-start.10 = (f32[8,256]{1,0:T(8,128)S(1)}, f32[8,256]{1,0:T(8,128)S(1)}, u32[]{:S(2)}, u32[]{:S(2)}) collective-permute-start(f32[8,256]{1,0:T(8,128)S(1)} %get-tuple-element.20), channel_id=1, source_target_pairs={{0,1},{1,0},{2,3},{3,2},{4,5},{5,4},{6,7},{7,6},{8,9},{9,8},{10,11... | collective-permute-start | bytes 24584 | tf_op jit(solution)/shard_map/ppermute | solution.py:119
  89.5 4.0 %collective-permute-start.11 = (f32[8,256]{1,0:T(8,128)S(1)}, f32[8,256]{1,0:T(8,128)S(1)}, u32[]{:S(2)}, u32[]{:S(2)}) collective-permute-start(f32[8,256]{1,0:T(8,128)S(1)} %add.134), channel_id=1, source_target_pairs={{0,2},{1,3},{2,0},{3,1},{4,6},{5,7},{6,4},{7,5},{8,10},{9,11},{10,... | collective-permute-start | bytes 24584 | tf_op jit(solution)/shard_map/ppermute | solution.py:119

commit v9 on v8

--- a/solution.py
+++ b/solution.py
@@ -159,9 +159,7 @@
     for i in range(steps):
         copy(i).start()
 
-    @pl.loop(0, steps)
-    def _(i):
-        copy(i).wait()
+    def log_sum(i):
         rows = block(i)
         top = fold([x_ref[rows, g] for g in groups], jnp.maximum).astype(jnp.float32)
         total = fold([jnp.exp(x_ref[rows, g].astype(jnp.float32) - top) for g in groups], jnp.add)
@@ -170,6 +168,13 @@
         row_total = jnp.sum(total * jnp.exp(top - row_top), axis=0, keepdims=True)
         out_ref[pl.ds(i, 1), :] = row_top + jnp.log(row_total)
 
+    @pl.loop(0, steps // 2)
+    def _(i):
+        copy(2 * i).wait()
+        copy(2 * i + 1).wait()
+        log_sum(2 * i)
+        log_sum(2 * i + 1)
+
 
 def transpose_kernel(e_hbm, out_ref, e_ref, sems):
     steps = e_ref.shape[0] // ROWS
@@ -218,13 +223,18 @@
     for i in range(steps):
         copy(i).start()
 
-    @pl.loop(0, steps)
-    def _(i):
-        copy(i).wait()
+    def fill(i):
         log_total = as_column(log_ref[pl.ds(i, 1), :])
         for g in lane_groups(spots):
             probs = jnp.exp(x_ref[block(i), g].astype(jnp.float32) - log_total)
             low[block(i), g] = probs.astype(jnp.bfloat16)
+
+    @pl.loop(0, steps // 2)
+    def _(i):
+        copy(2 * i).wait()
+        copy(2 * i + 1).wait()
+        fill(2 * i)
+        fill(2 * i + 1)
 
     part = jnp.dot(et_ref[...], low[...], preferred_element_type=jnp.float32)
     part_ref[...] = part.astype(jnp.bfloat16)

time: 96.3 us -> 96.1 us (level)
  no operation moved by 1% of the time
where the time goes in v9:
time: 96.1 us; the launch traced here: 95.9 us
  blocking collectives  39 us (41%)
  Pallas kernels  18.9 us (20%)
  starting transfers between devices  17.8 us (19%)
  waiting for transfers between devices  17.5 us (18%)
    all_to_all x2, blocking collectives, swap_second(): return lax.all_to_all(v, ('wide', 'narrow'), 0, 0, axis_index_groups=SECOND)  39 us
    ppermute x6, starting transfers between devices, narrow_combine(): v = op(v, lax.ppermute(v, 'narrow', [(i, i ^ d) for i in range(4)]))  12.3 us
    ppermute x6, waiting for transfers between devices, send_first(): return lax.ppermute(v, ('wide', 'narrow'), FIRST[k])  10.4 us
    ppermute x6, waiting for transfers between devices, narrow_combine(): v = op(v, lax.ppermute(v, 'narrow', [(i, i ^ d) for i in range(4)]))  7.15 us
    ppermute x6, starting transfers between devices, send_first(): return lax.ppermute(v, ('wide', 'narrow'), FIRST[k])  5.52 us
    pallas_call x1, Pallas kernels, partial_predicted(): pl.pallas_call(forward_kernel, in_specs=[HBM, VMEM, VMEM], out_specs=VMEM...  5.2 us
    pallas_call x1, Pallas kernels, local_log_sum(): pl.pallas_call(stats_kernel, in_specs=[HBM], out_specs=VMEM, out_shape=ja...  3.37 us
    pallas_call x1, Pallas kernels, probabilities(): pl.pallas_call(probs_kernel, in_specs=[HBM, HBM, VMEM], out_specs=[VMEM,...  2.96 us
  transfers between devices with their start and end apart: 12, of which 10 were waited for; matrix products, arithmetic and copies ran while one was open for 1% of the time, Pallas kernels for 5%

profile of v9, /device:TPU:1, one launch (start us, length us, event | category | flops | bytes accessed | tf_op | source)
XLA Modules:
  0.0 95.9 jit_solution(14915291146625378907)
XLA Ops:
  0.6 3.4 %stats.1 = f32[8,256]{1,0:T(8,128)S(1)} custom-call(bf16[2048,1024]{1,0:T(8,128)(2,1)} %x_hbm.5), custom_call_target="tpu_custom_call" | custom-call | flops 12582912 | bytes 4194304 | tf_op jit(solution)/shard_map/stats/pallas_call | solution.py:323
  4.0 3.3 %collective-permute-start = (f32[8,256]{1,0:T(8,128)S(1)}, f32[8,256]{1,0:T(8,128)S(1)}, u32[]{:S(2)}, u32[]{:S(2)}) collective-permute-start(f32[8,256]{1,0:T(8,128)S(1)} %stats.1), channel_id=1, source_target_pairs={{0,1},{1,0},{2,3},{3,2},{4,5},{5,4},{6,7},{7,6},{8,9},{9,8},{10,11... | collective-permute-start | bytes 24584 | tf_op jit(solution)/shard_map/ppermute | solution.py:119
  7.3 0.8 collective-permute-done
  8.2 1.1 %collective-permute-start.1 = (f32[8,256]{1,0:T(8,128)S(1)}, f32[8,256]{1,0:T(8,128)S(1)}, u32[]{:S(2)}, u32[]{:S(2)}) collective-permute-start(f32[8,256]{1,0:T(8,128)S(1)} %log_add_fusion.1), channel_id=1, source_target_pairs={{0,2},{1,3},{2,0},{3,1},{4,6},{5,7},{6,4},{7,5},{8,10},{9,11},{10,... | collective-permute-start | bytes 24584 | tf_op jit(solution)/shard_map/ppermute | solution.py:119
  9.3 2.0 %transpose.21.et_ref = bf16[512,2048]{1,0:T(8,128)(2,1)S(1)} custom-call(bf16[2048,512]{1,0:T(8,128)(2,1)} %e_hbm.3), custom_call_target="tpu_custom_call" | custom-call | bytes 4194304 | tf_op jit(solution)/shard_map/transpose/pallas_call | solution.py:340
  11.3 0.9 collective-permute-done.1
  12.3 5.2 %forward.1 = bf16[512,1024]{1,0:T(8,128)(2,1)S(1)} custom-call(bf16[2048,1024]{1,0:T(8,128)(2,1)} %x_hbm.5, bf16[512,2048]{1,0:T(8,128)(2,1)S(1)} %transpose.21.et_ref, f32[8,256]{1,0:T(8,128)S(1)} %log_add_fusion.log_ref), custom_call_target="tpu_custom_call" | custom-call | flops 2147483648 | bytes 8388608 | tf_op jit(solution)/shard_map/forward/pallas_call | solution.py:379
  17.5 0.0 copy-start
  17.5 0.1 copy.5
  17.6 0.1 broadcast_select_fusion
  17.7 0.1 dynamic-slice_bitcast_fusion.2
  17.8 0.1 collective-permute-start.2
  17.9 1.9 %collective-permute-start.4 = (bf16[128,1024]{1,0:T(8,128)(2,1)S(1)}, bf16[128,1024]{1,0:T(8,128)(2,1)S(1)}, u32[]{:S(2)}, u32[]{:S(2)}) collective-permute-start(bf16[128,1024]{1,0:T(8,128)(2,1)S(1)} %get-tuple-element.27), channel_id=1, source_target_pairs={{0,192},{1,13},{2,194},{3,15},{4,196},{5,9},{6,198},{7,11},{8,200}... | collective-permute-start | bytes 786440 | tf_op jit(solution)/shard_map/ppermute | solution.py:60
  19.8 0.7 collective-permute-start.3
  20.5 5.7 %collective-permute-done.2 = bf16[128,1024]{1,0:T(8,128)(2,1)S(1)} collective-permute-done((bf16[128,1024]{1,0:T(8,128)(2,1)S(1)}, bf16[128,1024]{1,0:T(8,128)(2,1)S(1)}, u32[]{:S(2)}, u32[]{:S(2)}) %collective-permute-start.2) | collective-permute-done | bytes 262176 | tf_op jit(solution)/shard_map/ppermute | solution.py:60
  26.2 0.0 collective-permute-done.4
  26.2 1.2 %collective-permute-done.3 = bf16[128,1024]{1,0:T(8,128)(2,1)S(1)} collective-permute-done((bf16[128,1024]{1,0:T(8,128)(2,1)S(1)}, bf16[128,1024]{1,0:T(8,128)(2,1)S(1)}, u32[]{:S(2)}, u32[]{:S(2)}) %collective-permute-start.3) | collective-permute-done | bytes 262176 | tf_op jit(solution)/shard_map/ppermute | solution.py:60
  27.4 0.2 fusion.2
  27.6 22.4 %all_to_all.10 = bf16[16,8,1024]{2,1,0:T(8,128)(2,1)S(1)} all-to-all(bf16[16,8,1024]{2,1,0:T(8,128)(2,1)S(1)} %fusion.2), channel_id=1, replica_groups={{0,4,8,12,16,20,24,28,32,36,40,44,48,52,56,60},{64,68,72,76,80,84,88,92..., dimensions={0} | all-to-all | bytes 524288 | tf_op jit(solution)/shard_map/all_to_all | solution.py:64
  50.0 0.0 copy-done
  50.1 0.1 collective-permute-start.5
  50.2 1.1 %collective-permute-done.5 = f32[24,128]{1,0:T(8,128)S(1)} collective-permute-done((f32[24,128]{1,0:T(8,128)S(1)}, f32[24,128]{1,0:T(8,128)S(1)}, u32[]{:S(2)}, u32[]{:S(2)}) %collective-permute-start.5) | collective-permute-done | bytes 12320 | tf_op jit(solution)/shard_map/ppermute | solution.py:119
  51.3 2.1 %collective-permute-start.6 = (f32[24,128]{1,0:T(8,128)S(1)}, f32[24,128]{1,0:T(8,128)S(1)}, u32[]{:S(2)}, u32[]{:S(2)}) collective-permute-start(f32[24,128]{1,0:T(8,128)S(1)} %add.128), channel_id=1, source_target_pairs={{0,2},{1,3},{2,0},{3,1},{4,6},{5,7},{6,4},{7,5},{8,10},{9,11},{10,... | collective-permute-start | bytes 36872 | tf_op jit(solution)/shard_map/ppermute | solution.py:119
  53.5 1.9 %collective-permute-done.6 = f32[24,128]{1,0:T(8,128)S(1)} collective-permute-done((f32[24,128]{1,0:T(8,128)S(1)}, f32[24,128]{1,0:T(8,128)S(1)}, u32[]{:S(2)}, u32[]{:S(2)}) %collective-permute-start.6) | collective-permute-done | bytes 12320 | tf_op jit(solution)/shard_map/ppermute | solution.py:119
  55.4 0.1 share.1
  55.5 16.6 %all_to_all.11 = bf16[16,8,1024]{2,1,0:T(8,128)(2,1)S(1)} all-to-all(bf16[16,8,1024]{2,1,0:T(8,128)(2,1)S(1)} %bitcast.37), channel_id=1, replica_groups={{0,4,8,12,16,20,24,28,32,36,40,44,48,52,56,60},{64,68,72,76,80,84,88,92..., dimensions={0} | all-to-all | bytes 524288 | tf_op jit(solution)/shard_map/all_to_all | solution.py:64
  72.1 1.7 %collective-permute-start.9 = (bf16[128,1024]{1,0:T(8,128)(2,1)S(1)}, bf16[128,1024]{1,0:T(8,128)(2,1)S(1)}, u32[]{:S(2)}, u32[]{:S(2)}) collective-permute-start(bf16[128,1024]{1,0:T(8,128)(2,1)S(1)} %bitcast.40), channel_id=1, source_target_pairs={{0,192},{1,13},{2,194},{3,15},{4,196},{5,9},{6,198},{7,11},{8,200}... | collective-permute-start | bytes 786440 | tf_op jit(solution)/shard_map/ppermute | solution.py:60
  73.8 1.1 %collective-permute-start.8 = (bf16[128,1024]{1,0:T(8,128)(2,1)S(1)}, bf16[128,1024]{1,0:T(8,128)(2,1)S(1)}, u32[]{:S(2)}, u32[]{:S(2)}) collective-permute-start(bf16[128,1024]{1,0:T(8,128)(2,1)S(1)} %bitcast.41), channel_id=1, source_target_pairs={{0,128},{1,5},{2,130},{3,7},{4,132},{5,1},{6,134},{7,3},{8,136},{9... | collective-permute-start | bytes 786440 | tf_op jit(solution)/shard_map/ppermute | solution.py:60
  74.9 0.0 collective-permute-start.7
  74.9 3.0 %probs.1 = (f32[2048,1024]{1,0:T(8,128)S(1)}, bf16[2048,512]{1,0:T(8,128)(2,1)S(1)}) custom-call(bf16[2048,1024]{1,0:T(8,128)(2,1)} %x_hbm.5, bf16[2048,512]{1,0:T(8,128)(2,1)} %e_hbm.3, f32[8,256]{1,0:T(8,128)S(1)} %log_add_fusion.log_ref), custom_call_target="tpu_custom_call" | custom-call | flops 8388608 | bytes 8388608 | tf_op jit(solution)/shard_map/probs/pallas_call | solution.py:358
  77.9 0.5 collective-permute-done.9
  78.3 3.0 %collective-permute-done.8 = bf16[128,1024]{1,0:T(8,128)(2,1)S(1)} collective-permute-done((bf16[128,1024]{1,0:T(8,128)(2,1)S(1)}, bf16[128,1024]{1,0:T(8,128)(2,1)S(1)}, u32[]{:S(2)}, u32[]{:S(2)}) %collective-permute-start.8) | collective-permute-done | bytes 262176 | tf_op jit(solution)/shard_map/ppermute | solution.py:60
  81.3 0.0 collective-permute-done.7
  81.3 0.1 select_bitcast_fusion.3
  81.5 0.1 pad_maximum_fusion
  81.6 0.1 copy.6
  81.7 0.2 bitcast_select_fusion.d_ref
  82.0 2.7 %backward.1 = (f32[2048,1024]{1,0:T(8,128)S(1)}, f32[8,256]{1,0:T(8,128)S(1)}) custom-call(f32[2048,1024]{1,0:T(8,128)S(1)} %get-tuple-element.16.probs_ref, bf16[2048,512]{1,0:T(8,128)(2,1)S(1)} %get-tuple-element.17.e_ref, bf16[512,1024]{1,0:T(8,128)(2,1)S(1)} %bitcast_select_fusion.d_ref), custom_call_target="tpu_custom_call" | custom-call | flops 2147483648 | bytes 8388608 | tf_op jit(solution)/shard_map/backward/pallas_call | solution.py:398
  84.6 3.8 %collective-permute-start.10 = (f32[8,256]{1,0:T(8,128)S(1)}, f32[8,256]{1,0:T(8,128)S(1)}, u32[]{:S(2)}, u32[]{:S(2)}) collective-permute-start(f32[8,256]{1,0:T(8,128)S(1)} %get-tuple-element.20), channel_id=1, source_target_pairs={{0,1},{1,0},{2,3},{3,2},{4,5},{5,4},{6,7},{7,6},{8,9},{9,8},{10,11... | collective-permute-start | bytes 24584 | tf_op jit(solution)/shard_map/ppermute | solution.py:119
  88.4 0.8 collective-permute-done.10
  89.2 1.9 %collective-permute-start.11 = (f32[8,256]{1,0:T(8,128)S(1)}, f32[8,256]{1,0:T(8,128)S(1)}, u32[]{:S(2)}, u32[]{:S(2)}) collective-permute-start(f32[8,256]{1,0:T(8,128)S(1)} %add.134), channel_id=1, source_target_pairs={{0,2},{1,3},{2,0},{3,1},{4,6},{5,7},{6,4},{7,5},{8,10},{9,11},{10,... | collective-permute-start | bytes 24584 | tf_op jit(solution)/shard_map/ppermute | solution.py:119
  91.1 0.6 slice_reduce_fusion
  91.7 1.5 %collective-permute-done.11 = f32[8,256]{1,0:T(8,128)S(1)} collective-permute-done((f32[8,256]{1,0:T(8,128)S(1)}, f32[8,256]{1,0:T(8,128)S(1)}, u32[]{:S(2)}, u32[]{:S(2)}) %collective-permute-start.11) | collective-permute-done | bytes 8224 | tf_op jit(solution)/shard_map/ppermute | solution.py:119
  93.2 2.5 %gradient.1 = bf16[2048,1024]{1,0:T(8,128)(2,1)} custom-call(f32[2048,1024]{1,0:T(8,128)S(1)} %get-tuple-element.16.probs_ref, f32[2048,1024]{1,0:T(8,128)S(1)} %get-tuple-element.19.dprobs_ref, f32[8,256]{1,0:T(8,128)S(1)} %add.135.dot_ref), custom_call_target="tpu_custom_call" | custom-call | flops 6291456 | bytes 8388608 | tf_op jit(solution)/shard_map/gradient/pallas_call | solution.py:415
  (7 shorter events, 0.1 us)
Async XLA Ops:
  4.0 4.2 %collective-permute-start = (f32[8,256]{1,0:T(8,128)S(1)}, f32[8,256]{1,0:T(8,128)S(1)}, u32[]{:S(2)}, u32[]{:S(2)}) collective-permute-start(f32[8,256]{1,0:T(8,128)S(1)} %stats.1), channel_id=1, source_target_pairs={{0,1},{1,0},{2,3},{3,2},{4,5},{5,4},{6,7},{7,6},{8,9},{9,8},{10,11... | collective-permute-start | bytes 24584 | tf_op jit(solution)/shard_map/ppermute | solution.py:119
  8.2 4.1 %collective-permute-start.1 = (f32[8,256]{1,0:T(8,128)S(1)}, f32[8,256]{1,0:T(8,128)S(1)}, u32[]{:S(2)}, u32[]{:S(2)}) collective-permute-start(f32[8,256]{1,0:T(8,128)S(1)} %log_add_fusion.1), channel_id=1, source_target_pairs={{0,2},{1,3},{2,0},{3,1},{4,6},{5,7},{6,4},{7,5},{8,10},{9,11},{10,... | collective-permute-start | bytes 24584 | tf_op jit(solution)/shard_map/ppermute | solution.py:119
  17.5 32.5 %copy-start = (f32[8,1024]{1,0:T(8,128)S(1)}, f32[8,1024]{1,0:T(8,128)}, u32[]{:S(2)}) copy-start(f32[8,1024]{1,0:T(8,128)} %measured_ref.3) | copy-start | bytes 98308
  17.8 8.4 %collective-permute-start.2 = (bf16[128,1024]{1,0:T(8,128)(2,1)S(1)}, bf16[128,1024]{1,0:T(8,128)(2,1)S(1)}, u32[]{:S(2)}, u32[]{:S(2)}) collective-permute-start(bf16[128,1024]{1,0:T(8,128)(2,1)S(1)} %get-tuple-element.26), channel_id=1, source_target_pairs={{0,128},{1,5},{2,130},{3,7},{4,132},{5,1},{6,134},{7,3},{8,136},{9... | collective-permute-start | bytes 786440 | tf_op jit(solution)/shard_map/ppermute | solution.py:60
  17.9 8.3 %collective-permute-start.4 = (bf16[128,1024]{1,0:T(8,128)(2,1)S(1)}, bf16[128,1024]{1,0:T(8,128)(2,1)S(1)}, u32[]{:S(2)}, u32[]{:S(2)}) collective-permute-start(bf16[128,1024]{1,0:T(8,128)(2,1)S(1)} %get-tuple-element.27), channel_id=1, source_target_pairs={{0,192},{1,13},{2,194},{3,15},{4,196},{5,9},{6,198},{7,11},{8,200}... | collective-permute-start | bytes 786440 | tf_op jit(solution)/shard_map/ppermute | solution.py:60
  19.8 7.6 %collective-permute-start.3 = (bf16[128,1024]{1,0:T(8,128)(2,1)S(1)}, bf16[128,1024]{1,0:T(8,128)(2,1)S(1)}, u32[]{:S(2)}, u32[]{:S(2)}) collective-permute-start(bf16[128,1024]{1,0:T(8,128)(2,1)S(1)} %get-tuple-element.28), channel_id=1, source_target_pairs={{0,64},{1,9},{2,66},{3,11},{4,68},{5,13},{6,70},{7,15},{8,72},{9,1... | collective-permute-start | bytes 786440 | tf_op jit(solution)/shard_map/ppermute | solution.py:60
  50.1 1.3 %collective-permute-start.5 = (f32[24,128]{1,0:T(8,128)S(1)}, f32[24,128]{1,0:T(8,128)S(1)}, u32[]{:S(2)}, u32[]{:S(2)}) collective-permute-start(f32[24,128]{1,0:T(8,128)S(1)} %get-tuple-element.12), channel_id=1, source_target_pairs={{0,1},{1,0},{2,3},{3,2},{4,5},{5,4},{6,7},{7,6},{8,9},{9,8},{10,11... | collective-permute-start | bytes 36872 | tf_op jit(solution)/shard_map/ppermute | solution.py:119
  51.3 4.0 %collective-permute-start.6 = (f32[24,128]{1,0:T(8,128)S(1)}, f32[24,128]{1,0:T(8,128)S(1)}, u32[]{:S(2)}, u32[]{:S(2)}) collective-permute-start(f32[24,128]{1,0:T(8,128)S(1)} %add.128), channel_id=1, source_target_pairs={{0,2},{1,3},{2,0},{3,1},{4,6},{5,7},{6,4},{7,5},{8,10},{9,11},{10,... | collective-permute-start | bytes 36872 | tf_op jit(solution)/shard_map/ppermute | solution.py:119
  72.1 6.2 %collective-permute-start.9 = (bf16[128,1024]{1,0:T(8,128)(2,1)S(1)}, bf16[128,1024]{1,0:T(8,128)(2,1)S(1)}, u32[]{:S(2)}, u32[]{:S(2)}) collective-permute-start(bf16[128,1024]{1,0:T(8,128)(2,1)S(1)} %bitcast.40), channel_id=1, source_target_pairs={{0,192},{1,13},{2,194},{3,15},{4,196},{5,9},{6,198},{7,11},{8,200}... | collective-permute-start | bytes 786440 | tf_op jit(solution)/shard_map/ppermute | solution.py:60
  73.8 7.5 %collective-permute-start.8 = (bf16[128,1024]{1,0:T(8,128)(2,1)S(1)}, bf16[128,1024]{1,0:T(8,128)(2,1)S(1)}, u32[]{:S(2)}, u32[]{:S(2)}) collective-permute-start(bf16[128,1024]{1,0:T(8,128)(2,1)S(1)} %bitcast.41), channel_id=1, source_target_pairs={{0,128},{1,5},{2,130},{3,7},{4,132},{5,1},{6,134},{7,3},{8,136},{9... | collective-permute-start | bytes 786440 | tf_op jit(solution)/shard_map/ppermute | solution.py:60
  74.9 6.4 %collective-permute-start.7 = (bf16[128,1024]{1,0:T(8,128)(2,1)S(1)}, bf16[128,1024]{1,0:T(8,128)(2,1)S(1)}, u32[]{:S(2)}, u32[]{:S(2)}) collective-permute-start(bf16[128,1024]{1,0:T(8,128)(2,1)S(1)} %bitcast.42), channel_id=1, source_target_pairs={{0,64},{1,9},{2,66},{3,11},{4,68},{5,13},{6,70},{7,15},{8,72},{9,1... | collective-permute-start | bytes 786440 | tf_op jit(solution)/shard_map/ppermute | solution.py:60
  84.6 4.6 %collective-permute-start.10 = (f32[8,256]{1,0:T(8,128)S(1)}, f32[8,256]{1,0:T(8,128)S(1)}, u32[]{:S(2)}, u32[]{:S(2)}) collective-permute-start(f32[8,256]{1,0:T(8,128)S(1)} %get-tuple-element.20), channel_id=1, source_target_pairs={{0,1},{1,0},{2,3},{3,2},{4,5},{5,4},{6,7},{7,6},{8,9},{9,8},{10,11... | collective-permute-start | bytes 24584 | tf_op jit(solution)/shard_map/ppermute | solution.py:119
  89.2 4.0 %collective-permute-start.11 = (f32[8,256]{1,0:T(8,128)S(1)}, f32[8,256]{1,0:T(8,128)S(1)}, u32[]{:S(2)}, u32[]{:S(2)}) collective-permute-start(f32[8,256]{1,0:T(8,128)S(1)} %add.134), channel_id=1, source_target_pairs={{0,2},{1,3},{2,0},{3,1},{4,6},{5,7},{6,4},{7,5},{8,10},{9,11},{10,... | collective-permute-start | bytes 24584 | tf_op jit(solution)/shard_map/ppermute | solution.py:119

commit v10 on v9

--- a/solution.py
+++ b/solution.py
@@ -213,31 +213,37 @@
     expression.wait()
 
 
-def forward_kernel(x_hbm, et_ref, log_ref, part_ref, x_ref, low, sems):
+def forward_kernel(size, x_hbm, et_ref, log_ref, part_ref, x_ref, low, acc, sems):
     cells, spots = x_ref.shape
-    steps = cells // ROWS
+    inner = size // ROWS
 
     def copy(i):
         return pltpu.make_async_copy(x_hbm.at[block(i), :], x_ref.at[block(i), :], sems.at[i])
 
-    for i in range(steps):
+    for i in range(cells // ROWS):
         copy(i).start()
 
-    def fill(i):
-        log_total = as_column(log_ref[pl.ds(i, 1), :])
-        for g in lane_groups(spots):
-            probs = jnp.exp(x_ref[block(i), g].astype(jnp.float32) - log_total)
-            low[block(i), g] = probs.astype(jnp.bfloat16)
-
-    @pl.loop(0, steps // 2)
-    def _(i):
-        copy(2 * i).wait()
-        copy(2 * i + 1).wait()
-        fill(2 * i)
-        fill(2 * i + 1)
-
-    part = jnp.dot(et_ref[...], low[...], preferred_element_type=jnp.float32)
-    part_ref[...] = part.astype(jnp.bfloat16)
+    def fill(step):
+        for i in range(step * inner, (step + 1) * inner):
+            copy(i).wait()
+        for i in range(step * inner, (step + 1) * inner):
+            rows = slice(i * ROWS, (i + 1) * ROWS)
+            log_total = as_column(log_ref[i : i + 1, :])
+            for g in lane_groups(spots):
+                probs = jnp.exp(x_ref[rows, g].astype(jnp.float32) - log_total)
+                low[rows, g] = probs.astype(jnp.bfloat16)
+
+    def partial(step):
+        rows = slice(step * size, (step + 1) * size)
+        return jnp.dot(et_ref[:, rows], low[rows, :], preferred_element_type=jnp.float32)
+
+    steps = cells // size
+    fill(0)
+    for step in range(steps - 1):
+        fill(step + 1)
+        part = partial(step)
+        acc[...] = part if step == 0 else acc[...] + part
+    part_ref[...] = (acc[...] + partial(steps - 1)).astype(jnp.bfloat16)
 
 
 def backward_kernel(size, probs_ref, e_ref, d_ref, dprobs_ref, dot_ref):
@@ -377,13 +383,14 @@
     cells, spots = logits.shape
     genes = expression_t.shape[0]
     return pl.pallas_call(
-        forward_kernel,
+        functools.partial(forward_kernel, 512),
         in_specs=[HBM, VMEM, VMEM],
         out_specs=VMEM,
         out_shape=jax.ShapeDtypeStruct((genes, spots), jnp.bfloat16),
         scratch_shapes=[
             pltpu.VMEM((cells, spots), jnp.bfloat16),
             pltpu.VMEM((cells, spots), jnp.bfloat16),
+            pltpu.VMEM((genes, spots), jnp.float32),
             pltpu.SemaphoreType.DMA((cells // ROWS,)),
         ],
         compiler_params=params(16),

time: 96.1 us -> 95.6 us (level)
  no operation moved by 1% of the time
where the time goes in v10:
time: 95.6 us; the launch traced here: 95.4 us
  blocking collectives  39 us (41%)
  Pallas kernels  18.4 us (19%)
  starting transfers between devices  17.8 us (19%)
  waiting for transfers between devices  17.5 us (18%)
    all_to_all x2, blocking collectives, swap_second(): return lax.all_to_all(v, ('wide', 'narrow'), 0, 0, axis_index_groups=SECOND)  39 us
    ppermute x6, starting transfers between devices, narrow_combine(): v = op(v, lax.ppermute(v, 'narrow', [(i, i ^ d) for i in range(4)]))  12.3 us
    ppermute x6, waiting for transfers between devices, send_first(): return lax.ppermute(v, ('wide', 'narrow'), FIRST[k])  10.4 us
    ppermute x6, waiting for transfers between devices, narrow_combine(): v = op(v, lax.ppermute(v, 'narrow', [(i, i ^ d) for i in range(4)]))  7.17 us
    ppermute x6, starting transfers between devices, send_first(): return lax.ppermute(v, ('wide', 'narrow'), FIRST[k])  5.54 us
    pallas_call x1, Pallas kernels, partial_predicted(): pl.pallas_call(functools.partial(forward_kernel, 512), in_specs=[HBM, VME...  4.66 us
    pallas_call x1, Pallas kernels, local_log_sum(): pl.pallas_call(stats_kernel, in_specs=[HBM], out_specs=VMEM, out_shape=ja...  3.37 us
    pallas_call x1, Pallas kernels, probabilities(): pl.pallas_call(probs_kernel, in_specs=[HBM, HBM, VMEM], out_specs=[VMEM,...  2.96 us
  transfers between devices with their start and end apart: 12, of which 10 were waited for; matrix products, arithmetic and copies ran while one was open for 1% of the time, Pallas kernels for 5%

profile of v10, /device:TPU:1, one launch (start us, length us, event | category | flops | bytes accessed | tf_op | source)
XLA Modules:
  0.0 95.4 jit_solution(8790269105969723600)
XLA Ops:
  0.6 3.4 %stats.1 = f32[8,256]{1,0:T(8,128)S(1)} custom-call(bf16[2048,1024]{1,0:T(8,128)(2,1)} %x_hbm.5), custom_call_target="tpu_custom_call" | custom-call | flops 12582912 | bytes 4194304 | tf_op jit(solution)/shard_map/stats/pallas_call | solution.py:329
  4.0 3.3 %collective-permute-start = (f32[8,256]{1,0:T(8,128)S(1)}, f32[8,256]{1,0:T(8,128)S(1)}, u32[]{:S(2)}, u32[]{:S(2)}) collective-permute-start(f32[8,256]{1,0:T(8,128)S(1)} %stats.1), channel_id=1, source_target_pairs={{0,1},{1,0},{2,3},{3,2},{4,5},{5,4},{6,7},{7,6},{8,9},{9,8},{10,11... | collective-permute-start | bytes 24584 | tf_op jit(solution)/shard_map/ppermute | solution.py:119
  7.3 0.8 collective-permute-done
  8.2 1.1 %collective-permute-start.1 = (f32[8,256]{1,0:T(8,128)S(1)}, f32[8,256]{1,0:T(8,128)S(1)}, u32[]{:S(2)}, u32[]{:S(2)}) collective-permute-start(f32[8,256]{1,0:T(8,128)S(1)} %log_add_fusion.1), channel_id=1, source_target_pairs={{0,2},{1,3},{2,0},{3,1},{4,6},{5,7},{6,4},{7,5},{8,10},{9,11},{10,... | collective-permute-start | bytes 24584 | tf_op jit(solution)/shard_map/ppermute | solution.py:119
  9.3 2.0 %transpose.21.et_ref = bf16[512,2048]{1,0:T(8,128)(2,1)S(1)} custom-call(bf16[2048,512]{1,0:T(8,128)(2,1)} %e_hbm.3), custom_call_target="tpu_custom_call" | custom-call | bytes 4194304 | tf_op jit(solution)/shard_map/transpose/pallas_call | solution.py:346
  11.3 0.9 collective-permute-done.1
  12.3 4.7 %forward.1 = bf16[512,1024]{1,0:T(8,128)(2,1)S(1)} custom-call(bf16[2048,1024]{1,0:T(8,128)(2,1)} %x_hbm.5, bf16[512,2048]{1,0:T(8,128)(2,1)S(1)} %transpose.21.et_ref, f32[8,256]{1,0:T(8,128)S(1)} %log_add_fusion.log_ref), custom_call_target="tpu_custom_call" | custom-call | flops 2147483648 | bytes 8388608 | tf_op jit(solution)/shard_map/forward/pallas_call | solution.py:385
  17.0 0.0 copy-start
  17.0 0.1 copy.5
  17.1 0.1 broadcast_select_fusion
  17.2 0.1 dynamic-slice_bitcast_fusion.2
  17.2 0.1 collective-permute-start.2
  17.3 1.9 %collective-permute-start.4 = (bf16[128,1024]{1,0:T(8,128)(2,1)S(1)}, bf16[128,1024]{1,0:T(8,128)(2,1)S(1)}, u32[]{:S(2)}, u32[]{:S(2)}) collective-permute-start(bf16[128,1024]{1,0:T(8,128)(2,1)S(1)} %get-tuple-element.27), channel_id=1, source_target_pairs={{0,192},{1,13},{2,194},{3,15},{4,196},{5,9},{6,198},{7,11},{8,200}... | collective-permute-start | bytes 786440 | tf_op jit(solution)/shard_map/ppermute | solution.py:60
  19.2 0.7 collective-permute-start.3
  20.0 5.7 %collective-permute-done.2 = bf16[128,1024]{1,0:T(8,128)(2,1)S(1)} collective-permute-done((bf16[128,1024]{1,0:T(8,128)(2,1)S(1)}, bf16[128,1024]{1,0:T(8,128)(2,1)S(1)}, u32[]{:S(2)}, u32[]{:S(2)}) %collective-permute-start.2) | collective-permute-done | bytes 262176 | tf_op jit(solution)/shard_map/ppermute | solution.py:60
  25.7 0.0 collective-permute-done.4
  25.7 1.2 %collective-permute-done.3 = bf16[128,1024]{1,0:T(8,128)(2,1)S(1)} collective-permute-done((bf16[128,1024]{1,0:T(8,128)(2,1)S(1)}, bf16[128,1024]{1,0:T(8,128)(2,1)S(1)}, u32[]{:S(2)}, u32[]{:S(2)}) %collective-permute-start.3) | collective-permute-done | bytes 262176 | tf_op jit(solution)/shard_map/ppermute | solution.py:60
  26.9 0.2 fusion.2
  27.1 22.4 %all_to_all.10 = bf16[16,8,1024]{2,1,0:T(8,128)(2,1)S(1)} all-to-all(bf16[16,8,1024]{2,1,0:T(8,128)(2,1)S(1)} %fusion.2), channel_id=1, replica_groups={{0,4,8,12,16,20,24,28,32,36,40,44,48,52,56,60},{64,68,72,76,80,84,88,92..., dimensions={0} | all-to-all | bytes 524288 | tf_op jit(solution)/shard_map/all_to_all | solution.py:64
  49.5 0.0 copy-done
  49.5 0.1 collective-permute-start.5
  49.6 1.2 %collective-permute-done.5 = f32[24,128]{1,0:T(8,128)S(1)} collective-permute-done((f32[24,128]{1,0:T(8,128)S(1)}, f32[24,128]{1,0:T(8,128)S(1)}, u32[]{:S(2)}, u32[]{:S(2)}) %collective-permute-start.5) | collective-permute-done | bytes 12320 | tf_op jit(solution)/shard_map/ppermute | solution.py:119
  50.8 2.1 %collective-permute-start.6 = (f32[24,128]{1,0:T(8,128)S(1)}, f32[24,128]{1,0:T(8,128)S(1)}, u32[]{:S(2)}, u32[]{:S(2)}) collective-permute-start(f32[24,128]{1,0:T(8,128)S(1)} %add.128), channel_id=1, source_target_pairs={{0,2},{1,3},{2,0},{3,1},{4,6},{5,7},{6,4},{7,5},{8,10},{9,11},{10,... | collective-permute-start | bytes 36872 | tf_op jit(solution)/shard_map/ppermute | solution.py:119
  52.9 1.9 %collective-permute-done.6 = f32[24,128]{1,0:T(8,128)S(1)} collective-permute-done((f32[24,128]{1,0:T(8,128)S(1)}, f32[24,128]{1,0:T(8,128)S(1)}, u32[]{:S(2)}, u32[]{:S(2)}) %collective-permute-start.6) | collective-permute-done | bytes 12320 | tf_op jit(solution)/shard_map/ppermute | solution.py:119
  54.9 0.1 share.1
  55.0 16.6 %all_to_all.11 = bf16[16,8,1024]{2,1,0:T(8,128)(2,1)S(1)} all-to-all(bf16[16,8,1024]{2,1,0:T(8,128)(2,1)S(1)} %bitcast.37), channel_id=1, replica_groups={{0,4,8,12,16,20,24,28,32,36,40,44,48,52,56,60},{64,68,72,76,80,84,88,92..., dimensions={0} | all-to-all | bytes 524288 | tf_op jit(solution)/shard_map/all_to_all | solution.py:64
  71.5 1.7 %collective-permute-start.9 = (bf16[128,1024]{1,0:T(8,128)(2,1)S(1)}, bf16[128,1024]{1,0:T(8,128)(2,1)S(1)}, u32[]{:S(2)}, u32[]{:S(2)}) collective-permute-start(bf16[128,1024]{1,0:T(8,128)(2,1)S(1)} %bitcast.40), channel_id=1, source_target_pairs={{0,192},{1,13},{2,194},{3,15},{4,196},{5,9},{6,198},{7,11},{8,200}... | collective-permute-start | bytes 786440 | tf_op jit(solution)/shard_map/ppermute | solution.py:60
  73.3 1.1 %collective-permute-start.8 = (bf16[128,1024]{1,0:T(8,128)(2,1)S(1)}, bf16[128,1024]{1,0:T(8,128)(2,1)S(1)}, u32[]{:S(2)}, u32[]{:S(2)}) collective-permute-start(bf16[128,1024]{1,0:T(8,128)(2,1)S(1)} %bitcast.41), channel_id=1, source_target_pairs={{0,128},{1,5},{2,130},{3,7},{4,132},{5,1},{6,134},{7,3},{8,136},{9... | collective-permute-start | bytes 786440 | tf_op jit(solution)/shard_map/ppermute | solution.py:60
  74.4 0.0 collective-permute-start.7
  74.4 3.0 %probs.1 = (f32[2048,1024]{1,0:T(8,128)S(1)}, bf16[2048,512]{1,0:T(8,128)(2,1)S(1)}) custom-call(bf16[2048,1024]{1,0:T(8,128)(2,1)} %x_hbm.5, bf16[2048,512]{1,0:T(8,128)(2,1)} %e_hbm.3, f32[8,256]{1,0:T(8,128)S(1)} %log_add_fusion.log_ref), custom_call_target="tpu_custom_call" | custom-call | flops 8388608 | bytes 8388608 | tf_op jit(solution)/shard_map/probs/pallas_call | solution.py:364
  77.3 0.5 collective-permute-done.9
  77.8 3.0 %collective-permute-done.8 = bf16[128,1024]{1,0:T(8,128)(2,1)S(1)} collective-permute-done((bf16[128,1024]{1,0:T(8,128)(2,1)S(1)}, bf16[128,1024]{1,0:T(8,128)(2,1)S(1)}, u32[]{:S(2)}, u32[]{:S(2)}) %collective-permute-start.8) | collective-permute-done | bytes 262176 | tf_op jit(solution)/shard_map/ppermute | solution.py:60
  80.8 0.0 collective-permute-done.7
  80.8 0.1 select_bitcast_fusion.3
  80.9 0.1 pad_maximum_fusion
  81.0 0.1 copy.6
  81.1 0.2 bitcast_select_fusion.d_ref
  81.4 2.7 %backward.1 = (f32[2048,1024]{1,0:T(8,128)S(1)}, f32[8,256]{1,0:T(8,128)S(1)}) custom-call(f32[2048,1024]{1,0:T(8,128)S(1)} %get-tuple-element.16.probs_ref, bf16[2048,512]{1,0:T(8,128)(2,1)S(1)} %get-tuple-element.17.e_ref, bf16[512,1024]{1,0:T(8,128)(2,1)S(1)} %bitcast_select_fusion.d_ref), custom_call_target="tpu_custom_call" | custom-call | flops 2147483648 | bytes 8388608 | tf_op jit(solution)/shard_map/backward/pallas_call | solution.py:405
  84.1 3.8 %collective-permute-start.10 = (f32[8,256]{1,0:T(8,128)S(1)}, f32[8,256]{1,0:T(8,128)S(1)}, u32[]{:S(2)}, u32[]{:S(2)}) collective-permute-start(f32[8,256]{1,0:T(8,128)S(1)} %get-tuple-element.20), channel_id=1, source_target_pairs={{0,1},{1,0},{2,3},{3,2},{4,5},{5,4},{6,7},{7,6},{8,9},{9,8},{10,11... | collective-permute-start | bytes 24584 | tf_op jit(solution)/shard_map/ppermute | solution.py:119
  87.8 0.8 collective-permute-done.10
  88.7 1.9 %collective-permute-start.11 = (f32[8,256]{1,0:T(8,128)S(1)}, f32[8,256]{1,0:T(8,128)S(1)}, u32[]{:S(2)}, u32[]{:S(2)}) collective-permute-start(f32[8,256]{1,0:T(8,128)S(1)} %add.134), channel_id=1, source_target_pairs={{0,2},{1,3},{2,0},{3,1},{4,6},{5,7},{6,4},{7,5},{8,10},{9,11},{10,... | collective-permute-start | bytes 24584 | tf_op jit(solution)/shard_map/ppermute | solution.py:119
  90.5 0.6 slice_reduce_fusion
  91.2 1.5 %collective-permute-done.11 = f32[8,256]{1,0:T(8,128)S(1)} collective-permute-done((f32[8,256]{1,0:T(8,128)S(1)}, f32[8,256]{1,0:T(8,128)S(1)}, u32[]{:S(2)}, u32[]{:S(2)}) %collective-permute-start.11) | collective-permute-done | bytes 8224 | tf_op jit(solution)/shard_map/ppermute | solution.py:119
  92.7 2.5 %gradient.1 = bf16[2048,1024]{1,0:T(8,128)(2,1)} custom-call(f32[2048,1024]{1,0:T(8,128)S(1)} %get-tuple-element.16.probs_ref, f32[2048,1024]{1,0:T(8,128)S(1)} %get-tuple-element.19.dprobs_ref, f32[8,256]{1,0:T(8,128)S(1)} %add.135.dot_ref), custom_call_target="tpu_custom_call" | custom-call | flops 6291456 | bytes 8388608 | tf_op jit(solution)/shard_map/gradient/pallas_call | solution.py:422
  (7 shorter events, 0.1 us)
Async XLA Ops:
  4.0 4.2 %collective-permute-start = (f32[8,256]{1,0:T(8,128)S(1)}, f32[8,256]{1,0:T(8,128)S(1)}, u32[]{:S(2)}, u32[]{:S(2)}) collective-permute-start(f32[8,256]{1,0:T(8,128)S(1)} %stats.1), channel_id=1, source_target_pairs={{0,1},{1,0},{2,3},{3,2},{4,5},{5,4},{6,7},{7,6},{8,9},{9,8},{10,11... | collective-permute-start | bytes 24584 | tf_op jit(solution)/shard_map/ppermute | solution.py:119
  8.2 4.1 %collective-permute-start.1 = (f32[8,256]{1,0:T(8,128)S(1)}, f32[8,256]{1,0:T(8,128)S(1)}, u32[]{:S(2)}, u32[]{:S(2)}) collective-permute-start(f32[8,256]{1,0:T(8,128)S(1)} %log_add_fusion.1), channel_id=1, source_target_pairs={{0,2},{1,3},{2,0},{3,1},{4,6},{5,7},{6,4},{7,5},{8,10},{9,11},{10,... | collective-permute-start | bytes 24584 | tf_op jit(solution)/shard_map/ppermute | solution.py:119
  17.0 32.5 %copy-start = (f32[8,1024]{1,0:T(8,128)S(1)}, f32[8,1024]{1,0:T(8,128)}, u32[]{:S(2)}) copy-start(f32[8,1024]{1,0:T(8,128)} %measured_ref.3) | copy-start | bytes 98308
  17.2 8.4 %collective-permute-start.2 = (bf16[128,1024]{1,0:T(8,128)(2,1)S(1)}, bf16[128,1024]{1,0:T(8,128)(2,1)S(1)}, u32[]{:S(2)}, u32[]{:S(2)}) collective-permute-start(bf16[128,1024]{1,0:T(8,128)(2,1)S(1)} %get-tuple-element.26), channel_id=1, source_target_pairs={{0,128},{1,5},{2,130},{3,7},{4,132},{5,1},{6,134},{7,3},{8,136},{9... | collective-permute-start | bytes 786440 | tf_op jit(solution)/shard_map/ppermute | solution.py:60
  17.3 8.3 %collective-permute-start.4 = (bf16[128,1024]{1,0:T(8,128)(2,1)S(1)}, bf16[128,1024]{1,0:T(8,128)(2,1)S(1)}, u32[]{:S(2)}, u32[]{:S(2)}) collective-permute-start(bf16[128,1024]{1,0:T(8,128)(2,1)S(1)} %get-tuple-element.27), channel_id=1, source_target_pairs={{0,192},{1,13},{2,194},{3,15},{4,196},{5,9},{6,198},{7,11},{8,200}... | collective-permute-start | bytes 786440 | tf_op jit(solution)/shard_map/ppermute | solution.py:60
  19.2 7.6 %collective-permute-start.3 = (bf16[128,1024]{1,0:T(8,128)(2,1)S(1)}, bf16[128,1024]{1,0:T(8,128)(2,1)S(1)}, u32[]{:S(2)}, u32[]{:S(2)}) collective-permute-start(bf16[128,1024]{1,0:T(8,128)(2,1)S(1)} %get-tuple-element.28), channel_id=1, source_target_pairs={{0,64},{1,9},{2,66},{3,11},{4,68},{5,13},{6,70},{7,15},{8,72},{9,1... | collective-permute-start | bytes 786440 | tf_op jit(solution)/shard_map/ppermute | solution.py:60
  49.5 1.3 %collective-permute-start.5 = (f32[24,128]{1,0:T(8,128)S(1)}, f32[24,128]{1,0:T(8,128)S(1)}, u32[]{:S(2)}, u32[]{:S(2)}) collective-permute-start(f32[24,128]{1,0:T(8,128)S(1)} %get-tuple-element.12), channel_id=1, source_target_pairs={{0,1},{1,0},{2,3},{3,2},{4,5},{5,4},{6,7},{7,6},{8,9},{9,8},{10,11... | collective-permute-start | bytes 36872 | tf_op jit(solution)/shard_map/ppermute | solution.py:119
  50.8 4.0 %collective-permute-start.6 = (f32[24,128]{1,0:T(8,128)S(1)}, f32[24,128]{1,0:T(8,128)S(1)}, u32[]{:S(2)}, u32[]{:S(2)}) collective-permute-start(f32[24,128]{1,0:T(8,128)S(1)} %add.128), channel_id=1, source_target_pairs={{0,2},{1,3},{2,0},{3,1},{4,6},{5,7},{6,4},{7,5},{8,10},{9,11},{10,... | collective-permute-start | bytes 36872 | tf_op jit(solution)/shard_map/ppermute | solution.py:119
  71.5 6.2 %collective-permute-start.9 = (bf16[128,1024]{1,0:T(8,128)(2,1)S(1)}, bf16[128,1024]{1,0:T(8,128)(2,1)S(1)}, u32[]{:S(2)}, u32[]{:S(2)}) collective-permute-start(bf16[128,1024]{1,0:T(8,128)(2,1)S(1)} %bitcast.40), channel_id=1, source_target_pairs={{0,192},{1,13},{2,194},{3,15},{4,196},{5,9},{6,198},{7,11},{8,200}... | collective-permute-start | bytes 786440 | tf_op jit(solution)/shard_map/ppermute | solution.py:60
  73.3 7.5 %collective-permute-start.8 = (bf16[128,1024]{1,0:T(8,128)(2,1)S(1)}, bf16[128,1024]{1,0:T(8,128)(2,1)S(1)}, u32[]{:S(2)}, u32[]{:S(2)}) collective-permute-start(bf16[128,1024]{1,0:T(8,128)(2,1)S(1)} %bitcast.41), channel_id=1, source_target_pairs={{0,128},{1,5},{2,130},{3,7},{4,132},{5,1},{6,134},{7,3},{8,136},{9... | collective-permute-start | bytes 786440 | tf_op jit(solution)/shard_map/ppermute | solution.py:60
  74.4 6.4 %collective-permute-start.7 = (bf16[128,1024]{1,0:T(8,128)(2,1)S(1)}, bf16[128,1024]{1,0:T(8,128)(2,1)S(1)}, u32[]{:S(2)}, u32[]{:S(2)}) collective-permute-start(bf16[128,1024]{1,0:T(8,128)(2,1)S(1)} %bitcast.42), channel_id=1, source_target_pairs={{0,64},{1,9},{2,66},{3,11},{4,68},{5,13},{6,70},{7,15},{8,72},{9,1... | collective-permute-start | bytes 786440 | tf_op jit(solution)/shard_map/ppermute | solution.py:60
  84.1 4.6 %collective-permute-start.10 = (f32[8,256]{1,0:T(8,128)S(1)}, f32[8,256]{1,0:T(8,128)S(1)}, u32[]{:S(2)}, u32[]{:S(2)}) collective-permute-start(f32[8,256]{1,0:T(8,128)S(1)} %get-tuple-element.20), channel_id=1, source_target_pairs={{0,1},{1,0},{2,3},{3,2},{4,5},{5,4},{6,7},{7,6},{8,9},{9,8},{10,11... | collective-permute-start | bytes 24584 | tf_op jit(solution)/shard_map/ppermute | solution.py:119
  88.7 4.0 %collective-permute-start.11 = (f32[8,256]{1,0:T(8,128)S(1)}, f32[8,256]{1,0:T(8,128)S(1)}, u32[]{:S(2)}, u32[]{:S(2)}) collective-permute-start(f32[8,256]{1,0:T(8,128)S(1)} %add.134), channel_id=1, source_target_pairs={{0,2},{1,3},{2,0},{3,1},{4,6},{5,7},{6,4},{7,5},{8,10},{9,11},{10,... | collective-permute-start | bytes 24584 | tf_op jit(solution)/shard_map/ppermute | solution.py:119

commit v11 on v10

--- a/solution.py
+++ b/solution.py
@@ -383,7 +383,7 @@
     cells, spots = logits.shape
     genes = expression_t.shape[0]
     return pl.pallas_call(
-        functools.partial(forward_kernel, 512),
+        functools.partial(forward_kernel, 256),
         in_specs=[HBM, VMEM, VMEM],
         out_specs=VMEM,
         out_shape=jax.ShapeDtypeStruct((genes, spots), jnp.bfloat16),

time: 95.6 us -> 95.4 us (level)
  no operation moved by 1% of the time
where the time goes in v11:
time: 95.4 us; the launch traced here: 95.2 us
  blocking collectives  39 us (41%)
  Pallas kernels  18.2 us (19%)
  starting transfers between devices  17.8 us (19%)
  waiting for transfers between devices  17.6 us (18%)
    all_to_all x2, blocking collectives, swap_second(): return lax.all_to_all(v, ('wide', 'narrow'), 0, 0, axis_index_groups=SECOND)  39 us
    ppermute x6, starting transfers between devices, narrow_combine(): v = op(v, lax.ppermute(v, 'narrow', [(i, i ^ d) for i in range(4)]))  12.3 us
    ppermute x6, waiting for transfers between devices, send_first(): return lax.ppermute(v, ('wide', 'narrow'), FIRST[k])  10.4 us
    ppermute x6, waiting for transfers between devices, narrow_combine(): v = op(v, lax.ppermute(v, 'narrow', [(i, i ^ d) for i in range(4)]))  7.18 us
    ppermute x6, starting transfers between devices, send_first(): return lax.ppermute(v, ('wide', 'narrow'), FIRST[k])  5.51 us
    pallas_call x1, Pallas kernels, partial_predicted(): pl.pallas_call(functools.partial(forward_kernel, 256), in_specs=[HBM, VME...  4.49 us
    pallas_call x1, Pallas kernels, local_log_sum(): pl.pallas_call(stats_kernel, in_specs=[HBM], out_specs=VMEM, out_shape=ja...  3.37 us
    pallas_call x1, Pallas kernels, probabilities(): pl.pallas_call(probs_kernel, in_specs=[HBM, HBM, VMEM], out_specs=[VMEM,...  2.96 us
  transfers between devices with their start and end apart: 12, of which 10 were waited for; matrix products, arithmetic and copies ran while one was open for 1% of the time, Pallas kernels for 5%

profile of v11, /device:TPU:1, one launch (start us, length us, event | category | flops | bytes accessed | tf_op | source)
XLA Modules:
  0.0 95.2 jit_solution(14043484646749889768)
XLA Ops:
  0.6 3.4 %stats.1 = f32[8,256]{1,0:T(8,128)S(1)} custom-call(bf16[2048,1024]{1,0:T(8,128)(2,1)} %x_hbm.5), custom_call_target="tpu_custom_call" | custom-call | flops 12582912 | bytes 4194304 | tf_op jit(solution)/shard_map/stats/pallas_call | solution.py:329
  4.0 3.3 %collective-permute-start = (f32[8,256]{1,0:T(8,128)S(1)}, f32[8,256]{1,0:T(8,128)S(1)}, u32[]{:S(2)}, u32[]{:S(2)}) collective-permute-start(f32[8,256]{1,0:T(8,128)S(1)} %stats.1), channel_id=1, source_target_pairs={{0,1},{1,0},{2,3},{3,2},{4,5},{5,4},{6,7},{7,6},{8,9},{9,8},{10,11... | collective-permute-start | bytes 24584 | tf_op jit(solution)/shard_map/ppermute | solution.py:119
  7.3 0.8 collective-permute-done
  8.2 1.1 %collective-permute-start.1 = (f32[8,256]{1,0:T(8,128)S(1)}, f32[8,256]{1,0:T(8,128)S(1)}, u32[]{:S(2)}, u32[]{:S(2)}) collective-permute-start(f32[8,256]{1,0:T(8,128)S(1)} %log_add_fusion.1), channel_id=1, source_target_pairs={{0,2},{1,3},{2,0},{3,1},{4,6},{5,7},{6,4},{7,5},{8,10},{9,11},{10,... | collective-permute-start | bytes 24584 | tf_op jit(solution)/shard_map/ppermute | solution.py:119
  9.3 2.0 %transpose.21.et_ref = bf16[512,2048]{1,0:T(8,128)(2,1)S(1)} custom-call(bf16[2048,512]{1,0:T(8,128)(2,1)} %e_hbm.3), custom_call_target="tpu_custom_call" | custom-call | bytes 4194304 | tf_op jit(solution)/shard_map/transpose/pallas_call | solution.py:346
  11.3 0.9 collective-permute-done.1
  12.3 4.5 %forward.1 = bf16[512,1024]{1,0:T(8,128)(2,1)S(1)} custom-call(bf16[2048,1024]{1,0:T(8,128)(2,1)} %x_hbm.5, bf16[512,2048]{1,0:T(8,128)(2,1)S(1)} %transpose.21.et_ref, f32[8,256]{1,0:T(8,128)S(1)} %log_add_fusion.log_ref), custom_call_target="tpu_custom_call" | custom-call | flops 2147483648 | bytes 8388608 | tf_op jit(solution)/shard_map/forward/pallas_call | solution.py:385
  16.8 0.0 copy-start
  16.8 0.1 copy.5
  16.9 0.1 broadcast_select_fusion
  17.0 0.1 dynamic-slice_bitcast_fusion.2
  17.1 0.1 collective-permute-start.2
  17.2 1.9 %collective-permute-start.4 = (bf16[128,1024]{1,0:T(8,128)(2,1)S(1)}, bf16[128,1024]{1,0:T(8,128)(2,1)S(1)}, u32[]{:S(2)}, u32[]{:S(2)}) collective-permute-start(bf16[128,1024]{1,0:T(8,128)(2,1)S(1)} %get-tuple-element.27), channel_id=1, source_target_pairs={{0,192},{1,13},{2,194},{3,15},{4,196},{5,9},{6,198},{7,11},{8,200}... | collective-permute-start | bytes 786440 | tf_op jit(solution)/shard_map/ppermute | solution.py:60
  19.1 0.7 collective-permute-start.3
  19.8 5.7 %collective-permute-done.2 = bf16[128,1024]{1,0:T(8,128)(2,1)S(1)} collective-permute-done((bf16[128,1024]{1,0:T(8,128)(2,1)S(1)}, bf16[128,1024]{1,0:T(8,128)(2,1)S(1)}, u32[]{:S(2)}, u32[]{:S(2)}) %collective-permute-start.2) | collective-permute-done | bytes 262176 | tf_op jit(solution)/shard_map/ppermute | solution.py:60
  25.5 0.0 collective-permute-done.4
  25.5 1.2 %collective-permute-done.3 = bf16[128,1024]{1,0:T(8,128)(2,1)S(1)} collective-permute-done((bf16[128,1024]{1,0:T(8,128)(2,1)S(1)}, bf16[128,1024]{1,0:T(8,128)(2,1)S(1)}, u32[]{:S(2)}, u32[]{:S(2)}) %collective-permute-start.3) | collective-permute-done | bytes 262176 | tf_op jit(solution)/shard_map/ppermute | solution.py:60
  26.7 0.2 fusion.2
  26.9 22.4 %all_to_all.10 = bf16[16,8,1024]{2,1,0:T(8,128)(2,1)S(1)} all-to-all(bf16[16,8,1024]{2,1,0:T(8,128)(2,1)S(1)} %fusion.2), channel_id=1, replica_groups={{0,4,8,12,16,20,24,28,32,36,40,44,48,52,56,60},{64,68,72,76,80,84,88,92..., dimensions={0} | all-to-all | bytes 524288 | tf_op jit(solution)/shard_map/all_to_all | solution.py:64
  49.3 0.0 copy-done
  49.4 0.1 collective-permute-start.5
  49.5 1.2 %collective-permute-done.5 = f32[24,128]{1,0:T(8,128)S(1)} collective-permute-done((f32[24,128]{1,0:T(8,128)S(1)}, f32[24,128]{1,0:T(8,128)S(1)}, u32[]{:S(2)}, u32[]{:S(2)}) %collective-permute-start.5) | collective-permute-done | bytes 12320 | tf_op jit(solution)/shard_map/ppermute | solution.py:119
  50.6 2.1 %collective-permute-start.6 = (f32[24,128]{1,0:T(8,128)S(1)}, f32[24,128]{1,0:T(8,128)S(1)}, u32[]{:S(2)}, u32[]{:S(2)}) collective-permute-start(f32[24,128]{1,0:T(8,128)S(1)} %add.128), channel_id=1, source_target_pairs={{0,2},{1,3},{2,0},{3,1},{4,6},{5,7},{6,4},{7,5},{8,10},{9,11},{10,... | collective-permute-start | bytes 36872 | tf_op jit(solution)/shard_map/ppermute | solution.py:119
  52.8 1.9 %collective-permute-done.6 = f32[24,128]{1,0:T(8,128)S(1)} collective-permute-done((f32[24,128]{1,0:T(8,128)S(1)}, f32[24,128]{1,0:T(8,128)S(1)}, u32[]{:S(2)}, u32[]{:S(2)}) %collective-permute-start.6) | collective-permute-done | bytes 12320 | tf_op jit(solution)/shard_map/ppermute | solution.py:119
  54.7 0.1 share.1
  54.8 16.6 %all_to_all.11 = bf16[16,8,1024]{2,1,0:T(8,128)(2,1)S(1)} all-to-all(bf16[16,8,1024]{2,1,0:T(8,128)(2,1)S(1)} %bitcast.37), channel_id=1, replica_groups={{0,4,8,12,16,20,24,28,32,36,40,44,48,52,56,60},{64,68,72,76,80,84,88,92..., dimensions={0} | all-to-all | bytes 524288 | tf_op jit(solution)/shard_map/all_to_all | solution.py:64
  71.4 1.7 %collective-permute-start.9 = (bf16[128,1024]{1,0:T(8,128)(2,1)S(1)}, bf16[128,1024]{1,0:T(8,128)(2,1)S(1)}, u32[]{:S(2)}, u32[]{:S(2)}) collective-permute-start(bf16[128,1024]{1,0:T(8,128)(2,1)S(1)} %bitcast.40), channel_id=1, source_target_pairs={{0,192},{1,13},{2,194},{3,15},{4,196},{5,9},{6,198},{7,11},{8,200}... | collective-permute-start | bytes 786440 | tf_op jit(solution)/shard_map/ppermute | solution.py:60
  73.1 1.1 %collective-permute-start.8 = (bf16[128,1024]{1,0:T(8,128)(2,1)S(1)}, bf16[128,1024]{1,0:T(8,128)(2,1)S(1)}, u32[]{:S(2)}, u32[]{:S(2)}) collective-permute-start(bf16[128,1024]{1,0:T(8,128)(2,1)S(1)} %bitcast.41), channel_id=1, source_target_pairs={{0,128},{1,5},{2,130},{3,7},{4,132},{5,1},{6,134},{7,3},{8,136},{9... | collective-permute-start | bytes 786440 | tf_op jit(solution)/shard_map/ppermute | solution.py:60
  74.2 0.0 collective-permute-start.7
  74.2 3.0 %probs.1 = (f32[2048,1024]{1,0:T(8,128)S(1)}, bf16[2048,512]{1,0:T(8,128)(2,1)S(1)}) custom-call(bf16[2048,1024]{1,0:T(8,128)(2,1)} %x_hbm.5, bf16[2048,512]{1,0:T(8,128)(2,1)} %e_hbm.3, f32[8,256]{1,0:T(8,128)S(1)} %log_add_fusion.log_ref), custom_call_target="tpu_custom_call" | custom-call | flops 8388608 | bytes 8388608 | tf_op jit(solution)/shard_map/probs/pallas_call | solution.py:364
  77.1 0.5 collective-permute-done.9
  77.6 3.0 %collective-permute-done.8 = bf16[128,1024]{1,0:T(8,128)(2,1)S(1)} collective-permute-done((bf16[128,1024]{1,0:T(8,128)(2,1)S(1)}, bf16[128,1024]{1,0:T(8,128)(2,1)S(1)}, u32[]{:S(2)}, u32[]{:S(2)}) %collective-permute-start.8) | collective-permute-done | bytes 262176 | tf_op jit(solution)/shard_map/ppermute | solution.py:60
  80.6 0.0 collective-permute-done.7
  80.6 0.1 select_bitcast_fusion.3
  80.8 0.1 pad_maximum_fusion
  80.9 0.1 copy.6
  81.0 0.2 bitcast_select_fusion.d_ref
  81.2 2.7 %backward.1 = (f32[2048,1024]{1,0:T(8,128)S(1)}, f32[8,256]{1,0:T(8,128)S(1)}) custom-call(f32[2048,1024]{1,0:T(8,128)S(1)} %get-tuple-element.16.probs_ref, bf16[2048,512]{1,0:T(8,128)(2,1)S(1)} %get-tuple-element.17.e_ref, bf16[512,1024]{1,0:T(8,128)(2,1)S(1)} %bitcast_select_fusion.d_ref), custom_call_target="tpu_custom_call" | custom-call | flops 2147483648 | bytes 8388608 | tf_op jit(solution)/shard_map/backward/pallas_call | solution.py:405
  83.9 3.8 %collective-permute-start.10 = (f32[8,256]{1,0:T(8,128)S(1)}, f32[8,256]{1,0:T(8,128)S(1)}, u32[]{:S(2)}, u32[]{:S(2)}) collective-permute-start(f32[8,256]{1,0:T(8,128)S(1)} %get-tuple-element.20), channel_id=1, source_target_pairs={{0,1},{1,0},{2,3},{3,2},{4,5},{5,4},{6,7},{7,6},{8,9},{9,8},{10,11... | collective-permute-start | bytes 24584 | tf_op jit(solution)/shard_map/ppermute | solution.py:119
  87.7 0.8 collective-permute-done.10
  88.5 1.9 %collective-permute-start.11 = (f32[8,256]{1,0:T(8,128)S(1)}, f32[8,256]{1,0:T(8,128)S(1)}, u32[]{:S(2)}, u32[]{:S(2)}) collective-permute-start(f32[8,256]{1,0:T(8,128)S(1)} %add.134), channel_id=1, source_target_pairs={{0,2},{1,3},{2,0},{3,1},{4,6},{5,7},{6,4},{7,5},{8,10},{9,11},{10,... | collective-permute-start | bytes 24584 | tf_op jit(solution)/shard_map/ppermute | solution.py:119
  90.4 0.6 slice_reduce_fusion
  91.0 1.5 %collective-permute-done.11 = f32[8,256]{1,0:T(8,128)S(1)} collective-permute-done((f32[8,256]{1,0:T(8,128)S(1)}, f32[8,256]{1,0:T(8,128)S(1)}, u32[]{:S(2)}, u32[]{:S(2)}) %collective-permute-start.11) | collective-permute-done | bytes 8224 | tf_op jit(solution)/shard_map/ppermute | solution.py:119
  92.5 2.5 %gradient.1 = bf16[2048,1024]{1,0:T(8,128)(2,1)} custom-call(f32[2048,1024]{1,0:T(8,128)S(1)} %get-tuple-element.16.probs_ref, f32[2048,1024]{1,0:T(8,128)S(1)} %get-tuple-element.19.dprobs_ref, f32[8,256]{1,0:T(8,128)S(1)} %add.135.dot_ref), custom_call_target="tpu_custom_call" | custom-call | flops 6291456 | bytes 8388608 | tf_op jit(solution)/shard_map/gradient/pallas_call | solution.py:422
  (7 shorter events, 0.1 us)
Async XLA Ops:
  4.0 4.2 %collective-permute-start = (f32[8,256]{1,0:T(8,128)S(1)}, f32[8,256]{1,0:T(8,128)S(1)}, u32[]{:S(2)}, u32[]{:S(2)}) collective-permute-start(f32[8,256]{1,0:T(8,128)S(1)} %stats.1), channel_id=1, source_target_pairs={{0,1},{1,0},{2,3},{3,2},{4,5},{5,4},{6,7},{7,6},{8,9},{9,8},{10,11... | collective-permute-start | bytes 24584 | tf_op jit(solution)/shard_map/ppermute | solution.py:119
  8.2 4.1 %collective-permute-start.1 = (f32[8,256]{1,0:T(8,128)S(1)}, f32[8,256]{1,0:T(8,128)S(1)}, u32[]{:S(2)}, u32[]{:S(2)}) collective-permute-start(f32[8,256]{1,0:T(8,128)S(1)} %log_add_fusion.1), channel_id=1, source_target_pairs={{0,2},{1,3},{2,0},{3,1},{4,6},{5,7},{6,4},{7,5},{8,10},{9,11},{10,... | collective-permute-start | bytes 24584 | tf_op jit(solution)/shard_map/ppermute | solution.py:119
  16.8 32.5 %copy-start = (f32[8,1024]{1,0:T(8,128)S(1)}, f32[8,1024]{1,0:T(8,128)}, u32[]{:S(2)}) copy-start(f32[8,1024]{1,0:T(8,128)} %measured_ref.3) | copy-start | bytes 98308
  17.1 8.4 %collective-permute-start.2 = (bf16[128,1024]{1,0:T(8,128)(2,1)S(1)}, bf16[128,1024]{1,0:T(8,128)(2,1)S(1)}, u32[]{:S(2)}, u32[]{:S(2)}) collective-permute-start(bf16[128,1024]{1,0:T(8,128)(2,1)S(1)} %get-tuple-element.26), channel_id=1, source_target_pairs={{0,128},{1,5},{2,130},{3,7},{4,132},{5,1},{6,134},{7,3},{8,136},{9... | collective-permute-start | bytes 786440 | tf_op jit(solution)/shard_map/ppermute | solution.py:60
  17.2 8.3 %collective-permute-start.4 = (bf16[128,1024]{1,0:T(8,128)(2,1)S(1)}, bf16[128,1024]{1,0:T(8,128)(2,1)S(1)}, u32[]{:S(2)}, u32[]{:S(2)}) collective-permute-start(bf16[128,1024]{1,0:T(8,128)(2,1)S(1)} %get-tuple-element.27), channel_id=1, source_target_pairs={{0,192},{1,13},{2,194},{3,15},{4,196},{5,9},{6,198},{7,11},{8,200}... | collective-permute-start | bytes 786440 | tf_op jit(solution)/shard_map/ppermute | solution.py:60
  19.1 7.6 %collective-permute-start.3 = (bf16[128,1024]{1,0:T(8,128)(2,1)S(1)}, bf16[128,1024]{1,0:T(8,128)(2,1)S(1)}, u32[]{:S(2)}, u32[]{:S(2)}) collective-permute-start(bf16[128,1024]{1,0:T(8,128)(2,1)S(1)} %get-tuple-element.28), channel_id=1, source_target_pairs={{0,64},{1,9},{2,66},{3,11},{4,68},{5,13},{6,70},{7,15},{8,72},{9,1... | collective-permute-start | bytes 786440 | tf_op jit(solution)/shard_map/ppermute | solution.py:60
  49.4 1.3 %collective-permute-start.5 = (f32[24,128]{1,0:T(8,128)S(1)}, f32[24,128]{1,0:T(8,128)S(1)}, u32[]{:S(2)}, u32[]{:S(2)}) collective-permute-start(f32[24,128]{1,0:T(8,128)S(1)} %get-tuple-element.12), channel_id=1, source_target_pairs={{0,1},{1,0},{2,3},{3,2},{4,5},{5,4},{6,7},{7,6},{8,9},{9,8},{10,11... | collective-permute-start | bytes 36872 | tf_op jit(solution)/shard_map/ppermute | solution.py:119
  50.6 4.0 %collective-permute-start.6 = (f32[24,128]{1,0:T(8,128)S(1)}, f32[24,128]{1,0:T(8,128)S(1)}, u32[]{:S(2)}, u32[]{:S(2)}) collective-permute-start(f32[24,128]{1,0:T(8,128)S(1)} %add.128), channel_id=1, source_target_pairs={{0,2},{1,3},{2,0},{3,1},{4,6},{5,7},{6,4},{7,5},{8,10},{9,11},{10,... | collective-permute-start | bytes 36872 | tf_op jit(solution)/shard_map/ppermute | solution.py:119
  71.4 6.2 %collective-permute-start.9 = (bf16[128,1024]{1,0:T(8,128)(2,1)S(1)}, bf16[128,1024]{1,0:T(8,128)(2,1)S(1)}, u32[]{:S(2)}, u32[]{:S(2)}) collective-permute-start(bf16[128,1024]{1,0:T(8,128)(2,1)S(1)} %bitcast.40), channel_id=1, source_target_pairs={{0,192},{1,13},{2,194},{3,15},{4,196},{5,9},{6,198},{7,11},{8,200}... | collective-permute-start | bytes 786440 | tf_op jit(solution)/shard_map/ppermute | solution.py:60
  73.1 7.5 %collective-permute-start.8 = (bf16[128,1024]{1,0:T(8,128)(2,1)S(1)}, bf16[128,1024]{1,0:T(8,128)(2,1)S(1)}, u32[]{:S(2)}, u32[]{:S(2)}) collective-permute-start(bf16[128,1024]{1,0:T(8,128)(2,1)S(1)} %bitcast.41), channel_id=1, source_target_pairs={{0,128},{1,5},{2,130},{3,7},{4,132},{5,1},{6,134},{7,3},{8,136},{9... | collective-permute-start | bytes 786440 | tf_op jit(solution)/shard_map/ppermute | solution.py:60
  74.2 6.4 %collective-permute-start.7 = (bf16[128,1024]{1,0:T(8,128)(2,1)S(1)}, bf16[128,1024]{1,0:T(8,128)(2,1)S(1)}, u32[]{:S(2)}, u32[]{:S(2)}) collective-permute-start(bf16[128,1024]{1,0:T(8,128)(2,1)S(1)} %bitcast.42), channel_id=1, source_target_pairs={{0,64},{1,9},{2,66},{3,11},{4,68},{5,13},{6,70},{7,15},{8,72},{9,1... | collective-permute-start | bytes 786440 | tf_op jit(solution)/shard_map/ppermute | solution.py:60
  83.9 4.6 %collective-permute-start.10 = (f32[8,256]{1,0:T(8,128)S(1)}, f32[8,256]{1,0:T(8,128)S(1)}, u32[]{:S(2)}, u32[]{:S(2)}) collective-permute-start(f32[8,256]{1,0:T(8,128)S(1)} %get-tuple-element.20), channel_id=1, source_target_pairs={{0,1},{1,0},{2,3},{3,2},{4,5},{5,4},{6,7},{7,6},{8,9},{9,8},{10,11... | collective-permute-start | bytes 24584 | tf_op jit(solution)/shard_map/ppermute | solution.py:119
  88.5 4.0 %collective-permute-start.11 = (f32[8,256]{1,0:T(8,128)S(1)}, f32[8,256]{1,0:T(8,128)S(1)}, u32[]{:S(2)}, u32[]{:S(2)}) collective-permute-start(f32[8,256]{1,0:T(8,128)S(1)} %add.134), channel_id=1, source_target_pairs={{0,2},{1,3},{2,0},{3,1},{4,6},{5,7},{6,4},{7,5},{8,10},{9,11},{10,... | collective-permute-start | bytes 24584 | tf_op jit(solution)/shard_map/ppermute | solution.py:119
